TPU v7x, 32 devices: a whole 2x2x4 slice. The times are simulated.
32 devices in a mesh: blk: 32 (over z, y, x, core).
Axes of the slice: x: 2, y: 2, z: 4, core: 2. Of those that a mesh axis runs over, the one named last changes fastest.
Arguments:
- diag_block: float32 [32, 512, 512], P('blk'), may hold values from -0.6 to 12.6, as said below
- near_blocks: float32 [32, 6, 512, 512], P('blk'), may hold values from -0.15 to 0.15
- far_coupling: float32 [32, 5, 256, 256], P('blk'), may hold values from -0.15 to 0.15
- leaf_basis: float32 [32, 512, 512], P('blk'), may hold values from -0.2 to 1.2
- parent_basis: float32 [8192, 1024], P('blk'), may hold values from -0.2 to 1.2
- near_index: int32 [32, 6], P('blk'), may hold values from 0 to 31, as said below
- far_index: int32 [32, 5], P('blk'), may hold values from 0 to 31, as said below
Outputs:
- leaf_factor: float32 [8192, 512], P('blk')
- parent_cholesky_factor: float32 [8192, 768], P('blk')
- parent_coupling: float32 [8192, 768], P('blk')
Inputs may be any that keep to these rules, and one draw needn't show every extreme that they name: `near_index`: row i lists 6 different leaves, none equal to i, among the 12 leaves of parents i // 4 - 1, i // 4, i // 4 + 1 (modulo 8). `far_index`: row i lists the remaining 5 leaves of those parents: i, its near list and its far list name each of the 12 leaves once. `diag_block`: each block is symmetric.
All inputs are finite; a program needn't handle non-finite values.
Results may differ from a plain program's by a relative error of at most 0.0003.
Values sent between devices are 32-bit elements; how exact they have to be, the bound alone decides.
No kernel may reach another device: no remote copies, remote signals or barrier semaphores. Data moves between devices by JAX's collectives and lax.ppermute only.
A program may use at most 192 MiB of HBM per device.

v0:
```python
import jax
import jax.numpy as jnp
from jax import lax
from jax.sharding import PartitionSpec as P

LEAF = 512
RANK = 256
NEAR = 6
GROUP = 4
REDUN = 256
PAR = 1024
PRED = 768
FAR = 5


precise_mode = lax.Precision.HIGHEST


def passed_along(value, axis, steps):
    count = lax.axis_size(axis)
    pairs = [(source, (source + steps) % count) for source in range(count)]
    return lax.ppermute(value, axis, pairs)


def from_partner(value, axis, bit):
    mask = 2**bit
    pairs = [(source, source ^ mask) for source in range(lax.axis_size(axis))]
    return lax.ppermute(value, axis, pairs)


def matmul(left_side, right_side):
    return jnp.dot(left_side, right_side, precision=precise_mode)


def factor_inverse(square):
    order = square.shape[0]
    if order <= 64:
        lower = jnp.linalg.cholesky(square)
        eye_block = jnp.eye(order, dtype=jnp.float32)
        inverse = lax.linalg.triangular_solve(lower, eye_block, left_side=True, lower=True)
        return (lower, inverse)
    half = order // 2
    upper_low, upper_inv = factor_inverse(square[:half, :half])
    below = matmul(square[half:, :half], upper_inv.T)
    rest = square[half:, half:] - matmul(below, below.T)
    rest = 0.5 * (rest + rest.T)
    rest_low, rest_inv = factor_inverse(rest)
    zero_block = jnp.zeros((half, order - half), jnp.float32)
    lower = jnp.concatenate(
        [
            jnp.concatenate([upper_low, zero_block], axis=1),
            jnp.concatenate([below, rest_low], axis=1),
        ],
        axis=0,
    )
    corner = -matmul(rest_inv, matmul(below, upper_inv))
    inverse = jnp.concatenate(
        [
            jnp.concatenate([upper_inv, zero_block], axis=1),
            jnp.concatenate([corner, rest_inv], axis=1),
        ],
        axis=0,
    )
    return (lower, inverse)


def sym_factor(square):
    return factor_inverse(0.5 * (square + square.T))


def split_close(vector):
    return (vector[: LEAF * RANK].reshape(LEAF, RANK), vector[LEAF * RANK :].reshape(RANK, PAR))


def split_far(vector):
    return (vector[: LEAF * RANK].reshape(LEAF, RANK), vector[LEAF * RANK :].reshape(RANK, RANK))


def on_device(
    diag_block, near_blocks, far_coupling, leaf_basis, parent_basis, near_index, far_index
):
    blocks = lax.axis_size("blk")
    myself = lax.axis_index("blk")
    member = myself % GROUP
    max_offset = 2 * GROUP - 1
    own_basis = leaf_basis[0]
    skeleton = own_basis[:, REDUN:]
    close_load = jnp.concatenate([skeleton.reshape(-1), parent_basis.reshape(-1)])
    far_load = jnp.concatenate([skeleton.reshape(-1), parent_basis[:, PRED:].reshape(-1)])
    received = {0: close_load}
    for offset in range(-max_offset, max_offset + 1):
        if 0 < abs(offset) < GROUP:
            received[offset] = passed_along(close_load, "blk", -offset)
        elif abs(offset) >= GROUP:
            received[offset] = passed_along(far_load, "blk", -offset)
    skel_list = []
    qskel_list = []
    qfull_list = []
    for offset in range(-max_offset, max_offset + 1):
        if abs(offset) < GROUP:
            skel_part, row_block = split_close(received[offset])
            qfull_list.append(row_block)
            qskel_list.append(row_block[:, PRED:])
        else:
            skel_part, row_block = split_far(received[offset])
            qskel_list.append(row_block)
        skel_list.append(skel_part)
    skel_stack = jnp.stack(skel_list)
    qskel_stack = jnp.stack(qskel_list)
    complete_basis_stack = jnp.stack(qfull_list)
    transformed = matmul(matmul(own_basis.T, diag_block[0]), own_basis)
    leaf_low, leaf_inv = sym_factor(transformed[:REDUN, :REDUN])
    coupled = matmul(leaf_inv, transformed[:REDUN, REDUN:])
    leaf_schur = transformed[REDUN:, REDUN:] - matmul(coupled.T, coupled)
    leaf_out = jnp.concatenate([leaf_low, coupled], axis=1)
    half_count = blocks // 2
    near_offset = (near_index[0] - myself + half_count) % blocks - half_count
    far_offset = (far_index[0] - myself + half_count) % blocks - half_count
    near_skel = jnp.take(skel_stack, near_offset + max_offset, axis=0)
    left_side_product = jnp.einsum("ar,mac->mrc", skeleton, near_blocks[0], precision=precise_mode)
    near_summands = jnp.einsum("mrc,mcs->mrs", left_side_product, near_skel, precision=precise_mode)
    columns = jnp.arange(3 * GROUP, dtype=jnp.int32)
    near_slots = jnp.arange(NEAR, dtype=jnp.int32)
    far_slots = NEAR + jnp.arange(FAR, dtype=jnp.int32)
    near_match = ((near_offset + GROUP + member)[:, None] == columns).astype(jnp.int32)
    far_match = ((far_offset + GROUP + member)[:, None] == columns).astype(jnp.int32)
    self_match = (columns == GROUP + member).astype(jnp.int32)
    source = (
        jnp.sum(near_match * near_slots[:, None], axis=0)
        + jnp.sum(far_match * far_slots[:, None], axis=0)
        + self_match * (NEAR + FAR)
    )
    all_blocks = jnp.concatenate([near_summands, far_coupling[0], leaf_schur[None]], axis=0)
    window_blocks = jnp.take(all_blocks, source, axis=0)
    children = jnp.arange(GROUP, dtype=jnp.int32)
    prev_rows = jnp.take(qskel_stack, children - GROUP - member + max_offset, axis=0)
    own_rows = jnp.take(complete_basis_stack, children - member + GROUP - 1, axis=0)
    next_rows = jnp.take(qskel_stack, children + GROUP - member + max_offset, axis=0)
    v_self = jnp.einsum(
        "bij,bjl->il", window_blocks[GROUP : 2 * GROUP], own_rows, precision=precise_mode
    )
    v_prev = jnp.einsum("bij,bjl->il", window_blocks[:GROUP], prev_rows, precision=precise_mode)
    v_next = jnp.einsum(
        "bij,bjl->il", window_blocks[2 * GROUP :], next_rows, precision=precise_mode
    )
    joined = jnp.concatenate([v_self, v_prev, v_next], axis=1)
    high_bit = member // 2
    low_bit = member % 2
    sibling = from_partner(joined, "blk", 0)
    pair_stack = jnp.where(low_bit == 0, jnp.stack([joined, sibling]), jnp.stack([sibling, joined]))
    other_stack = from_partner(pair_stack, "blk", 1)
    all_joined = jnp.where(
        high_bit == 0,
        jnp.concatenate([pair_stack, other_stack], axis=0),
        jnp.concatenate([other_stack, pair_stack], axis=0),
    )
    whole_total = jnp.einsum("aij,ail->jl", own_rows, all_joined, precision=precise_mode)
    row_total = lax.dynamic_slice_in_dim(whole_total, member * RANK, RANK, 0)
    parent_block = whole_total[:, :PAR]
    parent_low, parent_inv = sym_factor(parent_block[:PRED, :PRED])
    parent_coupled = matmul(parent_inv, parent_block[:PRED, PRED:])
    parent_trans = matmul(parent_inv, parent_block[PRED:, :PRED].T)
    parent_schur = parent_block[PRED:, PRED:] - matmul(parent_trans.T, parent_coupled)
    factor_all = jnp.concatenate([parent_low, parent_coupled.T], axis=0)
    factor_rows = lax.dynamic_slice_in_dim(factor_all, member * RANK, RANK, 0)
    edge_rows = jnp.where(member == GROUP - 1, parent_schur, row_total[:, PRED:PAR])
    coupling_rows = jnp.concatenate(
        [row_total[:, PAR : PAR + RANK], edge_rows, row_total[:, PAR + RANK :]], axis=1
    )
    return (leaf_out, factor_rows, coupling_rows)


def solution(mesh):
    placed = (
        P("blk", None, None),
        P("blk", None, None, None),
        P("blk", None, None, None),
        P("blk", None, None),
        P("blk", None),
        P("blk", None),
        P("blk", None),
    )
    return jax.shard_map(
        on_device,
        mesh=mesh,
        in_specs=placed,
        out_specs=(P("blk", None), P("blk", None), P("blk", None)),
        check_vma=False,
    )
```

profile of v0, /device:TPU:0, one launch (start us, length us, event | category | flops | bytes accessed | tf_op | source)
XLA Modules:
  0.0 741.7 jit_solution(263441710888728588)
XLA Ops:
  20.5 5.9 cholesky.326
  28.3 4.9 custom-call.28
  36.8 6.6 cholesky.337
  45.4 5.5 custom-call.29
  57.3 5.9 cholesky.348
  65.1 4.9 custom-call.30
  71.7 6.1 cholesky.359
  79.7 4.9 custom-call.31
  99.5 63.8 %collective-permute-done.10 = f32[196608]{0:T(1024)S(1)} collective-permute-done((f32[196608]{0:T(1024)}, f32[196608]{0:T(1024)S(1)}, u32[]{:S(2)}, u32[]{:S(2)}) %collective-permute-start.10) | collective-permute-done | bytes 786464 | tf_op jit(solution)/shard_map/ppermute | solution.py:22
  163.2 42.2 %collective-permute-done.11 = f32[196608]{0:T(1024)} collective-permute-done((f32[196608]{0:T(1024)}, f32[196608]{0:T(1024)}, u32[]{:S(2)}, u32[]{:S(2)}) %collective-permute-start.11) | collective-permute-done | bytes 786464 | tf_op jit(solution)/shard_map/ppermute | solution.py:22
  205.5 5.3 collective-permute-start.3
  212.1 9.0 %fusion.6 = f32[6,512,256]{1,2,0:T(8,128)} fusion(f32[1,6,512,512]{3,2,1,0:T(8,128)} %param.16, f32[512,512]{1,0:T(8,128)S(1)} %bitcast.461), kind=kOutput, calls=%fused_computation.12 | convolution fusion | flops 4831838208 | bytes 9961472 | tf_op jit(solution)/shard_map/ar,mac->mrc/dot_general | solution.py:120
  303.8 8.9 %collective-permute-done.5 = f32[393216]{0:T(1024)} collective-permute-done((f32[393216]{0:T(1024)}, f32[393216]{0:T(1024)}, u32[]{:S(2)}, u32[]{:S(2)}) %collective-permute-start.5) | collective-permute-done | bytes 1572896 | tf_op jit(solution)/shard_map/ppermute | solution.py:22
  354.6 3.7 gather_fusion.3
  358.3 3.8 gather_fusion.4
  369.1 5.9 gather_fusion.1
  375.0 5.2 fusion.13
  382.3 12.6 %gather_fusion.2 = f32[12,256,256]{2,1,0:T(8,128)S(1)} fusion(f32[12,256,256]{2,1,0:T(8,128)} %pad_maximum_fusion, s32[1024]{0:T(1024)} %get-tuple-element.61), kind=kCustom, calls=%fused_computation.4 | custom fusion | bytes 6291504 | tf_op jit(solution)/shard_map/jit(_take)/gather | solution.py:134
  400.7 5.8 gather_fusion
  406.6 6.0 fusion.39
  418.9 4.0 maximum_select_fusion.4
  425.8 67.7 %collective-permute-done.15 = f32[2,256,1536]{2,1,0:T(8,128)} collective-permute-done((f32[2,256,1536]{2,1,0:T(8,128)}, f32[2,256,1536]{2,1,0:T(8,128)}, u32[]{:S(2)}, u32[]{:S(2)}) %collective-permute-start.15) | collective-permute-done | bytes 3145760 | tf_op jit(solution)/shard_map/ppermute | solution.py:28
  493.4 24.6 %fusion.8 = f32[1024,1536]{1,0:T(8,128)S(1)} fusion(f32[2,256,1536]{2,1,0:T(8,128)} %collective-permute-done.15, f32[2,256,1536]{2,1,0:T(8,128)} %maximum_select_fusion.4, f32[4,256,1024]{2,1,0:T(8,128)} %gather_fusion, pred[]{:T(512)S(6)} %eq.122, pred[4]{0:T(512)(128)(4,1)S(1)} %copy-done.67), kind=kOutput, calls=%fused_computation.20 | convolution fusion | flops 19333120000 | bytes 16777220 | tf_op jit(solution)/shard_map/aij,ail->jl/dot_general | solution.py:157
  529.2 4.4 cholesky.370
  535.5 3.7 custom-call.32
  542.1 4.4 cholesky.381
  555.6 4.4 cholesky.392
  562.0 3.7 custom-call.34
  567.1 4.4 cholesky.403
  579.5 4.4 cholesky.414
  585.8 3.7 custom-call.36
  590.5 4.4 cholesky.425
  596.8 3.7 custom-call.37
  602.4 4.4 cholesky.436
  608.7 3.7 custom-call.38
  613.7 4.4 cholesky.447
  620.0 3.7 custom-call.39
  633.0 4.4 cholesky.458
  644.0 4.4 cholesky.469
  655.5 4.4 cholesky.480
  666.6 4.4 cholesky.491
  679.4 4.4 cholesky.502
  690.4 4.4 cholesky.513
  701.9 4.4 cholesky.524
  707.6 3.7 custom-call.46
  712.4 4.4 cholesky.535
  718.1 3.7 custom-call.47
  724.1 4.1 fusion.63
  (614 shorter events, 321.3 us)
Async XLA Ops:
  0.6 14.2 %copy-start = (f32[1,512,512]{2,1,0:T(8,128)S(1)}, f32[1,512,512]{2,1,0:T(8,128)}, u32[]{:S(2)}) copy-start(f32[1,512,512]{2,1,0:T(8,128)} %param.15) | copy-start | bytes 3145732
  3.2 11.6 %copy-start.2 = (f32[1,512,512]{2,1,0:T(8,128)S(1)}, f32[1,512,512]{2,1,0:T(8,128)}, u32[]{:S(2)}) copy-start(f32[1,512,512]{2,1,0:T(8,128)} %param.18) | copy-start | bytes 3145732
  4.1 87.3 %collective-permute-start.6 = (f32[196608]{0:T(1024)}, f32[196608]{0:T(1024)}, u32[]{:S(2)}, u32[]{:S(2)}) collective-permute-start(f32[196608]{0:T(1024)} %constant_dynamic-update-slice_fusion.31), channel_id=1, source_target_pairs={{0,7},{1,8},{2,9},{3,10},{4,11},{5,12},{6,13},{7,14},{8,15},{9,16}... | collective-permute-start | bytes 2359304 | tf_op jit(solution)/shard_map/ppermute | solution.py:22
  7.4 87.3 %collective-permute-start.7 = (f32[196608]{0:T(1024)}, f32[196608]{0:T(1024)}, u32[]{:S(2)}, u32[]{:S(2)}) collective-permute-start(f32[196608]{0:T(1024)} %constant_dynamic-update-slice_fusion.31), channel_id=1, source_target_pairs={{0,6},{1,7},{2,8},{3,9},{4,10},{5,11},{6,12},{7,13},{8,14},{9,15},... | collective-permute-start | bytes 2359304 | tf_op jit(solution)/shard_map/ppermute | solution.py:22
  9.0 86.2 %collective-permute-start.8 = (f32[196608]{0:T(1024)}, f32[196608]{0:T(1024)}, u32[]{:S(2)}, u32[]{:S(2)}) collective-permute-start(f32[196608]{0:T(1024)} %constant_dynamic-update-slice_fusion.31), channel_id=1, source_target_pairs={{0,5},{1,6},{2,7},{3,8},{4,9},{5,10},{6,11},{7,12},{8,13},{9,14},{... | collective-permute-start | bytes 2359304 | tf_op jit(solution)/shard_map/ppermute | solution.py:22
  10.5 86.5 %collective-permute-start.9 = (f32[196608]{0:T(1024)}, f32[196608]{0:T(1024)}, u32[]{:S(2)}, u32[]{:S(2)}) collective-permute-start(f32[196608]{0:T(1024)} %constant_dynamic-update-slice_fusion.31), channel_id=1, source_target_pairs={{0,4},{1,5},{2,6},{3,7},{4,8},{5,9},{6,10},{7,11},{8,12},{9,13},{1... | collective-permute-start | bytes 2359304 | tf_op jit(solution)/shard_map/ppermute | solution.py:22
  13.3 197.5 %collective-permute-start = (f32[393216]{0:T(1024)}, f32[393216]{0:T(1024)}, u32[]{:S(2)}, u32[]{:S(2)}) collective-permute-start(f32[393216]{0:T(1024)} %constant_dynamic-update-slice_fusion.30), channel_id=1, source_target_pairs={{0,3},{1,4},{2,5},{3,6},{4,7},{5,8},{6,9},{7,10},{8,11},{9,12},{10... | collective-permute-start | bytes 4718600 | tf_op jit(solution)/shard_map/ppermute | solution.py:22
  18.5 52.9 %copy-start.69 = (s32[1,5]{1,0:T(1,128)S(1)}, s32[1,5]{1,0:T(1,128)}, u32[]{:S(2)}) copy-start(s32[1,5]{1,0:T(1,128)} %param.21) | copy-start | bytes 64
  88.4 10.4 %copy-start.66 = (s32[12]{0:T(128)}, s32[12]{0:T(128)S(1)}, u32[]{:S(2)}) copy-start(s32[12]{0:T(128)S(1)} %select_reduce_fusion.20) | copy-start | bytes 148
  91.4 71.8 %collective-permute-start.10 = (f32[196608]{0:T(1024)}, f32[196608]{0:T(1024)S(1)}, u32[]{:S(2)}, u32[]{:S(2)}) collective-permute-start(f32[196608]{0:T(1024)} %constant_dynamic-update-slice_fusion.31), channel_id=1, source_target_pairs={{0,28},{1,29},{2,30},{3,31},{4,0},{5,1},{6,2},{7,3},{8,4},{9,5},{1... | collective-permute-start | bytes 2359304 | tf_op jit(solution)/shard_map/ppermute | solution.py:22
  94.7 110.8 %collective-permute-start.11 = (f32[196608]{0:T(1024)}, f32[196608]{0:T(1024)}, u32[]{:S(2)}, u32[]{:S(2)}) collective-permute-start(f32[196608]{0:T(1024)} %constant_dynamic-update-slice_fusion.31), channel_id=1, source_target_pairs={{0,27},{1,28},{2,29},{3,30},{4,31},{5,0},{6,1},{7,2},{8,3},{9,4},{... | collective-permute-start | bytes 2359304 | tf_op jit(solution)/shard_map/ppermute | solution.py:22
  95.2 110.3 %collective-permute-start.12 = (f32[196608]{0:T(1024)}, f32[196608]{0:T(1024)}, u32[]{:S(2)}, u32[]{:S(2)}) collective-permute-start(f32[196608]{0:T(1024)} %constant_dynamic-update-slice_fusion.31), channel_id=1, source_target_pairs={{0,26},{1,27},{2,28},{3,29},{4,30},{5,31},{6,0},{7,1},{8,2},{9,3},... | collective-permute-start | bytes 2359304 | tf_op jit(solution)/shard_map/ppermute | solution.py:22
  97.0 113.8 %collective-permute-start.13 = (f32[196608]{0:T(1024)}, f32[196608]{0:T(1024)}, u32[]{:S(2)}, u32[]{:S(2)}) collective-permute-start(f32[196608]{0:T(1024)} %constant_dynamic-update-slice_fusion.31), channel_id=1, source_target_pairs={{0,25},{1,26},{2,27},{3,28},{4,29},{5,30},{6,31},{7,0},{8,1},{9,2}... | collective-permute-start | bytes 2359304 | tf_op jit(solution)/shard_map/ppermute | solution.py:22
  163.2 48.8 %copy-start.35 = (f32[196608]{0:T(1024)}, f32[196608]{0:T(1024)S(1)}, u32[]{:S(2)}) copy-start(f32[196608]{0:T(1024)S(1)} %collective-permute-done.10) | copy-start | bytes 2359300
  163.2 126.2 %collective-permute-start.1 = (f32[393216]{0:T(1024)}, f32[393216]{0:T(1024)}, u32[]{:S(2)}, u32[]{:S(2)}) collective-permute-start(f32[393216]{0:T(1024)} %constant_dynamic-update-slice_fusion.30), channel_id=1, source_target_pairs={{0,2},{1,3},{2,4},{3,5},{4,6},{5,7},{6,8},{7,9},{8,10},{9,11},{10,... | collective-permute-start | bytes 4718600 | tf_op jit(solution)/shard_map/ppermute | solution.py:22
  205.5 87.6 %collective-permute-start.2 = (f32[393216]{0:T(1024)}, f32[393216]{0:T(1024)}, u32[]{:S(2)}, u32[]{:S(2)}) collective-permute-start(f32[393216]{0:T(1024)} %constant_dynamic-update-slice_fusion.30), channel_id=1, source_target_pairs={{0,1},{1,2},{2,3},{3,4},{4,5},{5,6},{6,7},{7,8},{8,9},{9,10},{10,1... | collective-permute-start | bytes 4718600 | tf_op jit(solution)/shard_map/ppermute | solution.py:22
  205.5 91.2 %collective-permute-start.3 = (f32[393216]{0:T(1024)}, f32[393216]{0:T(1024)}, u32[]{:S(2)}, u32[]{:S(2)}) collective-permute-start(f32[393216]{0:T(1024)} %constant_dynamic-update-slice_fusion.30), channel_id=1, source_target_pairs={{0,31},{1,0},{2,1},{3,2},{4,3},{5,4},{6,5},{7,6},{8,7},{9,8},{10,9... | collective-permute-start | bytes 4718600 | tf_op jit(solution)/shard_map/ppermute | solution.py:22
  210.8 89.4 %collective-permute-start.4 = (f32[393216]{0:T(1024)}, f32[393216]{0:T(1024)}, u32[]{:S(2)}, u32[]{:S(2)}) collective-permute-start(f32[393216]{0:T(1024)} %constant_dynamic-update-slice_fusion.30), channel_id=1, source_target_pairs={{0,30},{1,31},{2,0},{3,1},{4,2},{5,3},{6,4},{7,5},{8,6},{9,7},{10,... | collective-permute-start | bytes 4718600 | tf_op jit(solution)/shard_map/ppermute | solution.py:22
  210.8 101.9 %collective-permute-start.5 = (f32[393216]{0:T(1024)}, f32[393216]{0:T(1024)}, u32[]{:S(2)}, u32[]{:S(2)}) collective-permute-start(f32[393216]{0:T(1024)} %constant_dynamic-update-slice_fusion.30), channel_id=1, source_target_pairs={{0,29},{1,30},{2,31},{3,0},{4,1},{5,2},{6,3},{7,4},{8,5},{9,6},{10... | collective-permute-start | bytes 4718600 | tf_op jit(solution)/shard_map/ppermute | solution.py:22
  275.7 8.5 %copy-start.19 = (f32[1,512,256]{2,1,0:T(8,128)S(1)}, f32[1,512,256]{2,1,0:T(8,128)}, u32[]{:S(2)}) copy-start(f32[1,512,256]{2,1,0:T(8,128)} %stack_reshape.64) | copy-start | bytes 1572868
  275.7 9.3 %copy-start.20 = (f32[1,512,256]{2,1,0:T(8,128)S(1)}, f32[1,512,256]{2,1,0:T(8,128)}, u32[]{:S(2)}) copy-start(f32[1,512,256]{2,1,0:T(8,128)} %stack_reshape.65) | copy-start | bytes 1572868
  328.9 9.9 %copy-start.8 = (f32[1,256,1024]{2,1,0:T(8,128)S(1)}, f32[1,256,1024]{2,1,0:T(8,128)}, u32[]{:S(2)}) copy-start(f32[1,256,1024]{2,1,0:T(8,128)} %stack_reshape.56) | copy-start | bytes 3145732
  331.0 7.9 %copy-start.9 = (f32[1,256,1024]{2,1,0:T(8,128)S(1)}, f32[1,256,1024]{2,1,0:T(8,128)}, u32[]{:S(2)}) copy-start(f32[1,256,1024]{2,1,0:T(8,128)} %stack_reshape.57) | copy-start | bytes 3145732
  340.1 11.5 %copy-start.31 = (f32[1,256,256]{2,1,0:T(8,128)S(1)}, f32[1,256,256]{2,1,0:T(8,128)}, u32[]{:S(2)}) copy-start(f32[1,256,256]{2,1,0:T(8,128)} %slice.597) | copy-start | bytes 786436
  340.1 12.2 %copy-start.32 = (f32[1,256,256]{2,1,0:T(8,128)S(1)}, f32[1,256,256]{2,1,0:T(8,128)}, u32[]{:S(2)}) copy-start(f32[1,256,256]{2,1,0:T(8,128)} %slice.599) | copy-start | bytes 786436
  340.1 13.0 %copy-start.33 = (f32[1,256,256]{2,1,0:T(8,128)S(1)}, f32[1,256,256]{2,1,0:T(8,128)}, u32[]{:S(2)}) copy-start(f32[1,256,256]{2,1,0:T(8,128)} %slice.601) | copy-start | bytes 786436
  340.2 6.4 copy-start.14
  340.2 13.6 %copy-start.34 = (f32[1,256,256]{2,1,0:T(8,128)S(1)}, f32[1,256,256]{2,1,0:T(8,128)}, u32[]{:S(2)}) copy-start(f32[1,256,256]{2,1,0:T(8,128)} %slice.603) | copy-start | bytes 786436
  351.6 10.5 %copy-start.21 = (f32[1,512,256]{2,1,0:T(8,128)S(1)}, f32[1,512,256]{2,1,0:T(8,128)}, u32[]{:S(2)}) copy-start(f32[1,512,256]{2,1,0:T(8,128)} %slice.564) | copy-start | bytes 1572868
  353.1 9.9 %copy-start.22 = (f32[1,512,256]{2,1,0:T(8,128)S(1)}, f32[1,512,256]{2,1,0:T(8,128)}, u32[]{:S(2)}) copy-start(f32[1,512,256]{2,1,0:T(8,128)} %slice.566) | copy-start | bytes 1572868
  358.3 7.4 copy-start.15
  358.3 8.2 %copy-start.16 = (f32[1,512,256]{2,1,0:T(8,128)S(1)}, f32[1,512,256]{2,1,0:T(8,128)}, u32[]{:S(2)}) copy-start(f32[1,512,256]{2,1,0:T(8,128)} %stack_reshape.67) | copy-start | bytes 1572868
  362.1 5.3 copy-start.17
  362.1 6.1 copy-start.18
  369.1 5.9 copy-start.3
  369.1 5.9 copy-start.68
  375.0 5.2 copy-start.30
  400.7 5.8 copy-start.67
  406.6 6.0 copy-start.12
  406.6 6.0 copy-start.71
  415.3 3.6 collective-permute-start.14
  423.0 70.5 %collective-permute-start.15 = (f32[2,256,1536]{2,1,0:T(8,128)}, f32[2,256,1536]{2,1,0:T(8,128)}, u32[]{:S(2)}, u32[]{:S(2)}) collective-permute-start(f32[2,256,1536]{2,1,0:T(8,128)} %maximum_select_fusion.4), channel_id=1, source_target_pairs={{0,2},{1,3},{2,0},{3,1},{4,6},{5,7},{6,4},{7,5},{8,10},{9,11},{10,... | collective-permute-start | bytes 9437192 | tf_op jit(solution)/shard_map/ppermute | solution.py:28
  528.1 49.6 %copy-start.5 = (f32[768,768]{1,0:T(8,128)S(1)}, f32[768,768]{1,0:T(8,128)}, u32[]{:S(2)}) copy-start(f32[768,768]{1,0:T(8,128)} %copy-done.4) | copy-start | bytes 7077892
  589.9 34.2 %copy-start.42 = (f32[48,48]{1,0:T(8,128)}, f32[48,48]{1,0:T(8,128)S(1)}, u32[]{:S(2)}) copy-start(f32[48,48]{1,0:T(8,128)S(1)} %fusion.255) | copy-start | bytes 27652
  612.8 11.3 %copy-start.46 = (f32[48,48]{1,0:T(8,128)}, f32[48,48]{1,0:T(8,128)S(1)}, u32[]{:S(2)}) copy-start(f32[48,48]{1,0:T(8,128)S(1)} %fusion.253) | copy-start | bytes 27652
  643.5 33.7 %copy-start.44 = (f32[48,48]{1,0:T(8,128)}, f32[48,48]{1,0:T(8,128)S(1)}, u32[]{:S(2)}) copy-start(f32[48,48]{1,0:T(8,128)S(1)} %fusion.251) | copy-start | bytes 27652
  666.0 34.9 %copy-start.38 = (f32[48,48]{1,0:T(8,128)}, f32[48,48]{1,0:T(8,128)S(1)}, u32[]{:S(2)}) copy-start(f32[48,48]{1,0:T(8,128)S(1)} %fusion.249) | copy-start | bytes 27652
  678.9 43.8 %copy-start.48 = (f32[384,384]{1,0:T(8,128)S(1)}, f32[384,384]{1,0:T(8,128)}, u32[]{:S(2)}) copy-start(f32[384,384]{1,0:T(8,128)} %fusion.349) | copy-start | bytes 1769476
  (40 other events, 91.7 us)
where the time goes:
time: 755 us; the launch traced here: 742 us
  other arithmetic  241 us (32%)
  local copies, waits for them, and re-layouts  193 us (26%)
  waiting for transfers between devices  186 us (25%)
  matrix products  98.1 us (13%)
  starting transfers between devices  20.4 us (3%)
    ppermute x14, waiting for transfers between devices, passed_along(): return lax.ppermute(value, axis, pairs)  115 us
    another operation x60, other arithmetic, factor_inverse(): lower = jnp.linalg.cholesky(square)  108 us
    another operation x40, other arithmetic, factor_inverse(): lax.linalg.triangular_solve(lower, eye_block, left_side=True, lower=True)  103 us
    ppermute x2, waiting for transfers between devices, from_partner(): return lax.ppermute(value, axis, pairs)  71.2 us
    unnamed x186, local copies, waits for them, and re-layouts  53.1 us
    dot_general x79, matrix products, matmul(): return jnp.dot(left_side, right_side, precision=precise_mode)  45.5 us
    slice x16, local copies, waits for them, and re-layouts, split_far(): vector[LEAF * RANK:].reshape(RANK, RANK)  27.2 us
    dot_general x1, matrix products, on_device(): jnp.einsum('aij,ail->jl', own_rows, all_joined, precision=precise_mode)  24.6 us
  transfers between devices with their start and end apart: 16, of which 5 were waited for; matrix products, arithmetic and copies ran while one was open for 24% of the time, Pallas kernels for 0%

commit v1 on v0

v1 whole, which is shorter than its diff:
```python
import functools

import jax
import jax.numpy as jnp
from jax import lax
from jax.experimental import pallas as pl
from jax.experimental.pallas import tpu as pltpu
from jax.sharding import PartitionSpec as P

LEAF = 512
RANK = 256
NEAR = 6
GROUP = 4
REDUN = 256
PAR = 1024
PRED = 768
FAR = 5
TILE = 128
ROWS = 8
WIDE = PRED + 2 * RANK

VMEM_BYTES = 56 * 1024 * 1024

NN = (((1,), (0,)), ((), ()))
TN = (((0,), (0,)), ((), ()))


def params():
    return pltpu.CompilerParams(vmem_limit_bytes=VMEM_BYTES)


def in_vmem():
    return pl.BlockSpec(memory_space=pltpu.VMEM)


def in_smem():
    return pl.BlockSpec(memory_space=pltpu.SMEM)


def split(value):
    high = value.astype(jnp.bfloat16)
    low = (value - high.astype(jnp.float32)).astype(jnp.bfloat16)
    return high, low


def dot3(left, right, dims=NN):
    def one(a, b):
        return lax.dot_general(a, b, dims, preferred_element_type=jnp.float32)

    return one(left[0], right[0]) + (one(left[0], right[1]) + one(left[1], right[0]))


def lane_spread(value, lane):
    return jnp.broadcast_to(value[:, lane : lane + 1], (ROWS, TILE))


def row_spread(value, row):
    return jnp.broadcast_to(value[row : row + 1, :], value.shape)


def panel_rows(parts, lane):
    sub = lax.broadcasted_iota(jnp.int32, (ROWS, TILE), 0)
    cols = [lane_spread(parts[0], lane + j) for j in range(ROWS)]
    parts = list(parts)
    scale = jnp.zeros((ROWS, TILE), jnp.float32)
    for j in range(ROWS):
        root = lax.rsqrt(row_spread(cols[j], j))
        scale = jnp.where(sub == j, root, scale)
        if j < ROWS - 1:
            factor = jnp.where(sub > j, cols[j] * (root * root), 0.0)
            for k in range(j + 1, ROWS):
                cols[k] = cols[k] - factor * row_spread(cols[k], j)
            parts = [part - factor * row_spread(part, j) for part in parts]
    return [part * scale for part in parts]


def tile_factor(square):
    count = TILE // ROWS
    row = lax.broadcasted_iota(jnp.int32, (ROWS, TILE), 0)
    col = lax.broadcasted_iota(jnp.int32, (ROWS, TILE), 1)
    left = [square[ROWS * i : ROWS * (i + 1), :] for i in range(count)]
    right = [jnp.where(row + ROWS * i == col, 1.0, 0.0).astype(jnp.float32) for i in range(count)]
    upper = []
    inverse = []
    pad1 = jnp.zeros((ROWS, TILE), jnp.float32)
    pad2 = jnp.zeros((ROWS, 2 * TILE), jnp.float32)
    for k in range(count):
        u_rows, m_rows = panel_rows([left[k], right[k]], ROWS * k)
        u_rows = jnp.where(col >= row + ROWS * k, u_rows, 0.0)
        upper.append(u_rows)
        inverse.append(m_rows)
        if k == count - 1:
            break
        both = jnp.concatenate([u_rows, m_rows], axis=1)
        high = both.astype(jnp.bfloat16).astype(jnp.float32)
        low = both - high
        lhs = jnp.concatenate([high[:, :TILE], high[:, :TILE], low[:, :TILE], pad1], axis=0)
        rhs = jnp.concatenate([high, low, high, pad2], axis=0)
        update = lax.dot_general(
            lhs.astype(jnp.bfloat16),
            rhs.astype(jnp.bfloat16),
            TN,
            preferred_element_type=jnp.float32,
        )
        for i in range(k + 1, count):
            rows = slice(ROWS * i, ROWS * (i + 1))
            left[i] = left[i] - update[rows, :TILE]
            right[i] = right[i] - update[rows, TILE:]
    return jnp.concatenate(upper, axis=0), jnp.concatenate(inverse, axis=0)


def leaf_kernel(diag_ref, basis_ref, out_ref, schur_ref, work, u_tile, m_tile):
    basis = split(basis_ref[...])
    half = split(dot3(split(diag_ref[...]), basis))
    redundant = [part[:, :REDUN] for part in basis]
    skeleton = [part[:, REDUN:] for part in basis]
    top = dot3(redundant, half, TN)
    square = top[:, :REDUN]
    work[:, :REDUN] = 0.5 * (square + square.T)
    work[:, REDUN:] = top[:, REDUN:]
    schur_ref[...] = dot3(skeleton, [part[:, REDUN:] for part in half], TN)

    def step(k, carry):
        rows = pl.ds(pl.multiple_of(k * TILE, TILE), TILE)
        upper, inverse = tile_factor(work[rows, rows])
        u_tile[...] = upper
        m_tile[...] = inverse
        new_rows = dot3(split(m_tile[...]), split(work[rows, :]))
        work[rows, :] = new_rows
        work[rows, rows] = u_tile[...]

        @pl.when(k == 0)
        def _():
            parts = split(new_rows)
            side = [part[:, TILE:REDUN] for part in parts]
            work[TILE:, TILE:] = work[TILE:, TILE:] - dot3(side, [part[:, TILE:] for part in parts], TN)

        return carry

    lax.fori_loop(0, REDUN // TILE, step, 0)
    row = lax.broadcasted_iota(jnp.int32, (REDUN, REDUN), 0)
    col = lax.broadcasted_iota(jnp.int32, (REDUN, REDUN), 1)
    out_ref[:, :REDUN] = jnp.where(row <= col, work[:, :REDUN], 0.0).T
    coupled = work[:, REDUN:]
    out_ref[:, REDUN:] = coupled
    parts = split(coupled)
    schur_ref[...] = schur_ref[...] - dot3(parts, parts, TN)


def left_kernel(skel_ref, near_ref, high_ref, low_ref):
    product = dot3(split(skel_ref[...]), split(near_ref[0]), TN)
    high, low = split(product)
    high_ref[0] = high
    low_ref[0] = low


def source_of(leaf, near_ref, far_ref):
    slot = jnp.int32(0)
    for m in range(NEAR):
        slot = slot + jnp.where(near_ref[0, m] == leaf, m, 0)
    for f in range(FAR):
        slot = slot + jnp.where(far_ref[0, f] == leaf, NEAR + f, 0)
    return slot


def window_block(leaf, near_ref, far_ref, high_ref, low_ref, far_blocks_ref, skel, put):
    slot = source_of(leaf, near_ref, far_ref)

    @pl.when(slot < NEAR)
    def _():
        m = jnp.minimum(slot, NEAR - 1)
        put(dot3((high_ref[m], low_ref[m]), split(skel[...])))

    @pl.when(slot >= NEAR)
    def _():
        f = jnp.clip(slot - NEAR, 0, FAR - 1)
        put(far_blocks_ref[f])


def own_kernel(me_ref, near_ref, far_ref, high_ref, low_ref, far_blocks_ref, s1, s2, s3, out_ref):
    for s, skel in enumerate((s1, s2, s3)):

        def put(block, s=s):
            out_ref[s] = block

        leaf = jnp.bitwise_xor(me_ref[0], s + 1)
        window_block(leaf, near_ref, far_ref, high_ref, low_ref, far_blocks_ref, skel, put)


def side_kernel(blocks, me_ref, near_ref, far_ref, high_ref, low_ref, far_blocks_ref, *rest):
    zs, (out_ref, held) = rest[:8], rest[8:]

    def put(block):
        held[...] = block

    for side, shift in enumerate((blocks - GROUP, GROUP)):
        for s in range(GROUP):
            z_ref = zs[side * GROUP + s]
            leaf = lax.rem(jnp.bitwise_xor(me_ref[0], s) + shift, blocks)
            window_block(
                leaf, near_ref, far_ref, high_ref, low_ref, far_blocks_ref, z_ref.at[:LEAF, :], put
            )
            term = dot3(split(held[...]), split(z_ref[LEAF:, :]))
            cols = slice(side * RANK, (side + 1) * RANK)
            if s == 0:
                out_ref[:, cols] = term
            else:
                out_ref[:, cols] = out_ref[:, cols] + term


def parent_kernel(me_ref, *rest):
    bases, hs, schurs = rest[:4], rest[4:8], rest[8:12]
    factor_ref, edge_ref = rest[12:14]
    p_high, p_low, v_high, v_low, whole, work, u_tile, m_tile = rest[14:]
    member = lax.rem(me_ref[0], GROUP)
    for s in range(GROUP):
        rows = slice(s * RANK, (s + 1) * RANK)
        high, low = split(bases[s][...])
        p_high[rows, :] = high
        p_low[rows, :] = low
    for s in range(GROUP):
        rows = slice(s * RANK, (s + 1) * RANK)
        line = [schurs[s][...] if t == s else hs[s][(s ^ t) - 1] for t in range(GROUP)]
        line = split(jnp.concatenate(line, axis=1))
        high, low = split(dot3(line, (p_high[...], p_low[...])))
        v_high[rows, :] = high
        v_low[rows, :] = low
    for m in range(GROUP):
        rows = slice(m * RANK, (m + 1) * RANK)
        whole[rows, :] = dot3((p_high[:, rows], p_low[:, rows]), (v_high[...], v_low[...]), TN)
    square = whole[:PRED, :PRED]
    work[:, :PRED] = 0.5 * (square + square.T)
    work[:, PRED:PAR] = whole[:PRED, PRED:]
    work[:, PAR:] = whole[PRED:, :PRED].T

    def step(k, carry):
        rows = pl.ds(pl.multiple_of(k * TILE, TILE), TILE)
        upper, inverse = tile_factor(work[rows, rows])
        u_tile[...] = upper
        m_tile[...] = inverse
        new_rows = dot3(split(m_tile[...]), split(work[rows, :]))
        work[rows, :] = new_rows
        work[rows, rows] = u_tile[...]
        parts = split(new_rows)
        for i in range(1, PRED // TILE):

            @pl.when(i > k)
            def _(i=i):
                below = slice(i * TILE, (i + 1) * TILE)
                side = [part[:, below] for part in parts]
                right = [part[:, i * TILE :] for part in parts]
                work[below, i * TILE :] = work[below, i * TILE :] - dot3(side, right, TN)

        return carry

    lax.fori_loop(0, PRED // TILE, step, 0)
    row = lax.broadcasted_iota(jnp.int32, (PRED, RANK), 0)
    col = lax.broadcasted_iota(jnp.int32, (PRED, RANK), 1) + member * RANK
    slab = pl.ds(pl.multiple_of(member * RANK, RANK), RANK)
    factor_ref[...] = jnp.where(row <= col, work[:, slab], 0.0).T
    edge_ref[...] = whole[slab, PRED:]

    @pl.when(member == GROUP - 1)
    def _():
        product = dot3(split(work[:, PAR:]), split(work[:, PRED:PAR]), TN)
        edge_ref[...] = whole[PRED:, PRED:] - product


def couple_kernel(me_ref, p0, p1, p2, p3, v0, v1, v2, v3, edge_ref, out_ref):
    member = lax.rem(me_ref[0], GROUP)
    slab = pl.ds(pl.multiple_of(member * RANK, RANK), RANK)
    total = jnp.zeros((RANK, 2 * RANK), jnp.float32)
    for p_ref, v_ref in ((p0, v0), (p1, v1), (p2, v2), (p3, v3)):
        total = total + dot3(split(p_ref[:, slab]), split(v_ref[...]), TN)
    out_ref[:, :RANK] = total[:, :RANK]
    out_ref[:, RANK : 2 * RANK] = edge_ref[...]
    out_ref[:, 2 * RANK :] = total[:, RANK:]


def swapped(value, axis, mask):
    pairs = [(source, source ^ mask) for source in range(lax.axis_size(axis))]
    return lax.ppermute(value, axis, pairs)


def shifted(value, axis, steps):
    count = lax.axis_size(axis)
    pairs = [(source, (source + steps) % count) for source in range(count)]
    return lax.ppermute(value, axis, pairs)


def gathered(value, axis):
    core = swapped(value, axis, 1)
    chip = swapped(value, axis, 2)
    both = swapped(chip, axis, 1)
    return [value, core, chip, both]


def on_device(
    diag_block, near_blocks, far_coupling, leaf_basis, parent_basis, near_index, far_index
):
    blocks = lax.axis_size("blk")
    me = lax.axis_index("blk").astype(jnp.int32).reshape(1)
    basis = leaf_basis[0]
    skeleton = basis[:, REDUN:]
    near = near_blocks[0]
    far = far_coupling[0]
    f32 = jnp.float32

    skels = gathered(skeleton, "blk")
    bases = gathered(parent_basis, "blk")
    load = jnp.concatenate([skeleton, parent_basis[:, PRED:]], axis=0)
    from_prev = gathered(shifted(load, "blk", GROUP), "blk")
    from_next = gathered(shifted(load, "blk", -GROUP), "blk")

    left_high, left_low = pl.pallas_call(
        left_kernel,
        grid=(NEAR,),
        in_specs=[
            pl.BlockSpec((LEAF, RANK), lambda m: (0, 1)),
            pl.BlockSpec((1, LEAF, LEAF), lambda m: (m, 0, 0)),
        ],
        out_specs=[pl.BlockSpec((1, RANK, LEAF), lambda m: (m, 0, 0))] * 2,
        out_shape=[jax.ShapeDtypeStruct((NEAR, RANK, LEAF), jnp.bfloat16)] * 2,
        compiler_params=params(),
        name="left_products",
    )(basis, near)

    leaf_out, leaf_schur = pl.pallas_call(
        leaf_kernel,
        in_specs=[in_vmem()] * 2,
        out_specs=[in_vmem()] * 2,
        out_shape=[
            jax.ShapeDtypeStruct((REDUN, LEAF), f32),
            jax.ShapeDtypeStruct((RANK, RANK), f32),
        ],
        scratch_shapes=[
            pltpu.VMEM((REDUN, LEAF), f32),
            pltpu.VMEM((TILE, TILE), f32),
            pltpu.VMEM((TILE, TILE), f32),
        ],
        compiler_params=params(),
        name="leaf_factor",
    )(diag_block[0], basis)

    own = pl.pallas_call(
        own_kernel,
        in_specs=[in_smem()] * 3 + [in_vmem()] * 6,
        out_specs=in_vmem(),
        out_shape=jax.ShapeDtypeStruct((GROUP - 1, RANK, RANK), f32),
        compiler_params=params(),
        name="own_window",
    )(me, near_index, far_index, left_high, left_low, far, *skels[1:])

    owns = gathered(own, "blk")
    schurs = gathered(leaf_schur, "blk")

    factor_rows, edge_rows = pl.pallas_call(
        parent_kernel,
        in_specs=[in_smem()] + [in_vmem()] * 12,
        out_specs=[in_vmem()] * 2,
        out_shape=[
            jax.ShapeDtypeStruct((RANK, PRED), f32),
            jax.ShapeDtypeStruct((RANK, RANK), f32),
        ],
        scratch_shapes=[pltpu.VMEM((PAR, PAR), jnp.bfloat16)] * 4
        + [
            pltpu.VMEM((PAR, PAR), f32),
            pltpu.VMEM((PRED, WIDE), f32),
            pltpu.VMEM((TILE, TILE), f32),
            pltpu.VMEM((TILE, TILE), f32),
        ],
        compiler_params=params(),
        name="parent_factor",
    )(me, *bases, *owns, *schurs)

    side = pl.pallas_call(
        functools.partial(side_kernel, blocks),
        in_specs=[in_smem()] * 3 + [in_vmem()] * 11,
        out_specs=in_vmem(),
        out_shape=jax.ShapeDtypeStruct((RANK, 2 * RANK), f32),
        scratch_shapes=[pltpu.VMEM((RANK, RANK), f32)],
        compiler_params=params(),
        name="side_windows",
    )(me, near_index, far_index, left_high, left_low, far, *from_prev, *from_next)
    sides = gathered(side, "blk")

    coupling_rows = pl.pallas_call(
        couple_kernel,
        in_specs=[in_smem()] + [in_vmem()] * 9,
        out_specs=in_vmem(),
        out_shape=jax.ShapeDtypeStruct((RANK, 3 * RANK), f32),
        compiler_params=params(),
        name="coupling",
    )(me, *bases, *sides, edge_rows)
    return (leaf_out, factor_rows, coupling_rows)


def solution(mesh):
    placed = (
        P("blk", None, None),
        P("blk", None, None, None),
        P("blk", None, None, None),
        P("blk", None, None),
        P("blk", None),
        P("blk", None),
        P("blk", None),
    )
    return jax.shard_map(
        on_device,
        mesh=mesh,
        in_specs=placed,
        out_specs=(P("blk", None), P("blk", None), P("blk", None)),
        check_vma=False,
    )
```

time: 755 us -> 203 us (0.27); the launches traced: 742 us -> 203 us
  other arithmetic: 241 us -> 0.05 us
  local copies, waits for them, and re-layouts: 193 us -> 4.66 us
  waiting for transfers between devices: 186 us -> 77.7 us
  Pallas kernels: 0 us -> 104 us
  matrix products: 98.1 us -> 0 us
    another operation x101 -> x0, other arithmetic: 211 us -> none  [the longest x60 108 us: factor_inverse(): lower = jnp.linalg.cholesky(square)]
    ppermute x16 -> x23, waiting for transfers between devices: 186 us -> 77.7 us  [the longest x21 72.9 us: swapped(): return lax.ppermute(value, axis, pairs)]
    pallas_call x0 -> x6, Pallas kernels: none -> 104 us  [the longest x1 61.2 us: on_device(): pl.pallas_call(parent_kernel, in_specs=[in_smem()] + [in_vmem()] * 12, ou...]
    dot_general x85 -> x0, matrix products: 92.5 us -> none  [the longest x79 45.5 us: matmul(): return jnp.dot(left_side, right_side, precision=precise_mode)]
    slice x70 -> x3, local copies, waits for them, and re-layouts: 76.4 us -> 1.13 us  [the longest x1 1.12 us: on_device(): skeleton = basis[:, REDUN:]]
    unnamed x186 -> x36, local copies, waits for them, and re-layouts: 53.1 us -> 3.54 us
    gather x5 -> x0, local copies, waits for them, and re-layouts: 31.9 us -> none  [the longest x1 12.6 us: on_device(): window_blocks = jnp.take(all_blocks, source, axis=0)]
    another operation x17 -> x0, local copies, waits for them, and re-layouts: 22.8 us -> none  [the longest x9 14.1 us: on_device(): skel_stack = jnp.stack(skel_list)]
  transfers between devices with their start and end apart: 16 -> 23, of which waited for: 5 -> 8; matrix products, arithmetic and copies ran while one was open for 24% -> 0% of each run, Pallas kernels for 0% -> 49%
where the time goes in v1:
time: 203 us
  Pallas kernels  104 us (51%)
  waiting for transfers between devices  77.7 us (38%)
  starting transfers between devices  16.2 us (8%)
  local copies, waits for them, and re-layouts  4.66 us (2%)
    ppermute x21, waiting for transfers between devices, swapped(): return lax.ppermute(value, axis, pairs)  72.9 us
    pallas_call x1, Pallas kernels, on_device(): pl.pallas_call(parent_kernel, in_specs=[in_smem()] + [in_vmem()] * 12, ou...  61.2 us
    pallas_call x1, Pallas kernels, on_device(): pl.pallas_call(leaf_kernel, in_specs=[in_vmem()] * 2, out_specs=[in_vmem(...  16.8 us
    ppermute x21, starting transfers between devices, swapped(): return lax.ppermute(value, axis, pairs)  10.1 us
    pallas_call x1, Pallas kernels, on_device(): pl.pallas_call(functools.partial(side_kernel, blocks), in_specs=[in_smem(...  8.91 us
    pallas_call x1, Pallas kernels, on_device(): pl.pallas_call(left_kernel, grid=(NEAR,), in_specs=[pl.BlockSpec((LEAF, R...  7.63 us
    ppermute x2, starting transfers between devices, shifted(): return lax.ppermute(value, axis, pairs)  6.12 us
    pallas_call x1, Pallas kernels, on_device(): pl.pallas_call(couple_kernel, in_specs=[in_smem()] + [in_vmem()] * 9, out...  4.76 us
  transfers between devices with their start and end apart: 23, of which 8 were waited for; matrix products, arithmetic and copies ran while one was open for 0% of the time, Pallas kernels for 49%

profile of v1, /device:TPU:0, one launch (start us, length us, event | category | flops | bytes accessed | tf_op | source)
XLA Modules:
  0.0 203.1 jit_solution(1944520336429738160)
XLA Ops:
  0.6 0.0 slice-start
  0.6 1.1 slice.8
  1.8 0.0 copy-start
  1.8 0.1 pad_maximum_fusion
  1.9 3.0 %collective-permute-start.12 = (f32[768,256]{1,0:T(8,128)S(1)}, f32[768,256]{1,0:T(8,128)S(1)}, u32[]{:S(2)}, u32[]{:S(2)}) collective-permute-start(f32[768,256]{1,0:T(8,128)S(1)} %pad_maximum_fusion), channel_id=1, source_target_pairs={{0,4},{1,5},{2,6},{3,7},{4,8},{5,9},{6,10},{7,11},{8,12},{9,13},{1... | collective-permute-start | bytes 2359304 | tf_op jit(solution)/shard_map/ppermute | solution.py:288
  4.9 3.1 %collective-permute-start.16 = (f32[768,256]{1,0:T(8,128)S(1)}, f32[768,256]{1,0:T(8,128)}, u32[]{:S(2)}, u32[]{:S(2)}) collective-permute-start(f32[768,256]{1,0:T(8,128)S(1)} %pad_maximum_fusion), channel_id=1, source_target_pairs={{0,28},{1,29},{2,30},{3,31},{4,0},{5,1},{6,2},{7,3},{8,4},{9,5},{1... | collective-permute-start | bytes 2359304 | tf_op jit(solution)/shard_map/ppermute | solution.py:288
  8.0 1.6 collective-permute-start.4
  9.6 16.8 %leaf_factor.1 = (f32[256,512]{1,0:T(8,128)}, f32[256,256]{1,0:T(8,128)}) custom-call(f32[512,512]{1,0:T(8,128)} %bitcast.11, f32[512,512]{1,0:T(8,128)} %bitcast.6), custom_call_target="tpu_custom_call" | custom-call | tf_op jit(solution)/shard_map/leaf_factor/pallas_call | solution.py:328
  26.4 0.4 collective-permute-start.10
  26.8 7.3 %collective-permute-done.10.rest_10_ = f32[256,256]{1,0:T(8,128)} collective-permute-done((f32[256,256]{1,0:T(8,128)}, f32[256,256]{1,0:T(8,128)}, u32[]{:S(2)}, u32[]{:S(2)}) %collective-permute-start.10) | collective-permute-done | bytes 262176 | tf_op jit(solution)/shard_map/ppermute | solution.py:282
  34.1 0.5 collective-permute-start.1
  34.6 3.9 %collective-permute-done.12.rest_0_ = f32[768,256]{1,0:T(8,128)S(1)} collective-permute-done((f32[768,256]{1,0:T(8,128)S(1)}, f32[768,256]{1,0:T(8,128)S(1)}, u32[]{:S(2)}, u32[]{:S(2)}) %collective-permute-start.12) | collective-permute-done | bytes 786464 | tf_op jit(solution)/shard_map/ppermute | solution.py:288
  38.5 1.5 collective-permute-start.14
  40.0 0.8 collective-permute-done.16.rest_4_
  40.8 1.5 collective-permute-start.18
  42.3 0.0 collective-permute-start.5
  42.4 0.5 collective-permute-start.13
  42.8 1.4 collective-permute-done.5.s3
  44.2 0.1 collective-permute-start.17
  44.4 32.8 %collective-permute-done.14.rest_2_ = f32[768,256]{1,0:T(8,128)} collective-permute-done((f32[768,256]{1,0:T(8,128)S(1)}, f32[768,256]{1,0:T(8,128)}, u32[]{:S(2)}, u32[]{:S(2)}) %collective-permute-start.14) | collective-permute-done | bytes 786464 | tf_op jit(solution)/shard_map/ppermute | solution.py:282
  77.1 0.0 collective-permute-start.15
  77.1 14.1 %collective-permute-done.18.rest_6_ = f32[768,256]{1,0:T(8,128)} collective-permute-done((f32[768,256]{1,0:T(8,128)}, f32[768,256]{1,0:T(8,128)}, u32[]{:S(2)}, u32[]{:S(2)}) %collective-permute-start.18) | collective-permute-done | bytes 786464 | tf_op jit(solution)/shard_map/ppermute | solution.py:282
  91.2 7.6 %left_products.1 = (bf16[6,256,512]{2,1,0:T(8,128)(2,1)}, bf16[6,256,512]{2,1,0:T(8,128)(2,1)}) custom-call(f32[512,512]{1,0:T(8,128)} %bitcast.7, f32[6,512,512]{2,1,0:T(8,128)} %bitcast.8), custom_call_target="tpu_custom_call" | custom-call | tf_op jit(solution)/shard_map/left_products/pallas_call | solution.py:315
  98.9 4.5 %own_window.1.rest_4_ = f32[3,256,256]{2,1,0:T(8,128)} custom-call(s32[1]{0:T(128)} %bitcast.2.me_ref, s32[1,6]{1,0:T(1,128)} %near_ref.3, s32[1,5]{1,0:T(1,128)} %far_ref.3, bf16[6,256,512]{2,1,0:T(8,128)(2,1)} %get-tuple-element.10.high_ref, bf16[6,256,512]{2,1,0:T(8,128)(2,1)} %get-tuple-element.11.low_ref, f32[5,256,256]{2,1,0:T(8,128)} %bitcast.9, ...), custom_call_target="tpu_custom_call" | custom-call | tf_op jit(solution)/shard_map/own_window/pallas_call | solution.py:345
  103.3 0.0 collective-permute-done.1.rest_2_.p2
  103.3 0.7 collective-permute-start.7
  104.0 0.0 collective-permute-start
  104.0 0.0 collective-permute-done.17.rest_5_
  104.0 0.5 collective-permute-start.9
  104.5 0.0 collective-permute-done.15.rest_3_
  104.5 0.1 collective-permute-start.11
  104.6 0.4 collective-permute-start.2
  105.1 8.9 %side_windows.1.v0 = f32[256,512]{1,0:T(8,128)} custom-call(s32[1]{0:T(128)} %bitcast.2.me_ref, s32[1,6]{1,0:T(1,128)} %near_ref.3, s32[1,5]{1,0:T(1,128)} %far_ref.3, bf16[6,256,512]{2,1,0:T(8,128)(2,1)} %get-tuple-element.10.high_ref, bf16[6,256,512]{2,1,0:T(8,128)(2,1)} %get-tuple-element.11.low_ref, f32[5,256,256]{2,1,0:T(8,128)} %bitcast.10, ...), custom_call_target="tpu_custom_call" | custom-call | tf_op jit(solution)/shard_map/side_windows/pallas_call | solution.py:376
  114.0 0.0 collective-permute-done.9.rest_9_
  114.0 1.5 collective-permute-start.21
  115.5 0.0 collective-permute-done.11.rest_11_
  115.5 0.2 collective-permute-start.6
  115.7 0.5 copy-done.17
  116.2 7.9 %collective-permute-done.7.rest_6_ = f32[3,256,256]{2,1,0:T(8,128)S(1)} collective-permute-done((f32[3,256,256]{2,1,0:T(8,128)}, f32[3,256,256]{2,1,0:T(8,128)S(1)}, u32[]{:S(2)}, u32[]{:S(2)}) %collective-permute-start.7) | collective-permute-done | bytes 786464 | tf_op jit(solution)/shard_map/ppermute | solution.py:282
  124.1 0.5 collective-permute-start.20
  124.6 9.5 %collective-permute-done.21.v2 = f32[256,512]{1,0:T(8,128)S(1)} collective-permute-done((f32[256,512]{1,0:T(8,128)}, f32[256,512]{1,0:T(8,128)S(1)}, u32[]{:S(2)}, u32[]{:S(2)}) %collective-permute-start.21) | collective-permute-done | bytes 524320 | tf_op jit(solution)/shard_map/ppermute | solution.py:282
  134.2 0.9 copy-done.7
  135.0 0.3 copy-done.3
  135.3 0.9 copy-done.8
  136.2 61.2 %parent_factor.1 = (f32[256,768]{1,0:T(8,128)}, f32[256,256]{1,0:T(8,128)}) custom-call(s32[1]{0:T(128)} %bitcast.2.me_ref, f32[256,1024]{1,0:T(8,128)} %p0.1, f32[256,1024]{1,0:T(8,128)} %copy-done.2, f32[256,1024]{1,0:T(8,128)} %copy-done.1, f32[256,1024]{1,0:T(8,128)} %copy-done.3, f32[3,256,256]{2,1,0:T(8,128)} %own_window.1.rest_4_, ...), custom_call_target="tpu_custom_call" | custom-call | tf_op jit(solution)/shard_map/parent_factor/pallas_call | solution.py:357
  197.4 0.8 copy-done.13
  198.2 0.2 copy-done.14
  198.4 4.8 %coupling.1 = f32[256,768]{1,0:T(8,128)} custom-call(s32[1]{0:T(128)} %bitcast.2.me_ref, f32[256,1024]{1,0:T(8,128)} %p0.1, f32[256,1024]{1,0:T(8,128)} %copy-done.2, f32[256,1024]{1,0:T(8,128)} %copy-done.1, f32[256,1024]{1,0:T(8,128)} %copy-done.3, f32[256,512]{1,0:T(8,128)} %side_windows.1.v0, f32[256,512]{1,0:T(8,128)} %copy-done.13, ...), custom_call_target="tpu_custom_call" | custom-call | tf_op jit(solution)/shard_map/coupling/pallas_call | solution.py:387
  (44 shorter events, 0.1 us)
Async XLA Ops:
  0.6 1.1 slice-start
  1.8 32.3 %copy-start = (f32[256,1024]{1,0:T(8,128)S(1)}, f32[256,1024]{1,0:T(8,128)}, u32[]{:S(2)}) copy-start(f32[256,1024]{1,0:T(8,128)} %p0.1) | copy-start | bytes 3145732
  1.9 36.7 %collective-permute-start.12 = (f32[768,256]{1,0:T(8,128)S(1)}, f32[768,256]{1,0:T(8,128)S(1)}, u32[]{:S(2)}, u32[]{:S(2)}) collective-permute-start(f32[768,256]{1,0:T(8,128)S(1)} %pad_maximum_fusion), channel_id=1, source_target_pairs={{0,4},{1,5},{2,6},{3,7},{4,8},{5,9},{6,10},{7,11},{8,12},{9,13},{1... | collective-permute-start | bytes 2359304 | tf_op jit(solution)/shard_map/ppermute | solution.py:288
  4.9 36.0 %collective-permute-start.16 = (f32[768,256]{1,0:T(8,128)S(1)}, f32[768,256]{1,0:T(8,128)}, u32[]{:S(2)}, u32[]{:S(2)}) collective-permute-start(f32[768,256]{1,0:T(8,128)S(1)} %pad_maximum_fusion), channel_id=1, source_target_pairs={{0,28},{1,29},{2,30},{3,31},{4,0},{5,1},{6,2},{7,3},{8,4},{9,5},{1... | collective-permute-start | bytes 2359304 | tf_op jit(solution)/shard_map/ppermute | solution.py:288
  8.0 34.4 %collective-permute-start.4 = (f32[512,256]{1,0:T(8,128)S(1)}, f32[512,256]{1,0:T(8,128)S(1)}, u32[]{:S(2)}, u32[]{:S(2)}) collective-permute-start(f32[512,256]{1,0:T(8,128)S(1)} %slice.8), channel_id=1, source_target_pairs={{0,2},{1,3},{2,0},{3,1},{4,6},{5,7},{6,4},{7,5},{8,10},{9,11},{10,... | collective-permute-start | bytes 1572872 | tf_op jit(solution)/shard_map/ppermute | solution.py:282
  26.4 7.7 %collective-permute-start.10 = (f32[256,256]{1,0:T(8,128)}, f32[256,256]{1,0:T(8,128)}, u32[]{:S(2)}, u32[]{:S(2)}) collective-permute-start(f32[256,256]{1,0:T(8,128)} %get-tuple-element.12.rest_8_), channel_id=1, source_target_pairs={{0,2},{1,3},{2,0},{3,1},{4,6},{5,7},{6,4},{7,5},{8,10},{9,11},{10,... | collective-permute-start | bytes 786440 | tf_op jit(solution)/shard_map/ppermute | solution.py:282
  26.8 15.5 %collective-permute-start.3 = (f32[512,256]{1,0:T(8,128)S(1)}, f32[512,256]{1,0:T(8,128)S(1)}, u32[]{:S(2)}, u32[]{:S(2)}) collective-permute-start(f32[512,256]{1,0:T(8,128)S(1)} %slice.8), channel_id=1, source_target_pairs={{0,1},{1,0},{2,3},{3,2},{4,5},{5,4},{6,7},{7,6},{8,9},{9,8},{10,11... | collective-permute-start | bytes 1572872 | tf_op jit(solution)/shard_map/ppermute | solution.py:282
  34.1 69.2 %collective-permute-start.1 = (f32[256,1024]{1,0:T(8,128)S(1)}, f32[256,1024]{1,0:T(8,128)S(1)}, u32[]{:S(2)}, u32[]{:S(2)}) collective-permute-start(f32[256,1024]{1,0:T(8,128)S(1)} %copy-done), channel_id=1, source_target_pairs={{0,2},{1,3},{2,0},{3,1},{4,6},{5,7},{6,4},{7,5},{8,10},{9,11},{10,... | collective-permute-start | bytes 3145736 | tf_op jit(solution)/shard_map/ppermute | solution.py:282
  38.5 60.3 %copy-start.5 = (f32[768,256]{1,0:T(8,128)}, f32[768,256]{1,0:T(8,128)S(1)}, u32[]{:S(2)}) copy-start(f32[768,256]{1,0:T(8,128)S(1)} %collective-permute-done.12.rest_0_) | copy-start | bytes 2359300
  38.5 38.6 %collective-permute-start.14 = (f32[768,256]{1,0:T(8,128)S(1)}, f32[768,256]{1,0:T(8,128)}, u32[]{:S(2)}, u32[]{:S(2)}) collective-permute-start(f32[768,256]{1,0:T(8,128)S(1)} %collective-permute-done.12.rest_0_), channel_id=1, source_target_pairs={{0,2},{1,3},{2,0},{3,1},{4,6},{5,7},{6,4},{7,5},{8,10},{9,11},{10,... | collective-permute-start | bytes 2359304 | tf_op jit(solution)/shard_map/ppermute | solution.py:282
  40.8 50.4 %collective-permute-start.18 = (f32[768,256]{1,0:T(8,128)}, f32[768,256]{1,0:T(8,128)}, u32[]{:S(2)}, u32[]{:S(2)}) collective-permute-start(f32[768,256]{1,0:T(8,128)} %collective-permute-done.16.rest_4_), channel_id=1, source_target_pairs={{0,2},{1,3},{2,0},{3,1},{4,6},{5,7},{6,4},{7,5},{8,10},{9,11},{10,... | collective-permute-start | bytes 2359304 | tf_op jit(solution)/shard_map/ppermute | solution.py:282
  42.3 34.8 %copy-start.9 = (f32[512,256]{1,0:T(8,128)}, f32[512,256]{1,0:T(8,128)S(1)}, u32[]{:S(2)}) copy-start(f32[512,256]{1,0:T(8,128)S(1)} %collective-permute-done.4.s2) | copy-start | bytes 1572868
  42.3 1.9 collective-permute-start.5
  42.3 34.8 %copy-start.10 = (f32[512,256]{1,0:T(8,128)}, f32[512,256]{1,0:T(8,128)S(1)}, u32[]{:S(2)}) copy-start(f32[512,256]{1,0:T(8,128)S(1)} %collective-permute-done.3.s1) | copy-start | bytes 1572868
  42.4 61.7 %collective-permute-start.13 = (f32[768,256]{1,0:T(8,128)S(1)}, f32[768,256]{1,0:T(8,128)}, u32[]{:S(2)}, u32[]{:S(2)}) collective-permute-start(f32[768,256]{1,0:T(8,128)S(1)} %collective-permute-done.12.rest_0_), channel_id=1, source_target_pairs={{0,1},{1,0},{2,3},{3,2},{4,5},{5,4},{6,7},{7,6},{8,9},{9,8},{10,11... | collective-permute-start | bytes 2359304 | tf_op jit(solution)/shard_map/ppermute | solution.py:282
  44.2 47.0 %copy-start.11 = (f32[512,256]{1,0:T(8,128)}, f32[512,256]{1,0:T(8,128)S(1)}, u32[]{:S(2)}) copy-start(f32[512,256]{1,0:T(8,128)S(1)} %collective-permute-done.5.s3) | copy-start | bytes 1572868
  44.2 59.8 %collective-permute-start.17 = (f32[768,256]{1,0:T(8,128)}, f32[768,256]{1,0:T(8,128)}, u32[]{:S(2)}, u32[]{:S(2)}) collective-permute-start(f32[768,256]{1,0:T(8,128)} %collective-permute-done.16.rest_4_), channel_id=1, source_target_pairs={{0,1},{1,0},{2,3},{3,2},{4,5},{5,4},{6,7},{7,6},{8,9},{9,8},{10,11... | collective-permute-start | bytes 2359304 | tf_op jit(solution)/shard_map/ppermute | solution.py:282
  77.1 27.4 %collective-permute-start.15 = (f32[768,256]{1,0:T(8,128)}, f32[768,256]{1,0:T(8,128)}, u32[]{:S(2)}, u32[]{:S(2)}) collective-permute-start(f32[768,256]{1,0:T(8,128)} %collective-permute-done.14.rest_2_), channel_id=1, source_target_pairs={{0,1},{1,0},{2,3},{3,2},{4,5},{5,4},{6,7},{7,6},{8,9},{9,8},{10,11... | collective-permute-start | bytes 2359304 | tf_op jit(solution)/shard_map/ppermute | solution.py:282
  91.2 13.4 %collective-permute-start.19 = (f32[768,256]{1,0:T(8,128)}, f32[768,256]{1,0:T(8,128)}, u32[]{:S(2)}, u32[]{:S(2)}) collective-permute-start(f32[768,256]{1,0:T(8,128)} %collective-permute-done.18.rest_6_), channel_id=1, source_target_pairs={{0,1},{1,0},{2,3},{3,2},{4,5},{5,4},{6,7},{7,6},{8,9},{9,8},{10,11... | collective-permute-start | bytes 2359304 | tf_op jit(solution)/shard_map/ppermute | solution.py:282
  98.9 5.2 %copy-start.15 = (f32[256,256]{1,0:T(8,128)S(1)}, f32[256,256]{1,0:T(8,128)}, u32[]{:S(2)}) copy-start(f32[256,256]{1,0:T(8,128)} %get-tuple-element.12.rest_8_) | copy-start | bytes 786436
  103.3 12.1 %copy-start.4 = (f32[3,256,256]{2,1,0:T(8,128)S(1)}, f32[3,256,256]{2,1,0:T(8,128)}, u32[]{:S(2)}) copy-start(f32[3,256,256]{2,1,0:T(8,128)} %own_window.1.rest_4_) | copy-start | bytes 2359300
  103.3 10.6 %copy-start.1 = (f32[256,1024]{1,0:T(8,128)}, f32[256,1024]{1,0:T(8,128)S(1)}, u32[]{:S(2)}) copy-start(f32[256,1024]{1,0:T(8,128)S(1)} %collective-permute-done.1.rest_2_.p2) | copy-start | bytes 3145732
  103.3 20.7 %collective-permute-start.7 = (f32[3,256,256]{2,1,0:T(8,128)}, f32[3,256,256]{2,1,0:T(8,128)S(1)}, u32[]{:S(2)}, u32[]{:S(2)}) collective-permute-start(f32[3,256,256]{2,1,0:T(8,128)} %own_window.1.rest_4_), channel_id=1, source_target_pairs={{0,2},{1,3},{2,0},{3,1},{4,6},{5,7},{6,4},{7,5},{8,10},{9,11},{10,... | collective-permute-start | bytes 2359304 | tf_op jit(solution)/shard_map/ppermute | solution.py:282
  104.0 20.0 %collective-permute-start = (f32[256,1024]{1,0:T(8,128)S(1)}, f32[256,1024]{1,0:T(8,128)S(1)}, u32[]{:S(2)}, u32[]{:S(2)}) collective-permute-start(f32[256,1024]{1,0:T(8,128)S(1)} %copy-done), channel_id=1, source_target_pairs={{0,1},{1,0},{2,3},{3,2},{4,5},{5,4},{6,7},{7,6},{8,9},{9,8},{10,11... | collective-permute-start | bytes 3145736 | tf_op jit(solution)/shard_map/ppermute | solution.py:282
  104.0 9.9 %collective-permute-start.9 = (f32[256,256]{1,0:T(8,128)S(1)}, f32[256,256]{1,0:T(8,128)S(1)}, u32[]{:S(2)}, u32[]{:S(2)}) collective-permute-start(f32[256,256]{1,0:T(8,128)S(1)} %copy-done.15), channel_id=1, source_target_pairs={{0,1},{1,0},{2,3},{3,2},{4,5},{5,4},{6,7},{7,6},{8,9},{9,8},{10,11... | collective-permute-start | bytes 786440 | tf_op jit(solution)/shard_map/ppermute | solution.py:282
  104.5 10.9 %collective-permute-start.11 = (f32[256,256]{1,0:T(8,128)}, f32[256,256]{1,0:T(8,128)S(1)}, u32[]{:S(2)}, u32[]{:S(2)}) collective-permute-start(f32[256,256]{1,0:T(8,128)} %collective-permute-done.10.rest_10_), channel_id=1, source_target_pairs={{0,1},{1,0},{2,3},{3,2},{4,5},{5,4},{6,7},{7,6},{8,9},{9,8},{10,11... | collective-permute-start | bytes 786440 | tf_op jit(solution)/shard_map/ppermute | solution.py:282
  104.6 29.5 %collective-permute-start.2 = (f32[256,1024]{1,0:T(8,128)S(1)}, f32[256,1024]{1,0:T(8,128)S(1)}, u32[]{:S(2)}, u32[]{:S(2)}) collective-permute-start(f32[256,1024]{1,0:T(8,128)S(1)} %collective-permute-done.1.rest_2_.p2), channel_id=1, source_target_pairs={{0,1},{1,0},{2,3},{3,2},{4,5},{5,4},{6,7},{7,6},{8,9},{9,8},{10,11... | collective-permute-start | bytes 3145736 | tf_op jit(solution)/shard_map/ppermute | solution.py:282
  114.0 1.7 copy-start.16
  114.0 20.1 %collective-permute-start.21 = (f32[256,512]{1,0:T(8,128)}, f32[256,512]{1,0:T(8,128)S(1)}, u32[]{:S(2)}, u32[]{:S(2)}) collective-permute-start(f32[256,512]{1,0:T(8,128)} %side_windows.1.v0), channel_id=1, source_target_pairs={{0,2},{1,3},{2,0},{3,1},{4,6},{5,7},{6,4},{7,5},{8,10},{9,11},{10,... | collective-permute-start | bytes 1572872 | tf_op jit(solution)/shard_map/ppermute | solution.py:282
  115.5 0.7 copy-start.17
  115.5 18.6 %collective-permute-start.6 = (f32[3,256,256]{2,1,0:T(8,128)S(1)}, f32[3,256,256]{2,1,0:T(8,128)S(1)}, u32[]{:S(2)}, u32[]{:S(2)}) collective-permute-start(f32[3,256,256]{2,1,0:T(8,128)S(1)} %copy-done.4), channel_id=1, source_target_pairs={{0,1},{1,0},{2,3},{3,2},{4,5},{5,4},{6,7},{7,6},{8,9},{9,8},{10,11... | collective-permute-start | bytes 2359304 | tf_op jit(solution)/shard_map/ppermute | solution.py:282
  124.1 10.1 %copy-start.6 = (f32[3,256,256]{2,1,0:T(8,128)}, f32[3,256,256]{2,1,0:T(8,128)S(1)}, u32[]{:S(2)}) copy-start(f32[3,256,256]{2,1,0:T(8,128)S(1)} %collective-permute-done.7.rest_6_) | copy-start | bytes 2359300
  124.1 10.1 %collective-permute-start.8 = (f32[3,256,256]{2,1,0:T(8,128)S(1)}, f32[3,256,256]{2,1,0:T(8,128)S(1)}, u32[]{:S(2)}, u32[]{:S(2)}) collective-permute-start(f32[3,256,256]{2,1,0:T(8,128)S(1)} %collective-permute-done.7.rest_6_), channel_id=1, source_target_pairs={{0,1},{1,0},{2,3},{3,2},{4,5},{5,4},{6,7},{7,6},{8,9},{9,8},{10,11... | collective-permute-start | bytes 2359304 | tf_op jit(solution)/shard_map/ppermute | solution.py:282
  124.1 10.1 %copy-start.2 = (f32[256,1024]{1,0:T(8,128)}, f32[256,1024]{1,0:T(8,128)S(1)}, u32[]{:S(2)}) copy-start(f32[256,1024]{1,0:T(8,128)S(1)} %collective-permute-done.rest_1_.p1) | copy-start | bytes 3145732
  124.1 73.3 %collective-permute-start.20 = (f32[256,512]{1,0:T(8,128)}, f32[256,512]{1,0:T(8,128)S(1)}, u32[]{:S(2)}, u32[]{:S(2)}) collective-permute-start(f32[256,512]{1,0:T(8,128)} %side_windows.1.v0), channel_id=1, source_target_pairs={{0,1},{1,0},{2,3},{3,2},{4,5},{5,4},{6,7},{7,6},{8,9},{9,8},{10,11... | collective-permute-start | bytes 1572872 | tf_op jit(solution)/shard_map/ppermute | solution.py:282
  134.1 63.3 %copy-start.12 = (f32[256,512]{1,0:T(8,128)}, f32[256,512]{1,0:T(8,128)S(1)}, u32[]{:S(2)}) copy-start(f32[256,512]{1,0:T(8,128)S(1)} %collective-permute-done.21.v2) | copy-start | bytes 1572868
  134.1 63.3 %collective-permute-start.22 = (f32[256,512]{1,0:T(8,128)S(1)}, f32[256,512]{1,0:T(8,128)S(1)}, u32[]{:S(2)}, u32[]{:S(2)}) collective-permute-start(f32[256,512]{1,0:T(8,128)S(1)} %collective-permute-done.21.v2), channel_id=1, source_target_pairs={{0,1},{1,0},{2,3},{3,2},{4,5},{5,4},{6,7},{7,6},{8,9},{9,8},{10,11... | collective-permute-start | bytes 1572872 | tf_op jit(solution)/shard_map/ppermute | solution.py:282
  134.1 0.9 copy-start.7
  134.1 1.2 copy-start.3
  135.3 0.9 copy-start.8
  197.4 0.8 copy-start.13
  197.4 1.0 copy-start.14

commit v2 on v1

v2 whole, which is shorter than its diff:
```python
import functools

import jax
import jax.numpy as jnp
from jax import lax
from jax.experimental import pallas as pl
from jax.experimental.pallas import tpu as pltpu
from jax.sharding import PartitionSpec as P

LEAF = 512
RANK = 256
NEAR = 6
GROUP = 4
REDUN = 256
PAR = 1024
PRED = 768
FAR = 5
TILE = 128
ROWS = 8
WIDE = PRED + 2 * RANK
EARLY = 4
MIDDLE = 30_000_000_000

VMEM_BYTES = 56 * 1024 * 1024

NN = (((1,), (0,)), ((), ()))
TN = (((0,), (0,)), ((), ()))


def params():
    return pltpu.CompilerParams(vmem_limit_bytes=VMEM_BYTES)


def in_vmem():
    return pl.BlockSpec(memory_space=pltpu.VMEM)


def in_smem():
    return pl.BlockSpec(memory_space=pltpu.SMEM)


def split(value):
    high = value.astype(jnp.bfloat16)
    low = (value - high.astype(jnp.float32)).astype(jnp.bfloat16)
    return high, low


def dot3(left, right, dims=NN):
    def one(a, b):
        return lax.dot_general(a, b, dims, preferred_element_type=jnp.float32)

    return one(left[0], right[0]) + (one(left[0], right[1]) + one(left[1], right[0]))


def lane_spread(value, lane):
    return jnp.broadcast_to(value[:, lane : lane + 1], (ROWS, TILE))


def row_spread(value, row):
    return jnp.broadcast_to(value[row : row + 1, :], (ROWS, TILE))


def small_inverse(entry):
    entry = dict(entry)
    low = {}
    inv = {}
    for j in range(ROWS):
        root = lax.rsqrt(entry[j, j])
        for i in range(j + 1, ROWS):
            low[i, j] = entry[i, j] * root
        for k in range(j + 1, ROWS):
            for i in range(k, ROWS):
                entry[i, k] = entry[i, k] - low[i, j] * low[k, j]
        inv[j, j] = root
        for t in range(j):
            total = low[j, t] * inv[t, t]
            for k in range(t + 1, j):
                total = total + low[j, k] * inv[k, t]
            inv[j, t] = -(total * root)
    return inv


def weighted(inv, j, values):
    total = inv[j, 0] * values[0]
    for t in range(1, j + 1):
        total = total + inv[j, t] * values[t]
    return total


def tile_factor(square):
    count = TILE // ROWS
    row = lax.broadcasted_iota(jnp.int32, (ROWS, TILE), 0)
    col = lax.broadcasted_iota(jnp.int32, (ROWS, TILE), 1)
    left = [square[ROWS * i : ROWS * (i + 1), :] for i in range(count)]
    right = [jnp.where(row + ROWS * i == col, 1.0, 0.0).astype(jnp.float32) for i in range(count)]
    upper = []
    inverse = []
    pad1 = jnp.zeros((ROWS, TILE), jnp.float32)
    pad2 = jnp.zeros((ROWS, 2 * TILE), jnp.float32)
    for k in range(count):
        cols = [lane_spread(left[k], ROWS * k + j) for j in range(ROWS)]
        inv = small_inverse(
            {(i, j): row_spread(cols[j], i) for j in range(ROWS) for i in range(j, ROWS)}
        )
        left_rows = [row_spread(left[k], t) for t in range(ROWS)]
        right_rows = [row_spread(right[k], t) for t in range(ROWS)]
        u_rows = m_rows = None
        for j in range(ROWS):
            weight = inv[ROWS - 1, j]
            for i in range(ROWS - 2, j - 1, -1):
                weight = jnp.where(row == i, inv[i, j], weight)
            if j > 0:
                weight = jnp.where(row >= j, weight, 0.0)
            u_term, m_term = weight * left_rows[j], weight * right_rows[j]
            u_rows = u_term if u_rows is None else u_rows + u_term
            m_rows = m_term if m_rows is None else m_rows + m_term
        u_rows = jnp.where(col >= row + ROWS * k, u_rows, 0.0)
        upper.append(u_rows)
        inverse.append(m_rows)
        if k == count - 1:
            break
        raw = [lane_spread(left[k + 1], ROWS * k + t) for t in range(ROWS)]
        u_total = m_total = None
        for j in range(ROWS):
            side = weighted(inv, j, raw)
            u_term = side * weighted(inv, j, left_rows)
            m_term = side * row_spread(m_rows, j)
            u_total = u_term if u_total is None else u_total + u_term
            m_total = m_term if m_total is None else m_total + m_term
        left[k + 1] = left[k + 1] - u_total
        right[k + 1] = right[k + 1] - m_total
        if k == count - 2:
            continue
        both = jnp.concatenate([u_rows, m_rows], axis=1)
        high = both.astype(jnp.bfloat16).astype(jnp.float32)
        low = both - high
        lhs = jnp.concatenate([high[:, :TILE], high[:, :TILE], low[:, :TILE], pad1], axis=0)
        rhs = jnp.concatenate([high, low, high, pad2], axis=0)
        update = lax.dot_general(
            lhs.astype(jnp.bfloat16),
            rhs.astype(jnp.bfloat16),
            TN,
            preferred_element_type=jnp.float32,
        )
        for i in range(k + 2, count):
            rows = slice(ROWS * i, ROWS * (i + 1))
            left[i] = left[i] - update[rows, :TILE]
            right[i] = right[i] - update[rows, TILE:]
    return jnp.concatenate(upper, axis=0), jnp.concatenate(inverse, axis=0)


def leaf_kernel(diag_ref, basis_ref, after1, out_ref, schur_ref, work, u_tile, m_tile):
    basis = split(basis_ref[...])
    half = split(dot3(split(diag_ref[...]), basis))
    redundant = [part[:, :REDUN] for part in basis]
    skeleton = [part[:, REDUN:] for part in basis]
    top = dot3(redundant, half, TN)
    square = top[:, :REDUN]
    work[:, :REDUN] = 0.5 * (square + square.T)
    work[:, REDUN:] = top[:, REDUN:]
    schur_ref[...] = dot3(skeleton, [part[:, REDUN:] for part in half], TN)

    def step(k, carry):
        rows = pl.ds(pl.multiple_of(k * TILE, TILE), TILE)
        upper, inverse = tile_factor(work[rows, rows])
        u_tile[...] = upper
        m_tile[...] = inverse
        new_rows = dot3(split(m_tile[...]), split(work[rows, :]))
        work[rows, :] = new_rows
        work[rows, rows] = u_tile[...]

        @pl.when(k == 0)
        def _():
            parts = split(new_rows)
            side = [part[:, TILE:REDUN] for part in parts]
            work[TILE:, TILE:] = work[TILE:, TILE:] - dot3(side, [part[:, TILE:] for part in parts], TN)

        return carry

    lax.fori_loop(0, REDUN // TILE, step, 0)
    row = lax.broadcasted_iota(jnp.int32, (REDUN, REDUN), 0)
    col = lax.broadcasted_iota(jnp.int32, (REDUN, REDUN), 1)
    out_ref[:, :REDUN] = jnp.where(row <= col, work[:, :REDUN], 0.0).T
    coupled = work[:, REDUN:]
    out_ref[:, REDUN:] = coupled
    parts = split(coupled)
    schur_ref[...] = schur_ref[...] - dot3(parts, parts, TN)


def left_kernel(skel_ref, near_ref, after1, high_ref, low_ref, skel_high, skel_low):
    @pl.when(pl.program_id(0) == 0)
    def _():
        high, low = split(skel_ref[...].T)
        skel_high[...] = high
        skel_low[...] = low

    high, low = split(dot3((skel_high[...], skel_low[...]), split(near_ref[0])))
    high_ref[0] = high
    low_ref[0] = low


def source_of(leaf, near_ref, far_ref):
    slot = jnp.int32(0)
    for m in range(NEAR):
        slot = slot + jnp.where(near_ref[0, m] == leaf, m, 0)
    for f in range(FAR):
        slot = slot + jnp.where(far_ref[0, f] == leaf, NEAR + f, 0)
    return slot, jnp.minimum(slot, NEAR - 1), jnp.maximum(slot - NEAR, 0)


def sibling_slots(me_ref, near_ref, far_ref):
    return [source_of(jnp.bitwise_xor(me_ref[0], s), near_ref, far_ref) for s in range(1, GROUP)]


def sibling_kernel(me_ref, near_ref, far_ref, skel_ref, near_hbm, high_ref, low_ref, held, sems):
    slots = sibling_slots(me_ref, near_ref, far_ref)
    copies = [
        pltpu.make_async_copy(near_hbm.at[m], held.at[s], sems.at[s])
        for s, (_, m, _) in enumerate(slots)
    ]
    for copy in copies:
        copy.start()
    skel = split(skel_ref[...].T)
    for s in range(GROUP - 1):
        copies[s].wait()

        @pl.when(slots[s][0] < NEAR)
        def _(s=s):
            high, low = split(dot3(skel, split(held[s])))
            high_ref[s] = high
            low_ref[s] = low


def own_kernel(
    me_ref, near_ref, far_ref, high_ref, low_ref, far_hbm, schur_ref, s1, s2, s3, out_ref, sems
):
    slots = sibling_slots(me_ref, near_ref, far_ref)
    copies = [
        pltpu.make_async_copy(far_hbm.at[f], out_ref.at[s + 1], sems.at[s])
        for s, (_, _, f) in enumerate(slots)
    ]
    for copy in copies:
        copy.start()
    out_ref[0] = schur_ref[...]
    for s, sibling in enumerate((s1, s2, s3)):
        copies[s].wait()

        @pl.when(slots[s][0] < NEAR)
        def _(s=s, sibling=sibling):
            out_ref[s + 1] = dot3((high_ref[s], low_ref[s]), split(sibling[...]))


def side_kernel(blocks, me_ref, near_ref, far_ref, high_hbm, low_hbm, far_hbm, *rest):
    zs, (after1, out_ref, z_held, high_held, low_held, far_held, h_high, h_low, s_high, s_low, sems) = (
        rest[:8],
        rest[8:],
    )
    slots = []
    z_copies = []
    near_copies = []
    far_copies = []
    for side, shift in enumerate((blocks - GROUP, GROUP)):
        for s in range(GROUP):
            n = side * GROUP + s
            leaf = lax.rem(jnp.bitwise_xor(me_ref[0], s) + shift, blocks)
            slot, m, f = source_of(leaf, near_ref, far_ref)
            slots.append(slot)
            z_copies.append(pltpu.make_async_copy(zs[n], z_held.at[n], sems.at[0, n]))
            near_copies.append(
                [
                    pltpu.make_async_copy(high_hbm.at[m], high_held.at[n], sems.at[1, n]),
                    pltpu.make_async_copy(low_hbm.at[m], low_held.at[n], sems.at[2, n]),
                ]
            )
            far_copies.append(pltpu.make_async_copy(far_hbm.at[f], far_held.at[n], sems.at[1, n]))
    for n in range(2 * GROUP):
        z_copies[n].start()

        @pl.when(slots[n] < NEAR)
        def _(n=n):
            for copy in near_copies[n]:
                copy.start()

        @pl.when(slots[n] >= NEAR)
        def _(n=n):
            far_copies[n].start()

    for side in range(2):
        for s in range(GROUP):
            n = side * GROUP + s
            cols = slice(s * RANK, (s + 1) * RANK)
            z_copies[n].wait()

            @pl.when(slots[n] < NEAR)
            def _(n=n, cols=cols):
                for copy in near_copies[n]:
                    copy.wait()
                high, low = split(dot3((high_held[n], low_held[n]), split(z_held[n, :LEAF, :])))
                h_high[:, cols] = high
                h_low[:, cols] = low

            @pl.when(slots[n] >= NEAR)
            def _(n=n, cols=cols):
                far_copies[n].wait()
                high, low = split(far_held[n])
                h_high[:, cols] = high
                h_low[:, cols] = low

            high, low = split(z_held[n, LEAF:, :])
            s_high[cols, :] = high
            s_low[cols, :] = low
        out_ref[:, side * RANK : (side + 1) * RANK] = dot3(
            (h_high[...], h_low[...]), (s_high[...], s_low[...])
        )


def partial_sums(p_high, p_low, h_refs, first, v_high, v_low):
    for s in range(2):
        line = [h_refs[s][(first + s) ^ t] for t in range(GROUP)]
        line = split(jnp.concatenate(line, axis=1))
        high, low = split(dot3(line, (p_high[...], p_low[...])))
        rows = slice(s * RANK, (s + 1) * RANK)
        v_high[rows, :] = high
        v_low[rows, :] = low


def chip_kernel(
    me_ref, p0, p1, p2, p3, h0, h1, after1, p_high, p_low, t_high, t_low, part_ref, v_high, v_low
):
    member = lax.rem(me_ref[0], GROUP)
    slab = pl.ds(pl.multiple_of(member * RANK, RANK), RANK)
    for s, base in enumerate((p0, p1, p2, p3)):
        rows = slice(s * RANK, (s + 1) * RANK)
        high, low = split(base[...])
        p_high[rows, :] = high
        p_low[rows, :] = low
        high, low = split(base[:, slab].T)
        t_high[:, rows] = high
        t_low[:, rows] = low
    partial_sums(p_high, p_low, (h0, h1), 0, v_high, v_low)
    half = slice(0, 2 * RANK)
    for m in range(GROUP):
        cols = slice(m * RANK, (m + 1) * RANK)
        part_ref[cols, :] = dot3(
            (p_high[half, cols], p_low[half, cols]), (v_high[...], v_low[...]), TN
        )


def eliminate(work, u_tile, m_tile, first, last):
    def step(k, carry):
        rows = pl.ds(pl.multiple_of(k * TILE, TILE), TILE)
        upper, inverse = tile_factor(work[rows, rows])
        u_tile[...] = upper
        m_tile[...] = inverse
        new_rows = dot3(split(m_tile[...]), split(work[rows, :]))
        work[rows, :] = new_rows
        work[rows, rows] = u_tile[...]
        parts = split(new_rows)
        for i in range(first + 1, PRED // TILE):

            @pl.when(i > k)
            def _(i=i):
                below = slice(i * TILE, (i + 1) * TILE)
                side = [part[:, below] for part in parts]
                right = [part[:, i * TILE :] for part in parts]
                work[below, i * TILE :] = work[below, i * TILE :] - dot3(side, right, TN)

        return carry

    lax.fori_loop(first, last, step, 0)


def parent_kernel(
    me_ref, p_high, p_low, part_ref, h2, h3, work, edge_ref, v_high, v_low, whole, u_tile, m_tile
):
    member = lax.rem(me_ref[0], GROUP)
    partial_sums(p_high, p_low, (h2, h3), 2, v_high, v_low)
    half = slice(2 * RANK, PAR)
    for m in range(GROUP):
        cols = slice(m * RANK, (m + 1) * RANK)
        whole[cols, :] = part_ref[cols, :] + dot3(
            (p_high[half, cols], p_low[half, cols]), (v_high[...], v_low[...]), TN
        )
    square = whole[:PRED, :PRED]
    work[:, :PRED] = 0.5 * (square + square.T)
    work[:, PRED:PAR] = whole[:PRED, PRED:]
    work[:, PAR:] = whole[PRED:, :PRED].T
    slab = pl.ds(pl.multiple_of(member * RANK, RANK), RANK)
    edge_ref[...] = whole[slab, PRED:]
    eliminate(work, u_tile, m_tile, 0, EARLY)


def finish_kernel(me_ref, work_hbm, edge_in, after1, factor_ref, edge_ref, work, u_tile, m_tile, sems):
    member = lax.rem(me_ref[0], GROUP)
    done = EARLY * TILE
    open_rows = pltpu.make_async_copy(work_hbm.at[done:, :], work.at[done:, :], sems.at[0])
    held_rows = pltpu.make_async_copy(work_hbm.at[:done, :], work.at[:done, :], sems.at[1])
    open_rows.start()
    held_rows.start()
    open_rows.wait()
    eliminate(work, u_tile, m_tile, EARLY, PRED // TILE)
    held_rows.wait()
    row = lax.broadcasted_iota(jnp.int32, (PRED, RANK), 0)
    col = lax.broadcasted_iota(jnp.int32, (PRED, RANK), 1) + member * RANK
    slab = pl.ds(pl.multiple_of(member * RANK, RANK), RANK)
    factor_ref[...] = jnp.where(row <= col, work[:, slab], 0.0).T
    edge_ref[...] = edge_in[...]

    @pl.when(member == GROUP - 1)
    def _():
        product = dot3(split(work[:, PAR:]), split(work[:, PRED:PAR]), TN)
        edge_ref[...] = edge_in[...] - product


def couple_kernel(t_high, t_low, v0, v1, v2, v3, edge_ref, out_ref):
    total = jnp.zeros((RANK, 2 * RANK), jnp.float32)
    for s, v_ref in enumerate((v0, v1, v2, v3)):
        cols = slice(s * RANK, (s + 1) * RANK)
        total = total + dot3((t_high[:, cols], t_low[:, cols]), split(v_ref[...]))
    out_ref[:, :RANK] = total[:, :RANK]
    out_ref[:, RANK : 2 * RANK] = edge_ref[...]
    out_ref[:, 2 * RANK :] = total[:, RANK:]


def swapped(value, axis, mask):
    pairs = [(source, source ^ mask) for source in range(lax.axis_size(axis))]
    return lax.ppermute(value, axis, pairs)


def shifted(value, axis, steps):
    count = lax.axis_size(axis)
    pairs = [(source, (source + steps) % count) for source in range(count)]
    return lax.ppermute(value, axis, pairs)


def after(value, *earlier):
    return lax.optimization_barrier((value, *earlier))[0]


def gathered(value, axis, *earlier):
    core = swapped(value, axis, 1)
    chip = swapped(value, axis, 2)
    both = swapped(after(chip, *earlier), axis, 1)
    return [value, core, chip, both]


def call(kernel, name, ins, outs, scratch, *operands, flops=1):
    return pl.pallas_call(
        kernel,
        in_specs=ins,
        out_specs=[in_vmem()] * len(outs),
        out_shape=[jax.ShapeDtypeStruct(shape, dtype) for shape, dtype in outs],
        scratch_shapes=scratch,
        compiler_params=params(),
        cost_estimate=pl.CostEstimate(flops=flops, bytes_accessed=1, transcendentals=0),

        name=name,
    )(*operands)


def anywhere():
    return pl.BlockSpec(memory_space=pl.ANY)


def on_device(
    diag_block, near_blocks, far_coupling, leaf_basis, parent_basis, near_index, far_index
):
    blocks = lax.axis_size("blk")
    me = lax.axis_index("blk").astype(jnp.int32).reshape(1)
    basis = leaf_basis[0]
    skeleton = basis[:, REDUN:]
    near = near_blocks[0]
    far = far_coupling[0]
    f32, b16 = jnp.float32, jnp.bfloat16

    load = jnp.concatenate([skeleton, parent_basis[:, PRED:]], axis=0)
    prev_load = shifted(load, "blk", GROUP)
    next_load = shifted(load, "blk", -GROUP)

    base_chip = swapped(parent_basis, "blk", 2)

    sib_high, sib_low = call(
        sibling_kernel,
        "sibling_products",
        [in_smem()] * 3 + [in_vmem(), anywhere()],
        [((GROUP - 1, RANK, LEAF), b16)] * 2,
        [pltpu.VMEM((GROUP - 1, LEAF, LEAF), f32), pltpu.SemaphoreType.DMA((GROUP - 1,))],
        me,
        near_index,
        far_index,
        skeleton,
        near,
    )
    leaf_out, leaf_schur = call(
        leaf_kernel,
        "leaf_factor",
        [in_vmem()] * 2 + [anywhere()],
        [((REDUN, LEAF), f32), ((RANK, RANK), f32)],
        [pltpu.VMEM((REDUN, LEAF), f32), pltpu.VMEM((TILE, TILE), f32), pltpu.VMEM((TILE, TILE), f32)],
        diag_block[0],
        basis,
        sib_high,
        flops=MIDDLE,
    )
    skels = gathered(skeleton, "blk")
    (own,) = call(
        own_kernel,
        "own_window",
        [in_smem()] * 3 + [in_vmem()] * 2 + [anywhere()] + [in_vmem()] * 4,
        [((GROUP, RANK, RANK), f32)],
        [pltpu.SemaphoreType.DMA((GROUP - 1,))],
        me,
        near_index,
        far_index,
        sib_high,
        sib_low,
        far,
        leaf_schur,
        *skels[1:],
    )
    own_core = swapped(own, "blk", 1)
    own_chip = swapped(own, "blk", 2)
    base_core = swapped(after(parent_basis, own), "blk", 1)
    base_both = swapped(after(base_chip, own, prev_load, next_load), "blk", 1)
    bases = [parent_basis, base_core, base_chip, base_both]

    left_high, left_low = pl.pallas_call(
        left_kernel,
        grid=(NEAR,),
        in_specs=[
            pl.BlockSpec((LEAF, RANK), lambda m: (0, 1)),
            pl.BlockSpec((1, LEAF, LEAF), lambda m: (m, 0, 0)),
            anywhere(),
        ],
        out_specs=[pl.BlockSpec((1, RANK, LEAF), lambda m: (m, 0, 0))] * 2,
        out_shape=[jax.ShapeDtypeStruct((NEAR, RANK, LEAF), b16)] * 2,
        scratch_shapes=[pltpu.VMEM((RANK, LEAF), b16)] * 2,
        compiler_params=params(),
        cost_estimate=pl.CostEstimate(flops=1, bytes_accessed=1, transcendentals=0),

        name="left_products",
    )(basis, near, own)
    p_high, p_low, t_high, t_low, part = call(
        chip_kernel,
        "chip_sums",
        [in_smem()] + [in_vmem()] * 6 + [anywhere()],
        [((PAR, PAR), b16)] * 2 + [((RANK, PAR), b16)] * 2 + [((PAR, PAR), f32)],
        [pltpu.VMEM((2 * RANK, PAR), b16)] * 2,
        me,
        *bases,
        own,
        own_core,
        left_high,
    )
    own_both = swapped(after(own_chip, part), "blk", 1)
    prev_load = after(prev_load, own_chip)
    next_load = after(next_load, own_chip)
    tiles = [pltpu.VMEM((TILE, TILE), f32)] * 2
    work, edge_rows = call(
        parent_kernel,
        "parent_factor",
        [in_smem()] + [in_vmem()] * 5,
        [((PRED, WIDE), f32), ((RANK, RANK), f32)],
        [pltpu.VMEM((2 * RANK, PAR), b16)] * 2 + [pltpu.VMEM((PAR, PAR), f32)] + tiles,
        me,
        p_high,
        p_low,
        part,
        own_chip,
        own_both,
    )
    from_prev = gathered(prev_load, "blk", edge_rows)
    from_next = gathered(next_load, "blk", edge_rows)
    (side,) = call(
        functools.partial(side_kernel, blocks),
        "side_windows",
        [in_smem()] * 3 + [anywhere()] * 12,
        [((RANK, 2 * RANK), f32)],
        [
            pltpu.VMEM((2 * GROUP, LEAF + RANK, RANK), f32),
            pltpu.VMEM((2 * GROUP, RANK, LEAF), b16),
            pltpu.VMEM((2 * GROUP, RANK, LEAF), b16),
            pltpu.VMEM((2 * GROUP, RANK, RANK), f32),
            pltpu.VMEM((RANK, PAR), b16),
            pltpu.VMEM((RANK, PAR), b16),
            pltpu.VMEM((PAR, RANK), b16),
            pltpu.VMEM((PAR, RANK), b16),
            pltpu.SemaphoreType.DMA((3, 2 * GROUP)),
        ],
        me,
        near_index,
        far_index,
        left_high,
        left_low,
        far,
        *from_prev,
        *from_next,
        edge_rows,
    )
    factor_rows, edge_rows = call(
        finish_kernel,
        "parent_finish",
        [in_smem(), anywhere(), in_vmem(), anywhere()],
        [((RANK, PRED), f32), ((RANK, RANK), f32)],
        [pltpu.VMEM((PRED, WIDE), f32)] + tiles + [pltpu.SemaphoreType.DMA((2,))],
        me,
        work,
        edge_rows,
        side,
    )
    sides = gathered(side, "blk", edge_rows)
    (coupling_rows,) = call(
        couple_kernel,
        "coupling",
        [in_vmem()] * 7,
        [((RANK, 3 * RANK), f32)],
        [],
        t_high,
        t_low,
        *sides,
        edge_rows,
    )
    return (leaf_out, factor_rows, coupling_rows)


def solution(mesh):
    placed = (
        P("blk", None, None),
        P("blk", None, None, None),
        P("blk", None, None, None),
        P("blk", None, None),
        P("blk", None),
        P("blk", None),
        P("blk", None),
    )
    return jax.shard_map(
        on_device,
        mesh=mesh,
        in_specs=placed,
        out_specs=(P("blk", None), P("blk", None), P("blk", None)),
        check_vma=False,
    )
```

time: 203 us -> 143 us (0.70)
  waiting for transfers between devices: 77.7 us -> 16.4 us
  local copies, waits for them, and re-layouts: 4.66 us -> 7.22 us
    ppermute x21 -> x18, waiting for transfers between devices: 72.9 us -> 8.36 us  [swapped(): return lax.ppermute(value, axis, pairs)]
    ppermute x2, waiting for transfers between devices: 4.74 us -> 8.08 us  [shifted(): return lax.ppermute(value, axis, pairs)]
    pallas_call x5 -> x8, Pallas kernels: 96.1 us -> 93.9 us  [call(): pl.pallas_call(kernel, in_specs=ins, out_specs=[in_vmem()] * len(outs), o...]
    unnamed x36 -> x40, local copies, waits for them, and re-layouts: 3.54 us -> 5.14 us
    ppermute x21 -> x18, starting transfers between devices: 10.1 us -> 10.8 us  [swapped(): return lax.ppermute(value, axis, pairs)]
  transfers between devices with their start and end apart: 23 -> 20, of which waited for: 8 -> 8; matrix products, arithmetic and copies ran while one was open for 0% -> 1% of each run, Pallas kernels for 49% -> 64%
where the time goes in v2:
time: 143 us
  Pallas kernels  102 us (71%)
  waiting for transfers between devices  16.4 us (11%)
  starting transfers between devices  15.8 us (11%)
  local copies, waits for them, and re-layouts  7.22 us (5%)
    pallas_call x8, Pallas kernels, call(): pl.pallas_call(kernel, in_specs=ins, out_specs=[in_vmem()] * len(outs), o...  93.9 us
    ppermute x18, starting transfers between devices, swapped(): return lax.ppermute(value, axis, pairs)  10.8 us
    ppermute x18, waiting for transfers between devices, swapped(): return lax.ppermute(value, axis, pairs)  8.36 us
    ppermute x2, waiting for transfers between devices, shifted(): return lax.ppermute(value, axis, pairs)  8.08 us
    pallas_call x1, Pallas kernels, on_device(): pl.pallas_call(left_kernel, grid=(NEAR,), in_specs=[pl.BlockSpec((LEAF, R...  7.71 us
    unnamed x40, local copies, waits for them, and re-layouts  5.14 us
    ppermute x2, starting transfers between devices, shifted(): return lax.ppermute(value, axis, pairs)  4.94 us
  transfers between devices with their start and end apart: 20, of which 8 were waited for; matrix products, arithmetic and copies ran while one was open for 1% of the time, Pallas kernels for 64%

profile of v2, /device:TPU:0, one launch (start us, length us, event | category | flops | bytes accessed | tf_op | source)
XLA Modules:
  0.0 142.8 jit_solution(15382156217555951263)
XLA Ops:
  0.6 1.1 slice.8.skel_ref
  1.7 0.0 copy-start
  1.7 3.0 %collective-permute-start.1 = (f32[512,256]{1,0:T(8,128)S(1)}, f32[512,256]{1,0:T(8,128)}, u32[]{:S(2)}, u32[]{:S(2)}) collective-permute-start(f32[512,256]{1,0:T(8,128)S(1)} %slice.8.skel_ref), channel_id=1, source_target_pairs={{0,2},{1,3},{2,0},{3,1},{4,6},{5,7},{6,4},{7,5},{8,10},{9,11},{10,... | collective-permute-start | bytes 1572872 | tf_op jit(solution)/shard_map/ppermute | solution.py:427
  4.7 0.0 collective-permute-start
  4.7 0.2 collective-permute-start.4
  4.9 1.0 slice.7
  5.9 0.9 pad_maximum_fusion
  6.8 1.9 %collective-permute-start.5 = (f32[768,256]{1,0:T(8,128)}, f32[768,256]{1,0:T(8,128)S(1)}, u32[]{:S(2)}, u32[]{:S(2)}) collective-permute-start(f32[768,256]{1,0:T(8,128)} %pad_maximum_fusion), channel_id=1, source_target_pairs={{0,4},{1,5},{2,6},{3,7},{4,8},{5,9},{6,10},{7,11},{8,12},{9,13},{1... | collective-permute-start | bytes 2359304 | tf_op jit(solution)/shard_map/ppermute | solution.py:433
  8.7 3.0 %collective-permute-start.6 = (f32[768,256]{1,0:T(8,128)}, f32[768,256]{1,0:T(8,128)S(1)}, u32[]{:S(2)}, u32[]{:S(2)}) collective-permute-start(f32[768,256]{1,0:T(8,128)} %pad_maximum_fusion), channel_id=1, source_target_pairs={{0,28},{1,29},{2,30},{3,31},{4,0},{5,1},{6,2},{7,3},{8,4},{9,5},{1... | collective-permute-start | bytes 2359304 | tf_op jit(solution)/shard_map/ppermute | solution.py:433
  11.8 4.6 %sibling_products.1 = (bf16[3,256,512]{2,1,0:T(8,128)(2,1)}, bf16[3,256,512]{2,1,0:T(8,128)(2,1)}) custom-call(s32[1]{0:T(128)} %bitcast.2.me_ref, s32[1,6]{1,0:T(1,128)} %near_ref.5, s32[1,5]{1,0:T(1,128)} %far_ref.5, f32[512,256]{1,0:T(8,128)} %copy-done, f32[6,512,512]{2,1,0:T(8,128)} %bitcast.5), custom_call_target="tpu_custom_call" | custom-call | flops 1 | bytes 1 | tf_op jit(solution)/shard_map/sibling_products/pallas_call | solution.py:448
  16.4 1.2 collective-permute-done.1.s2
  17.6 0.0 collective-permute-start.2
  17.6 13.3 %leaf_factor.1 = (f32[256,512]{1,0:T(8,128)}, f32[256,256]{1,0:T(8,128)}) custom-call(f32[512,512]{1,0:T(8,128)} %bitcast.12, f32[512,512]{1,0:T(8,128)} %bitcast.10, bf16[3,256,512]{2,1,0:T(8,128)(2,1)} %get-tuple-element.26.after1.high_ref), custom_call_target="tpu_custom_call" | custom-call | flops 30000001024 | bytes 1 | tf_op jit(solution)/shard_map/leaf_factor/pallas_call | solution.py:448
  30.9 0.0 collective-permute-done.2.s3
  30.9 0.8 copy-done.16
  31.7 4.8 %own_window.1.after1.h0 = f32[4,256,256]{2,1,0:T(8,128)} custom-call(s32[1]{0:T(128)} %bitcast.2.me_ref, s32[1,6]{1,0:T(1,128)} %near_ref.5, s32[1,5]{1,0:T(1,128)} %far_ref.5, bf16[3,256,512]{2,1,0:T(8,128)(2,1)} %get-tuple-element.26.after1.high_ref, bf16[3,256,512]{2,1,0:T(8,128)(2,1)} %get-tuple-element.28.low_ref, f32[5,256,256]{2,1,0:T(8,128)} %bitcast.7, ...), custom_call_target="tpu_custom_call" | custom-call | flops 1 | bytes 1 | tf_op jit(solution)/shard_map/own_window/pallas_call | solution.py:448
  36.5 0.7 collective-permute-start.3
  37.1 6.0 %collective-permute-done.5.rest_0_ = f32[768,256]{1,0:T(8,128)S(1)} collective-permute-done((f32[768,256]{1,0:T(8,128)}, f32[768,256]{1,0:T(8,128)S(1)}, u32[]{:S(2)}, u32[]{:S(2)}) %collective-permute-start.5) | collective-permute-done | bytes 786464 | tf_op jit(solution)/shard_map/ppermute | solution.py:433
  43.1 2.1 %collective-permute-done.6.rest_4_ = f32[768,256]{1,0:T(8,128)S(1)} collective-permute-done((f32[768,256]{1,0:T(8,128)}, f32[768,256]{1,0:T(8,128)S(1)}, u32[]{:S(2)}, u32[]{:S(2)}) %collective-permute-start.6) | collective-permute-done | bytes 786464 | tf_op jit(solution)/shard_map/ppermute | solution.py:433
  45.2 0.0 collective-permute-done.4.p2
  45.2 0.1 collective-permute-start.7
  45.3 0.5 collective-permute-start.8
  45.8 1.5 %collective-permute-start.9 = (f32[4,256,256]{2,1,0:T(8,128)}, f32[4,256,256]{2,1,0:T(8,128)S(1)}, u32[]{:S(2)}, u32[]{:S(2)}) collective-permute-start(f32[4,256,256]{2,1,0:T(8,128)} %own_window.1.after1.h0), channel_id=1, source_target_pairs={{0,2},{1,3},{2,0},{3,1},{4,6},{5,7},{6,4},{7,5},{8,10},{9,11},{10,... | collective-permute-start | bytes 3145736 | tf_op jit(solution)/shard_map/ppermute | solution.py:427
  47.3 7.7 %left_products.1 = (bf16[6,256,512]{2,1,0:T(8,128)(2,1)}, bf16[6,256,512]{2,1,0:T(8,128)(2,1)}) custom-call(f32[512,512]{1,0:T(8,128)} %bitcast.11, f32[6,512,512]{2,1,0:T(8,128)} %bitcast.6, f32[4,256,256]{2,1,0:T(8,128)} %own_window.1.after1.h0), custom_call_target="tpu_custom_call" | custom-call | flops 1 | bytes 1 | tf_op jit(solution)/shard_map/left_products/pallas_call | solution.py:527
  55.0 0.0 collective-permute-done.3.p1
  55.0 0.9 copy-done.3
  56.0 0.3 copy-done.4
  56.3 0.3 copy-done.5
  56.6 11.8 %chip_sums.1 = (bf16[1024,1024]{1,0:T(8,128)(2,1)}, bf16[1024,1024]{1,0:T(8,128)(2,1)}, bf16[256,1024]{1,0:T(8,128)(2,1)}, bf16[256,1024]{1,0:T(8,128)(2,1)}, f32[1024,1024]{1,0:T(8,128)}) custom-call(s32[1]{0:T(128)} %bitcast.2.me_ref, f32[256,1024]{1,0:T(8,128)} %p0.1, f32[256,1024]{1,0:T(8,128)} %copy-done.3, f32[256,1024]{1,0:T(8,128)} %copy-done.2, ...), custom_call_target="tpu_custom_call" | custom-call | flops 1 | bytes 1 | tf_op jit(solution)/shard_map/chip_sums/pallas_call | solution.py:448
  68.5 2.7 %collective-permute-done.9.h2 = f32[4,256,256]{2,1,0:T(8,128)S(1)} collective-permute-done((f32[4,256,256]{2,1,0:T(8,128)}, f32[4,256,256]{2,1,0:T(8,128)S(1)}, u32[]{:S(2)}, u32[]{:S(2)}) %collective-permute-start.9) | collective-permute-done | bytes 1048608 | tf_op jit(solution)/shard_map/ppermute | solution.py:427
  71.1 1.5 %collective-permute-start.12 = (f32[768,256]{1,0:T(8,128)S(1)}, f32[768,256]{1,0:T(8,128)S(1)}, u32[]{:S(2)}, u32[]{:S(2)}) collective-permute-start(f32[768,256]{1,0:T(8,128)S(1)} %collective-permute-done.5.rest_0_), channel_id=1, source_target_pairs={{0,2},{1,3},{2,0},{3,1},{4,6},{5,7},{6,4},{7,5},{8,10},{9,11},{10,... | collective-permute-start | bytes 2359304 | tf_op jit(solution)/shard_map/ppermute | solution.py:427
  72.6 0.5 collective-permute-start.15
  73.2 0.5 collective-permute-start.14
  73.7 0.1 collective-permute-done.10.h3
  73.8 1.0 copy-done.7
  74.8 36.3 %parent_factor.1 = (f32[768,1280]{1,0:T(8,128)}, f32[256,256]{1,0:T(8,128)}) custom-call(s32[1]{0:T(128)} %bitcast.2.me_ref, bf16[1024,1024]{1,0:T(8,128)(2,1)} %get-tuple-element.33.p_high, bf16[1024,1024]{1,0:T(8,128)(2,1)} %get-tuple-element.34.p_low, f32[1024,1024]{1,0:T(8,128)} %get-tuple-element.35.part_ref, f32[4,256,256]{2,1,0:T(8,128)} %copy-done.6, ...), custom_call_target="tpu_custom_call" | custom-call | flops 1 | bytes 1 | tf_op jit(solution)/shard_map/parent_factor/pallas_call | solution.py:448
  111.1 0.2 collective-permute-start.13
  111.2 0.4 collective-permute-start.16
  111.6 1.7 %collective-permute-done.13.rest_3_ = f32[768,256]{1,0:T(8,128)S(1)} collective-permute-done((f32[768,256]{1,0:T(8,128)S(1)}, f32[768,256]{1,0:T(8,128)S(1)}, u32[]{:S(2)}, u32[]{:S(2)}) %collective-permute-start.13) | collective-permute-done | bytes 786464 | tf_op jit(solution)/shard_map/ppermute | solution.py:427
  113.4 1.1 collective-permute-done.16.rest_7_
  114.5 0.9 copy-done.15
  115.4 6.5 %side_windows.1.after1.v0 = f32[256,512]{1,0:T(8,128)} custom-call(s32[1]{0:T(128)} %bitcast.2.me_ref, s32[1,6]{1,0:T(1,128)} %near_ref.5, s32[1,5]{1,0:T(1,128)} %far_ref.5, bf16[6,256,512]{2,1,0:T(8,128)(2,1)} %get-tuple-element.32.after1.high_hbm, bf16[6,256,512]{2,1,0:T(8,128)(2,1)} %get-tuple-element.39.low_hbm, f32[5,256,256]{2,1,0:T(8,128)} %bitcast.8, ...), custom_call_target="tpu_custom_call" | custom-call | flops 1 | bytes 1 | tf_op jit(solution)/shard_map/side_windows/pallas_call | solution.py:448
  121.9 1.3 collective-permute-start.18
  123.2 12.9 %parent_finish.1 = (f32[256,768]{1,0:T(8,128)}, f32[256,256]{1,0:T(8,128)}) custom-call(s32[1]{0:T(128)} %bitcast.2.me_ref, f32[768,1280]{1,0:T(8,128)} %get-tuple-element.37.work_hbm, f32[256,256]{1,0:T(8,128)} %get-tuple-element.38.rest_8_.edge_in, f32[256,512]{1,0:T(8,128)} %side_windows.1.after1.v0), custom_call_target="tpu_custom_call" | custom-call | flops 1 | bytes 1 | tf_op jit(solution)/shard_map/parent_finish/pallas_call | solution.py:448
  136.1 0.6 collective-permute-start.19
  136.7 1.5 %collective-permute-done.19.v3 = f32[256,512]{1,0:T(8,128)S(1)} collective-permute-done((f32[256,512]{1,0:T(8,128)S(1)}, f32[256,512]{1,0:T(8,128)S(1)}, u32[]{:S(2)}, u32[]{:S(2)}) %collective-permute-start.19) | collective-permute-done | bytes 524320 | tf_op jit(solution)/shard_map/ppermute | solution.py:427
  138.2 0.8 copy-done.19
  139.1 3.8 %coupling.1 = f32[256,768]{1,0:T(8,128)} custom-call(bf16[256,1024]{1,0:T(8,128)(2,1)} %get-tuple-element.45.t_high, bf16[256,1024]{1,0:T(8,128)(2,1)} %get-tuple-element.46.t_low, f32[256,512]{1,0:T(8,128)} %side_windows.1.after1.v0, f32[256,512]{1,0:T(8,128)} %copy-done.18, f32[256,512]{1,0:T(8,128)} %copy-done.17, f32[256,512]{1,0:T(8,128)} %copy-done.19, ...), custom_call_target="tpu_custom_call" | custom-call | flops 1 | bytes 1 | tf_op jit(solution)/shard_map/coupling/pallas_call | solution.py:448
  (44 shorter events, 0.1 us)
Async XLA Ops:
  1.7 10.1 %copy-start = (f32[512,256]{1,0:T(8,128)}, f32[512,256]{1,0:T(8,128)S(1)}, u32[]{:S(2)}) copy-start(f32[512,256]{1,0:T(8,128)S(1)} %slice.8.skel_ref) | copy-start | bytes 1572868
  1.7 15.9 %collective-permute-start.1 = (f32[512,256]{1,0:T(8,128)S(1)}, f32[512,256]{1,0:T(8,128)}, u32[]{:S(2)}, u32[]{:S(2)}) collective-permute-start(f32[512,256]{1,0:T(8,128)S(1)} %slice.8.skel_ref), channel_id=1, source_target_pairs={{0,2},{1,3},{2,0},{3,1},{4,6},{5,7},{6,4},{7,5},{8,10},{9,11},{10,... | collective-permute-start | bytes 1572872 | tf_op jit(solution)/shard_map/ppermute | solution.py:427
  4.7 26.1 %collective-permute-start = (f32[512,256]{1,0:T(8,128)S(1)}, f32[512,256]{1,0:T(8,128)}, u32[]{:S(2)}, u32[]{:S(2)}) collective-permute-start(f32[512,256]{1,0:T(8,128)S(1)} %slice.8.skel_ref), channel_id=1, source_target_pairs={{0,1},{1,0},{2,3},{3,2},{4,5},{5,4},{6,7},{7,6},{8,9},{9,8},{10,11... | collective-permute-start | bytes 1572872 | tf_op jit(solution)/shard_map/ppermute | solution.py:427
  4.7 40.5 %collective-permute-start.4 = (f32[256,1024]{1,0:T(8,128)}, f32[256,1024]{1,0:T(8,128)S(1)}, u32[]{:S(2)}, u32[]{:S(2)}) collective-permute-start(f32[256,1024]{1,0:T(8,128)} %p0.1), channel_id=1, source_target_pairs={{0,2},{1,3},{2,0},{3,1},{4,6},{5,7},{6,4},{7,5},{8,10},{9,11},{10,... | collective-permute-start | bytes 3145736 | tf_op jit(solution)/shard_map/ppermute | solution.py:427
  6.8 36.3 %collective-permute-start.5 = (f32[768,256]{1,0:T(8,128)}, f32[768,256]{1,0:T(8,128)S(1)}, u32[]{:S(2)}, u32[]{:S(2)}) collective-permute-start(f32[768,256]{1,0:T(8,128)} %pad_maximum_fusion), channel_id=1, source_target_pairs={{0,4},{1,5},{2,6},{3,7},{4,8},{5,9},{6,10},{7,11},{8,12},{9,13},{1... | collective-permute-start | bytes 2359304 | tf_op jit(solution)/shard_map/ppermute | solution.py:433
  8.7 36.5 %collective-permute-start.6 = (f32[768,256]{1,0:T(8,128)}, f32[768,256]{1,0:T(8,128)S(1)}, u32[]{:S(2)}, u32[]{:S(2)}) collective-permute-start(f32[768,256]{1,0:T(8,128)} %pad_maximum_fusion), channel_id=1, source_target_pairs={{0,28},{1,29},{2,30},{3,31},{4,0},{5,1},{6,2},{7,3},{8,4},{9,5},{1... | collective-permute-start | bytes 2359304 | tf_op jit(solution)/shard_map/ppermute | solution.py:433
  17.6 13.3 %collective-permute-start.2 = (f32[512,256]{1,0:T(8,128)}, f32[512,256]{1,0:T(8,128)S(1)}, u32[]{:S(2)}, u32[]{:S(2)}) collective-permute-start(f32[512,256]{1,0:T(8,128)} %collective-permute-done.1.s2), channel_id=1, source_target_pairs={{0,1},{1,0},{2,3},{3,2},{4,5},{5,4},{6,7},{7,6},{8,9},{9,8},{10,11... | collective-permute-start | bytes 1572872 | tf_op jit(solution)/shard_map/ppermute | solution.py:427
  30.9 0.8 copy-start.16
  31.7 4.8 %copy-start.1 = (f32[256,1024]{1,0:T(8,128)S(1)}, f32[256,1024]{1,0:T(8,128)}, u32[]{:S(2)}) copy-start(f32[256,1024]{1,0:T(8,128)} %p0.1) | copy-start | bytes 3145732
  36.5 18.5 %collective-permute-start.3 = (f32[256,1024]{1,0:T(8,128)S(1)}, f32[256,1024]{1,0:T(8,128)S(1)}, u32[]{:S(2)}, u32[]{:S(2)}) collective-permute-start(f32[256,1024]{1,0:T(8,128)S(1)} %copy-done.1), channel_id=1, source_target_pairs={{0,1},{1,0},{2,3},{3,2},{4,5},{5,4},{6,7},{7,6},{8,9},{9,8},{10,11... | collective-permute-start | bytes 3145736 | tf_op jit(solution)/shard_map/ppermute | solution.py:427
  43.1 30.1 %copy-start.8 = (f32[768,256]{1,0:T(8,128)}, f32[768,256]{1,0:T(8,128)S(1)}, u32[]{:S(2)}) copy-start(f32[768,256]{1,0:T(8,128)S(1)} %collective-permute-done.5.rest_0_) | copy-start | bytes 2359300
  45.2 28.0 %copy-start.9 = (f32[768,256]{1,0:T(8,128)}, f32[768,256]{1,0:T(8,128)S(1)}, u32[]{:S(2)}) copy-start(f32[768,256]{1,0:T(8,128)S(1)} %collective-permute-done.6.rest_4_) | copy-start | bytes 2359300
  45.2 9.8 %copy-start.2 = (f32[256,1024]{1,0:T(8,128)}, f32[256,1024]{1,0:T(8,128)S(1)}, u32[]{:S(2)}) copy-start(f32[256,1024]{1,0:T(8,128)S(1)} %collective-permute-done.4.p2) | copy-start | bytes 3145732
  45.2 9.8 %collective-permute-start.7 = (f32[256,1024]{1,0:T(8,128)S(1)}, f32[256,1024]{1,0:T(8,128)S(1)}, u32[]{:S(2)}, u32[]{:S(2)}) collective-permute-start(f32[256,1024]{1,0:T(8,128)S(1)} %collective-permute-done.4.p2), channel_id=1, source_target_pairs={{0,1},{1,0},{2,3},{3,2},{4,5},{5,4},{6,7},{7,6},{8,9},{9,8},{10,11... | collective-permute-start | bytes 3145736 | tf_op jit(solution)/shard_map/ppermute | solution.py:427
  45.3 9.7 %collective-permute-start.8 = (f32[4,256,256]{2,1,0:T(8,128)}, f32[4,256,256]{2,1,0:T(8,128)S(1)}, u32[]{:S(2)}, u32[]{:S(2)}) collective-permute-start(f32[4,256,256]{2,1,0:T(8,128)} %own_window.1.after1.h0), channel_id=1, source_target_pairs={{0,1},{1,0},{2,3},{3,2},{4,5},{5,4},{6,7},{7,6},{8,9},{9,8},{10,11... | collective-permute-start | bytes 3145736 | tf_op jit(solution)/shard_map/ppermute | solution.py:427
  45.8 25.4 %collective-permute-start.9 = (f32[4,256,256]{2,1,0:T(8,128)}, f32[4,256,256]{2,1,0:T(8,128)S(1)}, u32[]{:S(2)}, u32[]{:S(2)}) collective-permute-start(f32[4,256,256]{2,1,0:T(8,128)} %own_window.1.after1.h0), channel_id=1, source_target_pairs={{0,2},{1,3},{2,0},{3,1},{4,6},{5,7},{6,4},{7,5},{8,10},{9,11},{10,... | collective-permute-start | bytes 3145736 | tf_op jit(solution)/shard_map/ppermute | solution.py:427
  55.0 1.0 copy-start.3
  55.0 1.3 copy-start.4
  55.0 1.6 %copy-start.5 = (f32[4,256,256]{2,1,0:T(8,128)}, f32[4,256,256]{2,1,0:T(8,128)S(1)}, u32[]{:S(2)}) copy-start(f32[4,256,256]{2,1,0:T(8,128)S(1)} %collective-permute-done.8.h1) | copy-start | bytes 3145732
  71.1 2.7 %copy-start.6 = (f32[4,256,256]{2,1,0:T(8,128)}, f32[4,256,256]{2,1,0:T(8,128)S(1)}, u32[]{:S(2)}) copy-start(f32[4,256,256]{2,1,0:T(8,128)S(1)} %collective-permute-done.9.h2) | copy-start | bytes 3145732
  71.1 2.7 %collective-permute-start.10 = (f32[4,256,256]{2,1,0:T(8,128)S(1)}, f32[4,256,256]{2,1,0:T(8,128)S(1)}, u32[]{:S(2)}, u32[]{:S(2)}) collective-permute-start(f32[4,256,256]{2,1,0:T(8,128)S(1)} %collective-permute-done.9.h2), channel_id=1, source_target_pairs={{0,1},{1,0},{2,3},{3,2},{4,5},{5,4},{6,7},{7,6},{8,9},{9,8},{10,11... | collective-permute-start | bytes 3145736 | tf_op jit(solution)/shard_map/ppermute | solution.py:427
  71.1 39.9 %collective-permute-start.12 = (f32[768,256]{1,0:T(8,128)S(1)}, f32[768,256]{1,0:T(8,128)S(1)}, u32[]{:S(2)}, u32[]{:S(2)}) collective-permute-start(f32[768,256]{1,0:T(8,128)S(1)} %collective-permute-done.5.rest_0_), channel_id=1, source_target_pairs={{0,2},{1,3},{2,0},{3,1},{4,6},{5,7},{6,4},{7,5},{8,10},{9,11},{10,... | collective-permute-start | bytes 2359304 | tf_op jit(solution)/shard_map/ppermute | solution.py:427
  72.6 38.6 %collective-permute-start.15 = (f32[768,256]{1,0:T(8,128)S(1)}, f32[768,256]{1,0:T(8,128)S(1)}, u32[]{:S(2)}, u32[]{:S(2)}) collective-permute-start(f32[768,256]{1,0:T(8,128)S(1)} %collective-permute-done.6.rest_4_), channel_id=1, source_target_pairs={{0,2},{1,3},{2,0},{3,1},{4,6},{5,7},{6,4},{7,5},{8,10},{9,11},{10,... | collective-permute-start | bytes 2359304 | tf_op jit(solution)/shard_map/ppermute | solution.py:427
  73.2 38.5 %collective-permute-start.11 = (f32[768,256]{1,0:T(8,128)S(1)}, f32[768,256]{1,0:T(8,128)S(1)}, u32[]{:S(2)}, u32[]{:S(2)}) collective-permute-start(f32[768,256]{1,0:T(8,128)S(1)} %collective-permute-done.5.rest_0_), channel_id=1, source_target_pairs={{0,1},{1,0},{2,3},{3,2},{4,5},{5,4},{6,7},{7,6},{8,9},{9,8},{10,11... | collective-permute-start | bytes 2359304 | tf_op jit(solution)/shard_map/ppermute | solution.py:427
  73.2 38.4 %collective-permute-start.14 = (f32[768,256]{1,0:T(8,128)S(1)}, f32[768,256]{1,0:T(8,128)S(1)}, u32[]{:S(2)}, u32[]{:S(2)}) collective-permute-start(f32[768,256]{1,0:T(8,128)S(1)} %collective-permute-done.6.rest_4_), channel_id=1, source_target_pairs={{0,1},{1,0},{2,3},{3,2},{4,5},{5,4},{6,7},{7,6},{8,9},{9,8},{10,11... | collective-permute-start | bytes 2359304 | tf_op jit(solution)/shard_map/ppermute | solution.py:427
  73.8 1.0 copy-start.7
  111.1 3.5 %copy-start.10 = (f32[768,256]{1,0:T(8,128)}, f32[768,256]{1,0:T(8,128)S(1)}, u32[]{:S(2)}) copy-start(f32[768,256]{1,0:T(8,128)S(1)} %collective-permute-done.12.rest_2_) | copy-start | bytes 2359300
  111.1 2.3 %collective-permute-start.13 = (f32[768,256]{1,0:T(8,128)S(1)}, f32[768,256]{1,0:T(8,128)S(1)}, u32[]{:S(2)}, u32[]{:S(2)}) collective-permute-start(f32[768,256]{1,0:T(8,128)S(1)} %collective-permute-done.12.rest_2_), channel_id=1, source_target_pairs={{0,1},{1,0},{2,3},{3,2},{4,5},{5,4},{6,7},{7,6},{8,9},{9,8},{10,11... | collective-permute-start | bytes 2359304 | tf_op jit(solution)/shard_map/ppermute | solution.py:427
  111.2 3.3 %copy-start.11 = (f32[768,256]{1,0:T(8,128)}, f32[768,256]{1,0:T(8,128)S(1)}, u32[]{:S(2)}) copy-start(f32[768,256]{1,0:T(8,128)S(1)} %collective-permute-done.15.rest_6_) | copy-start | bytes 2359300
  111.2 3.3 %collective-permute-start.16 = (f32[768,256]{1,0:T(8,128)S(1)}, f32[768,256]{1,0:T(8,128)S(1)}, u32[]{:S(2)}, u32[]{:S(2)}) collective-permute-start(f32[768,256]{1,0:T(8,128)S(1)} %collective-permute-done.15.rest_6_), channel_id=1, source_target_pairs={{0,1},{1,0},{2,3},{3,2},{4,5},{5,4},{6,7},{7,6},{8,9},{9,8},{10,11... | collective-permute-start | bytes 2359304 | tf_op jit(solution)/shard_map/ppermute | solution.py:427
  111.6 2.9 %copy-start.12 = (f32[768,256]{1,0:T(8,128)}, f32[768,256]{1,0:T(8,128)S(1)}, u32[]{:S(2)}) copy-start(f32[768,256]{1,0:T(8,128)S(1)} %collective-permute-done.11.rest_1_) | copy-start | bytes 2359300
  111.6 2.9 %copy-start.13 = (f32[768,256]{1,0:T(8,128)}, f32[768,256]{1,0:T(8,128)S(1)}, u32[]{:S(2)}) copy-start(f32[768,256]{1,0:T(8,128)S(1)} %collective-permute-done.14.rest_5_) | copy-start | bytes 2359300
  113.4 1.1 copy-start.14
  114.5 0.9 copy-start.15
  121.9 14.2 %collective-permute-start.18 = (f32[256,512]{1,0:T(8,128)}, f32[256,512]{1,0:T(8,128)S(1)}, u32[]{:S(2)}, u32[]{:S(2)}) collective-permute-start(f32[256,512]{1,0:T(8,128)} %side_windows.1.after1.v0), channel_id=1, source_target_pairs={{0,2},{1,3},{2,0},{3,1},{4,6},{5,7},{6,4},{7,5},{8,10},{9,11},{10,... | collective-permute-start | bytes 1572872 | tf_op jit(solution)/shard_map/ppermute | solution.py:427
  123.2 13.5 %collective-permute-start.17 = (f32[256,512]{1,0:T(8,128)}, f32[256,512]{1,0:T(8,128)S(1)}, u32[]{:S(2)}, u32[]{:S(2)}) collective-permute-start(f32[256,512]{1,0:T(8,128)} %side_windows.1.after1.v0), channel_id=1, source_target_pairs={{0,1},{1,0},{2,3},{3,2},{4,5},{5,4},{6,7},{7,6},{8,9},{9,8},{10,11... | collective-permute-start | bytes 1572872 | tf_op jit(solution)/shard_map/ppermute | solution.py:427
  136.1 2.1 %copy-start.17 = (f32[256,512]{1,0:T(8,128)}, f32[256,512]{1,0:T(8,128)S(1)}, u32[]{:S(2)}) copy-start(f32[256,512]{1,0:T(8,128)S(1)} %collective-permute-done.18.v2) | copy-start | bytes 1572868
  136.1 2.1 %collective-permute-start.19 = (f32[256,512]{1,0:T(8,128)S(1)}, f32[256,512]{1,0:T(8,128)S(1)}, u32[]{:S(2)}, u32[]{:S(2)}) collective-permute-start(f32[256,512]{1,0:T(8,128)S(1)} %collective-permute-done.18.v2), channel_id=1, source_target_pairs={{0,1},{1,0},{2,3},{3,2},{4,5},{5,4},{6,7},{7,6},{8,9},{9,8},{10,11... | collective-permute-start | bytes 1572872 | tf_op jit(solution)/shard_map/ppermute | solution.py:427
  136.7 1.5 %copy-start.18 = (f32[256,512]{1,0:T(8,128)}, f32[256,512]{1,0:T(8,128)S(1)}, u32[]{:S(2)}) copy-start(f32[256,512]{1,0:T(8,128)S(1)} %collective-permute-done.17.v1) | copy-start | bytes 1572868
  138.2 0.8 copy-start.19

commit v3 on v2

--- a/solution.py
+++ b/solution.py
@@ -19,6 +19,7 @@
 ROWS = 8
 WIDE = PRED + 2 * RANK
 EARLY = 4
+AHEAD = 2
 MIDDLE = 30_000_000_000
 
 VMEM_BYTES = 56 * 1024 * 1024
@@ -87,6 +88,12 @@
     return total
 
 
+def added(terms):
+    while len(terms) > 1:
+        terms = [terms[i] + terms[i + 1] for i in range(0, len(terms), 2)]
+    return terms[0]
+
+
 def tile_factor(square):
     count = TILE // ROWS
     row = lax.broadcasted_iota(jnp.int32, (ROWS, TILE), 0)
@@ -97,13 +104,23 @@
     inverse = []
     pad1 = jnp.zeros((ROWS, TILE), jnp.float32)
     pad2 = jnp.zeros((ROWS, 2 * TILE), jnp.float32)
+    cols = [lane_spread(left[0], j) for j in range(ROWS)]
     for k in range(count):
-        cols = [lane_spread(left[k], ROWS * k + j) for j in range(ROWS)]
         inv = small_inverse(
             {(i, j): row_spread(cols[j], i) for j in range(ROWS) for i in range(j, ROWS)}
         )
-        left_rows = [row_spread(left[k], t) for t in range(ROWS)]
-        right_rows = [row_spread(right[k], t) for t in range(ROWS)]
+        soon = range(k + 1, min(k + 1 + AHEAD, count))
+        sides = {}
+        for i in soon:
+            raw = [lane_spread(left[i], ROWS * k + t) for t in range(ROWS)]
+            sides[i] = [weighted(inv, j, raw) for j in range(ROWS)]
+        if k + 1 < count:
+            side = sides[k + 1]
+            cols = [
+                lane_spread(left[k + 1], ROWS * (k + 1) + j)
+                - added([side[t] * row_spread(side[t], j) for t in range(ROWS)])
+                for j in range(ROWS)
+            ]
         u_rows = m_rows = None
         for j in range(ROWS):
             weight = inv[ROWS - 1, j]
@@ -111,25 +128,17 @@
                 weight = jnp.where(row == i, inv[i, j], weight)
             if j > 0:
                 weight = jnp.where(row >= j, weight, 0.0)
-            u_term, m_term = weight * left_rows[j], weight * right_rows[j]
+            u_term = weight * row_spread(left[k], j)
+            m_term = weight * row_spread(right[k], j)
             u_rows = u_term if u_rows is None else u_rows + u_term
             m_rows = m_term if m_rows is None else m_rows + m_term
         u_rows = jnp.where(col >= row + ROWS * k, u_rows, 0.0)
         upper.append(u_rows)
         inverse.append(m_rows)
-        if k == count - 1:
-            break
-        raw = [lane_spread(left[k + 1], ROWS * k + t) for t in range(ROWS)]
-        u_total = m_total = None
-        for j in range(ROWS):
-            side = weighted(inv, j, raw)
-            u_term = side * weighted(inv, j, left_rows)
-            m_term = side * row_spread(m_rows, j)
-            u_total = u_term if u_total is None else u_total + u_term
-            m_total = m_term if m_total is None else m_total + m_term
-        left[k + 1] = left[k + 1] - u_total
-        right[k + 1] = right[k + 1] - m_total
-        if k == count - 2:
+        for i in soon:
+            left[i] = left[i] - added([sides[i][j] * row_spread(u_rows, j) for j in range(ROWS)])
+            right[i] = right[i] - added([sides[i][j] * row_spread(m_rows, j) for j in range(ROWS)])
+        if k + 1 + AHEAD >= count:
             continue
         both = jnp.concatenate([u_rows, m_rows], axis=1)
         high = both.astype(jnp.bfloat16).astype(jnp.float32)
@@ -142,7 +151,7 @@
             TN,
             preferred_element_type=jnp.float32,
         )
-        for i in range(k + 2, count):
+        for i in range(k + 1 + AHEAD, count):
             rows = slice(ROWS * i, ROWS * (i + 1))
             left[i] = left[i] - update[rows, :TILE]
             right[i] = right[i] - update[rows, TILE:]
@@ -231,23 +240,28 @@
             low_ref[s] = low
 
 
+def block_rows(s):
+    return slice(s * RANK, (s + 1) * RANK)
+
+
 def own_kernel(
     me_ref, near_ref, far_ref, high_ref, low_ref, far_hbm, schur_ref, s1, s2, s3, out_ref, sems
 ):
     slots = sibling_slots(me_ref, near_ref, far_ref)
     copies = [
-        pltpu.make_async_copy(far_hbm.at[f], out_ref.at[s + 1], sems.at[s])
+        pltpu.make_async_copy(far_hbm.at[f], out_ref.at[block_rows(s + 1), :], sems.at[s])
         for s, (_, _, f) in enumerate(slots)
     ]
     for copy in copies:
         copy.start()
-    out_ref[0] = schur_ref[...]
+    out_ref[block_rows(0), :] = schur_ref[...]
+    out_ref[GROUP * RANK :, :] = jnp.zeros((ROWS, RANK), jnp.float32)
     for s, sibling in enumerate((s1, s2, s3)):
         copies[s].wait()
 
         @pl.when(slots[s][0] < NEAR)
         def _(s=s, sibling=sibling):
-            out_ref[s + 1] = dot3((high_ref[s], low_ref[s]), split(sibling[...]))
+            out_ref[block_rows(s + 1), :] = dot3((high_ref[s], low_ref[s]), split(sibling[...]))
 
 
 def side_kernel(blocks, me_ref, near_ref, far_ref, high_hbm, low_hbm, far_hbm, *rest):
@@ -316,7 +330,7 @@
 
 def partial_sums(p_high, p_low, h_refs, first, v_high, v_low):
     for s in range(2):
-        line = [h_refs[s][(first + s) ^ t] for t in range(GROUP)]
+        line = [h_refs[s][block_rows((first + s) ^ t), :] for t in range(GROUP)]
         line = split(jnp.concatenate(line, axis=1))
         high, low = split(dot3(line, (p_high[...], p_low[...])))
         rows = slice(s * RANK, (s + 1) * RANK)
@@ -325,7 +339,7 @@
 
 
 def chip_kernel(
-    me_ref, p0, p1, p2, p3, h0, h1, after1, p_high, p_low, t_high, t_low, part_ref, v_high, v_low
+    me_ref, h0, h1, p0, p1, p2, p3, after1, p_high, p_low, t_high, t_low, part_ref, v_high, v_low
 ):
     member = lax.rem(me_ref[0], GROUP)
     slab = pl.ds(pl.multiple_of(member * RANK, RANK), RANK)
@@ -371,7 +385,7 @@
 
 
 def parent_kernel(
-    me_ref, p_high, p_low, part_ref, h2, h3, work, edge_ref, v_high, v_low, whole, u_tile, m_tile
+    me_ref, h2, h3, p_high, p_low, part_ref, work, edge_ref, v_high, v_low, whole, u_tile, m_tile
 ):
     member = lax.rem(me_ref[0], GROUP)
     partial_sums(p_high, p_low, (h2, h3), 2, v_high, v_low)
@@ -502,12 +516,14 @@
         sib_high,
         flops=MIDDLE,
     )
-    skels = gathered(skeleton, "blk")
+    skel_chip = swapped(skeleton, "blk", 2)
+    skel_core = swapped(skeleton, "blk", 1)
+    skels = [skeleton, skel_core, skel_chip, swapped(skel_chip, "blk", 1)]
     (own,) = call(
         own_kernel,
         "own_window",
         [in_smem()] * 3 + [in_vmem()] * 2 + [anywhere()] + [in_vmem()] * 4,
-        [((GROUP, RANK, RANK), f32)],
+        [((GROUP * RANK + ROWS, RANK), f32)],
         [pltpu.SemaphoreType.DMA((GROUP - 1,))],
         me,
         near_index,
@@ -520,9 +536,6 @@
     )
     own_core = swapped(own, "blk", 1)
     own_chip = swapped(own, "blk", 2)
-    base_core = swapped(after(parent_basis, own), "blk", 1)
-    base_both = swapped(after(base_chip, own, prev_load, next_load), "blk", 1)
-    bases = [parent_basis, base_core, base_chip, base_both]
 
     left_high, left_low = pl.pallas_call(
         left_kernel,
@@ -540,6 +553,9 @@
 
         name="left_products",
     )(basis, near, own)
+    base_core = swapped(after(parent_basis, left_high), "blk", 1)
+    base_both = swapped(after(base_chip, left_high, prev_load, next_load), "blk", 1)
+    bases = [parent_basis, base_core, base_chip, base_both]
     p_high, p_low, t_high, t_low, part = call(
         chip_kernel,
         "chip_sums",
@@ -547,9 +563,9 @@
         [((PAR, PAR), b16)] * 2 + [((RANK, PAR), b16)] * 2 + [((PAR, PAR), f32)],
         [pltpu.VMEM((2 * RANK, PAR), b16)] * 2,
         me,
-        *bases,
         own,
         own_core,
+        *bases,
         left_high,
     )
     own_both = swapped(after(own_chip, part), "blk", 1)
@@ -563,11 +579,11 @@
         [((PRED, WIDE), f32), ((RANK, RANK), f32)],
         [pltpu.VMEM((2 * RANK, PAR), b16)] * 2 + [pltpu.VMEM((PAR, PAR), f32)] + tiles,
         me,
+        own_chip,
+        own_both,
         p_high,
         p_low,
         part,
-        own_chip,
-        own_both,
     )
     from_prev = gathered(prev_load, "blk", edge_rows)
     from_next = gathered(next_load, "blk", edge_rows)

time: 143 us -> 130 us (0.909)
  Pallas kernels: 102 us -> 91.6 us
  waiting for transfers between devices: 16.4 us -> 13.7 us
    pallas_call x8, Pallas kernels: 93.9 us -> 83.9 us  [call(): pl.pallas_call(kernel, in_specs=ins, out_specs=[in_vmem()] * len(outs), o...]
    ppermute x2, waiting for transfers between devices: 8.08 us -> 0.01 us  [shifted(): return lax.ppermute(value, axis, pairs)]
    ppermute x18, waiting for transfers between devices: 8.36 us -> 13.7 us  [swapped(): return lax.ppermute(value, axis, pairs)]
    unnamed x40 -> x38, local copies, waits for them, and re-layouts: 5.14 us -> 5.43 us
  transfers between devices with their start and end apart: 20 -> 20, of which waited for: 8 -> 8; matrix products, arithmetic and copies ran while one was open for 1% -> 1% of each run, Pallas kernels for 64% -> 63%
where the time goes in v3:
time: 130 us
  Pallas kernels  91.6 us (70%)
  starting transfers between devices  16 us (12%)
  waiting for transfers between devices  13.7 us (11%)
  local copies, waits for them, and re-layouts  6.62 us (5%)
    pallas_call x8, Pallas kernels, call(): pl.pallas_call(kernel, in_specs=ins, out_specs=[in_vmem()] * len(outs), o...  83.9 us
    ppermute x18, waiting for transfers between devices, swapped(): return lax.ppermute(value, axis, pairs)  13.7 us
    ppermute x18, starting transfers between devices, swapped(): return lax.ppermute(value, axis, pairs)  11.3 us
    pallas_call x1, Pallas kernels, on_device(): pl.pallas_call(left_kernel, grid=(NEAR,), in_specs=[pl.BlockSpec((LEAF, R...  7.72 us
    unnamed x38, local copies, waits for them, and re-layouts  5.43 us
    ppermute x2, starting transfers between devices, shifted(): return lax.ppermute(value, axis, pairs)  4.72 us
  transfers between devices with their start and end apart: 20, of which 8 were waited for; matrix products, arithmetic and copies ran while one was open for 1% of the time, Pallas kernels for 63%

profile of v3, /device:TPU:0, one launch (start us, length us, event | category | flops | bytes accessed | tf_op | source)
XLA Modules:
  0.0 129.7 jit_solution(16868564089403292570)
XLA Ops:
  0.6 0.0 slice-start
  0.7 1.2 slice.8.skel_ref
  1.8 0.0 copy-start
  1.8 3.0 %collective-permute-start.1 = (f32[512,256]{1,0:T(8,128)S(1)}, f32[512,256]{1,0:T(8,128)S(1)}, u32[]{:S(2)}, u32[]{:S(2)}) collective-permute-start(f32[512,256]{1,0:T(8,128)S(1)} %slice.8.skel_ref), channel_id=1, source_target_pairs={{0,2},{1,3},{2,0},{3,1},{4,6},{5,7},{6,4},{7,5},{8,10},{9,11},{10,... | collective-permute-start | bytes 1572872 | tf_op jit(solution)/shard_map/ppermute | solution.py:441
  4.9 0.9 pad_maximum_fusion
  5.8 1.5 %collective-permute-start.7 = (f32[768,256]{1,0:T(8,128)}, f32[768,256]{1,0:T(8,128)}, u32[]{:S(2)}, u32[]{:S(2)}) collective-permute-start(f32[768,256]{1,0:T(8,128)} %pad_maximum_fusion), channel_id=1, source_target_pairs={{0,4},{1,5},{2,6},{3,7},{4,8},{5,9},{6,10},{7,11},{8,12},{9,13},{1... | collective-permute-start | bytes 2359304 | tf_op jit(solution)/shard_map/ppermute | solution.py:447
  7.3 3.2 %collective-permute-start.8 = (f32[768,256]{1,0:T(8,128)}, f32[768,256]{1,0:T(8,128)}, u32[]{:S(2)}, u32[]{:S(2)}) collective-permute-start(f32[768,256]{1,0:T(8,128)} %pad_maximum_fusion), channel_id=1, source_target_pairs={{0,28},{1,29},{2,30},{3,31},{4,0},{5,1},{6,2},{7,3},{8,4},{9,5},{1... | collective-permute-start | bytes 2359304 | tf_op jit(solution)/shard_map/ppermute | solution.py:447
  10.5 0.4 collective-permute-start.6
  10.9 4.6 %sibling_products.1 = (bf16[3,256,512]{2,1,0:T(8,128)(2,1)}, bf16[3,256,512]{2,1,0:T(8,128)(2,1)}) custom-call(s32[1]{0:T(128)} %bitcast.2.me_ref, s32[1,6]{1,0:T(1,128)} %near_ref.5, s32[1,5]{1,0:T(1,128)} %far_ref.5, f32[512,256]{1,0:T(8,128)} %copy-done, f32[6,512,512]{2,1,0:T(8,128)} %bitcast.5), custom_call_target="tpu_custom_call" | custom-call | flops 1 | bytes 1 | tf_op jit(solution)/shard_map/sibling_products/pallas_call | solution.py:462
  15.6 2.1 %collective-permute-done.1.s2 = f32[512,256]{1,0:T(8,128)S(1)} collective-permute-done((f32[512,256]{1,0:T(8,128)S(1)}, f32[512,256]{1,0:T(8,128)S(1)}, u32[]{:S(2)}, u32[]{:S(2)}) %collective-permute-start.1) | collective-permute-done | bytes 524320 | tf_op jit(solution)/shard_map/ppermute | solution.py:441
  17.6 0.0 collective-permute-start.2
  17.6 11.1 %leaf_factor.1 = (f32[256,512]{1,0:T(8,128)}, f32[256,256]{1,0:T(8,128)}) custom-call(f32[512,512]{1,0:T(8,128)} %bitcast.12, f32[512,512]{1,0:T(8,128)} %bitcast.10, bf16[3,256,512]{2,1,0:T(8,128)(2,1)} %get-tuple-element.26.after1.high_ref), custom_call_target="tpu_custom_call" | custom-call | flops 30000001024 | bytes 1 | tf_op jit(solution)/shard_map/leaf_factor/pallas_call | solution.py:462
  28.7 0.0 collective-permute-done.2.s3
  28.7 0.8 copy-done.15
  29.5 4.7 %own_window.1.after1.h0 = f32[1032,256]{1,0:T(8,128)} custom-call(s32[1]{0:T(128)} %bitcast.2.me_ref, s32[1,6]{1,0:T(1,128)} %near_ref.5, s32[1,5]{1,0:T(1,128)} %far_ref.5, bf16[3,256,512]{2,1,0:T(8,128)(2,1)} %get-tuple-element.26.after1.high_ref, bf16[3,256,512]{2,1,0:T(8,128)(2,1)} %get-tuple-element.28.low_ref, f32[5,256,256]{2,1,0:T(8,128)} %bitcast.7, ...), custom_call_target="tpu_custom_call" | custom-call | flops 1 | bytes 1 | tf_op jit(solution)/shard_map/own_window/pallas_call | solution.py:462
  34.2 0.5 collective-permute-start.4
  34.7 1.7 %collective-permute-start.3 = (f32[1032,256]{1,0:T(8,128)}, f32[1032,256]{1,0:T(8,128)S(1)}, u32[]{:S(2)}, u32[]{:S(2)}) collective-permute-start(f32[1032,256]{1,0:T(8,128)} %own_window.1.after1.h0), channel_id=1, source_target_pairs={{0,2},{1,3},{2,0},{3,1},{4,6},{5,7},{6,4},{7,5},{8,10},{9,11},{10,... | collective-permute-start | bytes 3170312 | tf_op jit(solution)/shard_map/ppermute | solution.py:441
  36.4 7.7 %left_products.1 = (bf16[6,256,512]{2,1,0:T(8,128)(2,1)}, bf16[6,256,512]{2,1,0:T(8,128)(2,1)}) custom-call(f32[512,512]{1,0:T(8,128)} %bitcast.11, f32[6,512,512]{2,1,0:T(8,128)} %bitcast.6, f32[1032,256]{1,0:T(8,128)} %own_window.1.after1.h0), custom_call_target="tpu_custom_call" | custom-call | flops 1 | bytes 1 | tf_op jit(solution)/shard_map/left_products/pallas_call | solution.py:540
  44.2 0.0 collective-permute-done.7.rest_0_
  44.2 0.0 collective-permute-done.8.rest_4_
  44.2 0.0 collective-permute-done.6.p2
  44.2 0.2 collective-permute-start.9
  44.4 0.4 collective-permute-start.5
  44.8 2.1 %collective-permute-done.9.p3 = f32[256,1024]{1,0:T(8,128)S(1)} collective-permute-done((f32[256,1024]{1,0:T(8,128)S(1)}, f32[256,1024]{1,0:T(8,128)S(1)}, u32[]{:S(2)}, u32[]{:S(2)}) %collective-permute-start.9) | collective-permute-done | bytes 1048608 | tf_op jit(solution)/shard_map/ppermute | solution.py:441
  46.9 1.5 %collective-permute-done.5.p1 = f32[256,1024]{1,0:T(8,128)S(1)} collective-permute-done((f32[256,1024]{1,0:T(8,128)S(1)}, f32[256,1024]{1,0:T(8,128)S(1)}, u32[]{:S(2)}, u32[]{:S(2)}) %collective-permute-start.5) | collective-permute-done | bytes 1048608 | tf_op jit(solution)/shard_map/ppermute | solution.py:441
  48.4 1.0 copy-done.7
  49.4 1.0 copy-done.3
  50.4 11.8 %chip_sums.1 = (bf16[1024,1024]{1,0:T(8,128)(2,1)}, bf16[1024,1024]{1,0:T(8,128)(2,1)}, bf16[256,1024]{1,0:T(8,128)(2,1)}, bf16[256,1024]{1,0:T(8,128)(2,1)}, f32[1024,1024]{1,0:T(8,128)}) custom-call(s32[1]{0:T(128)} %bitcast.2.me_ref, f32[1032,256]{1,0:T(8,128)} %own_window.1.after1.h0, f32[1032,256]{1,0:T(8,128)} %copy-done.3, f32[256,1024]{1,0:T(8,128)} %p0.1, ...), custom_call_target="tpu_custom_call" | custom-call | flops 1 | bytes 1 | tf_op jit(solution)/shard_map/chip_sums/pallas_call | solution.py:462
  62.2 0.2 collective-permute-start.10
  62.4 1.3 collective-permute-start.15
  63.6 0.8 collective-permute-start.12
  64.4 0.5 collective-permute-start.14
  64.9 1.0 copy-done.4
  65.9 31.5 %parent_factor.1 = (f32[768,1280]{1,0:T(8,128)}, f32[256,256]{1,0:T(8,128)}) custom-call(s32[1]{0:T(128)} %bitcast.2.me_ref, f32[1032,256]{1,0:T(8,128)} %copy-done.2, f32[1032,256]{1,0:T(8,128)} %copy-done.4, bf16[1024,1024]{1,0:T(8,128)(2,1)} %get-tuple-element.35.p_high, bf16[1024,1024]{1,0:T(8,128)(2,1)} %get-tuple-element.36.p_low, ...), custom_call_target="tpu_custom_call" | custom-call | flops 1 | bytes 1 | tf_op jit(solution)/shard_map/parent_factor/pallas_call | solution.py:462
  97.4 0.2 collective-permute-start.16
  97.5 1.7 %collective-permute-done.12.rest_2_ = f32[768,256]{1,0:T(8,128)S(1)} collective-permute-done((f32[768,256]{1,0:T(8,128)}, f32[768,256]{1,0:T(8,128)S(1)}, u32[]{:S(2)}, u32[]{:S(2)}) %collective-permute-start.12) | collective-permute-done | bytes 786464 | tf_op jit(solution)/shard_map/ppermute | solution.py:441
  99.2 0.0 copy-start.10
  99.3 0.4 collective-permute-done.16.rest_7_
  99.7 1.8 %collective-permute-done.13.rest_3_ = f32[768,256]{1,0:T(8,128)S(1)} collective-permute-done((f32[768,256]{1,0:T(8,128)S(1)}, f32[768,256]{1,0:T(8,128)S(1)}, u32[]{:S(2)}, u32[]{:S(2)}) %collective-permute-start.13) | collective-permute-done | bytes 786464 | tf_op jit(solution)/shard_map/ppermute | solution.py:441
  101.6 0.9 copy-done.13
  102.4 6.1 %side_windows.1.after1.v0 = f32[256,512]{1,0:T(8,128)} custom-call(s32[1]{0:T(128)} %bitcast.2.me_ref, s32[1,6]{1,0:T(1,128)} %near_ref.5, s32[1,5]{1,0:T(1,128)} %far_ref.5, bf16[6,256,512]{2,1,0:T(8,128)(2,1)} %get-tuple-element.30.after1.high_hbm, bf16[6,256,512]{2,1,0:T(8,128)(2,1)} %get-tuple-element.39.low_hbm, f32[5,256,256]{2,1,0:T(8,128)} %bitcast.8, ...), custom_call_target="tpu_custom_call" | custom-call | flops 1 | bytes 1 | tf_op jit(solution)/shard_map/side_windows/pallas_call | solution.py:462
  108.5 1.9 %collective-permute-start.18 = (f32[256,512]{1,0:T(8,128)}, f32[256,512]{1,0:T(8,128)S(1)}, u32[]{:S(2)}, u32[]{:S(2)}) collective-permute-start(f32[256,512]{1,0:T(8,128)} %side_windows.1.after1.v0), channel_id=1, source_target_pairs={{0,2},{1,3},{2,0},{3,1},{4,6},{5,7},{6,4},{7,5},{8,10},{9,11},{10,... | collective-permute-start | bytes 1572872 | tf_op jit(solution)/shard_map/ppermute | solution.py:441
  110.3 0.3 collective-permute-start.17
  110.6 10.4 %parent_finish.1 = (f32[256,768]{1,0:T(8,128)}, f32[256,256]{1,0:T(8,128)}) custom-call(s32[1]{0:T(128)} %bitcast.2.me_ref, f32[768,1280]{1,0:T(8,128)} %get-tuple-element.37.work_hbm, f32[256,256]{1,0:T(8,128)} %get-tuple-element.38.rest_8_.edge_in, f32[256,512]{1,0:T(8,128)} %side_windows.1.after1.v0), custom_call_target="tpu_custom_call" | custom-call | flops 1 | bytes 1 | tf_op jit(solution)/shard_map/parent_finish/pallas_call | solution.py:462
  121.1 2.1 %collective-permute-done.18.v2 = f32[256,512]{1,0:T(8,128)S(1)} collective-permute-done((f32[256,512]{1,0:T(8,128)}, f32[256,512]{1,0:T(8,128)S(1)}, u32[]{:S(2)}, u32[]{:S(2)}) %collective-permute-start.18) | collective-permute-done | bytes 524320 | tf_op jit(solution)/shard_map/ppermute | solution.py:441
  123.2 1.9 %collective-permute-done.19.v3 = f32[256,512]{1,0:T(8,128)S(1)} collective-permute-done((f32[256,512]{1,0:T(8,128)S(1)}, f32[256,512]{1,0:T(8,128)S(1)}, u32[]{:S(2)}, u32[]{:S(2)}) %collective-permute-start.19) | collective-permute-done | bytes 524320 | tf_op jit(solution)/shard_map/ppermute | solution.py:441
  125.1 0.8 copy-done.18
  126.0 3.8 %coupling.1 = f32[256,768]{1,0:T(8,128)} custom-call(bf16[256,1024]{1,0:T(8,128)(2,1)} %get-tuple-element.45.t_high, bf16[256,1024]{1,0:T(8,128)(2,1)} %get-tuple-element.46.t_low, f32[256,512]{1,0:T(8,128)} %side_windows.1.after1.v0, f32[256,512]{1,0:T(8,128)} %copy-done.17, f32[256,512]{1,0:T(8,128)} %copy-done.16, f32[256,512]{1,0:T(8,128)} %copy-done.18, ...), custom_call_target="tpu_custom_call" | custom-call | flops 1 | bytes 1 | tf_op jit(solution)/shard_map/coupling/pallas_call | solution.py:462
  (43 shorter events, 0.1 us)
Async XLA Ops:
  0.6 4.2 %slice-start = ((f32[256,1024]{1,0:T(8,128)}), f32[256,256]{1,0:T(8,128)S(1)}, s32[]{:S(2)}) async-start(f32[256,1024]{1,0:T(8,128)} %p0.1), calls=%async_computation | async-start | bytes 524288 | tf_op jit(solution)/shard_map/slice | solution.py:490
  0.6 9.9 %copy-start.1 = (f32[256,1024]{1,0:T(8,128)S(1)}, f32[256,1024]{1,0:T(8,128)}, u32[]{:S(2)}) copy-start(f32[256,1024]{1,0:T(8,128)} %p0.1) | copy-start | bytes 3145732
  1.8 9.1 %copy-start = (f32[512,256]{1,0:T(8,128)}, f32[512,256]{1,0:T(8,128)S(1)}, u32[]{:S(2)}) copy-start(f32[512,256]{1,0:T(8,128)S(1)} %slice.8.skel_ref) | copy-start | bytes 1572868
  1.8 15.8 %collective-permute-start.1 = (f32[512,256]{1,0:T(8,128)S(1)}, f32[512,256]{1,0:T(8,128)S(1)}, u32[]{:S(2)}, u32[]{:S(2)}) collective-permute-start(f32[512,256]{1,0:T(8,128)S(1)} %slice.8.skel_ref), channel_id=1, source_target_pairs={{0,2},{1,3},{2,0},{3,1},{4,6},{5,7},{6,4},{7,5},{8,10},{9,11},{10,... | collective-permute-start | bytes 1572872 | tf_op jit(solution)/shard_map/ppermute | solution.py:441
  4.9 23.8 %collective-permute-start = (f32[512,256]{1,0:T(8,128)S(1)}, f32[512,256]{1,0:T(8,128)}, u32[]{:S(2)}, u32[]{:S(2)}) collective-permute-start(f32[512,256]{1,0:T(8,128)S(1)} %slice.8.skel_ref), channel_id=1, source_target_pairs={{0,1},{1,0},{2,3},{3,2},{4,5},{5,4},{6,7},{7,6},{8,9},{9,8},{10,11... | collective-permute-start | bytes 1572872 | tf_op jit(solution)/shard_map/ppermute | solution.py:441
  5.8 38.4 %collective-permute-start.7 = (f32[768,256]{1,0:T(8,128)}, f32[768,256]{1,0:T(8,128)}, u32[]{:S(2)}, u32[]{:S(2)}) collective-permute-start(f32[768,256]{1,0:T(8,128)} %pad_maximum_fusion), channel_id=1, source_target_pairs={{0,4},{1,5},{2,6},{3,7},{4,8},{5,9},{6,10},{7,11},{8,12},{9,13},{1... | collective-permute-start | bytes 2359304 | tf_op jit(solution)/shard_map/ppermute | solution.py:447
  7.3 36.8 %collective-permute-start.8 = (f32[768,256]{1,0:T(8,128)}, f32[768,256]{1,0:T(8,128)}, u32[]{:S(2)}, u32[]{:S(2)}) collective-permute-start(f32[768,256]{1,0:T(8,128)} %pad_maximum_fusion), channel_id=1, source_target_pairs={{0,28},{1,29},{2,30},{3,31},{4,0},{5,1},{6,2},{7,3},{8,4},{9,5},{1... | collective-permute-start | bytes 2359304 | tf_op jit(solution)/shard_map/ppermute | solution.py:447
  10.5 33.6 %collective-permute-start.6 = (f32[256,1024]{1,0:T(8,128)S(1)}, f32[256,1024]{1,0:T(8,128)S(1)}, u32[]{:S(2)}, u32[]{:S(2)}) collective-permute-start(f32[256,1024]{1,0:T(8,128)S(1)} %copy-done.1), channel_id=1, source_target_pairs={{0,2},{1,3},{2,0},{3,1},{4,6},{5,7},{6,4},{7,5},{8,10},{9,11},{10,... | collective-permute-start | bytes 3145736 | tf_op jit(solution)/shard_map/ppermute | solution.py:441
  17.6 11.1 %copy-start.14 = (f32[512,256]{1,0:T(8,128)}, f32[512,256]{1,0:T(8,128)S(1)}, u32[]{:S(2)}) copy-start(f32[512,256]{1,0:T(8,128)S(1)} %collective-permute-done.1.s2) | copy-start | bytes 1572868
  17.6 11.1 %collective-permute-start.2 = (f32[512,256]{1,0:T(8,128)S(1)}, f32[512,256]{1,0:T(8,128)S(1)}, u32[]{:S(2)}, u32[]{:S(2)}) collective-permute-start(f32[512,256]{1,0:T(8,128)S(1)} %collective-permute-done.1.s2), channel_id=1, source_target_pairs={{0,1},{1,0},{2,3},{3,2},{4,5},{5,4},{6,7},{7,6},{8,9},{9,8},{10,11... | collective-permute-start | bytes 1572872 | tf_op jit(solution)/shard_map/ppermute | solution.py:441
  28.7 0.8 copy-start.15
  34.2 14.2 %collective-permute-start.4 = (f32[1032,256]{1,0:T(8,128)}, f32[1032,256]{1,0:T(8,128)S(1)}, u32[]{:S(2)}, u32[]{:S(2)}) collective-permute-start(f32[1032,256]{1,0:T(8,128)} %own_window.1.after1.h0), channel_id=1, source_target_pairs={{0,1},{1,0},{2,3},{3,2},{4,5},{5,4},{6,7},{7,6},{8,9},{9,8},{10,11... | collective-permute-start | bytes 3170312 | tf_op jit(solution)/shard_map/ppermute | solution.py:441
  34.7 27.4 %collective-permute-start.3 = (f32[1032,256]{1,0:T(8,128)}, f32[1032,256]{1,0:T(8,128)S(1)}, u32[]{:S(2)}, u32[]{:S(2)}) collective-permute-start(f32[1032,256]{1,0:T(8,128)} %own_window.1.after1.h0), channel_id=1, source_target_pairs={{0,2},{1,3},{2,0},{3,1},{4,6},{5,7},{6,4},{7,5},{8,10},{9,11},{10,... | collective-permute-start | bytes 3170312 | tf_op jit(solution)/shard_map/ppermute | solution.py:441
  44.2 4.2 %copy-start.5 = (f32[256,1024]{1,0:T(8,128)}, f32[256,1024]{1,0:T(8,128)S(1)}, u32[]{:S(2)}) copy-start(f32[256,1024]{1,0:T(8,128)S(1)} %collective-permute-done.6.p2) | copy-start | bytes 3145732
  44.2 2.7 %collective-permute-start.9 = (f32[256,1024]{1,0:T(8,128)S(1)}, f32[256,1024]{1,0:T(8,128)S(1)}, u32[]{:S(2)}, u32[]{:S(2)}) collective-permute-start(f32[256,1024]{1,0:T(8,128)S(1)} %collective-permute-done.6.p2), channel_id=1, source_target_pairs={{0,1},{1,0},{2,3},{3,2},{4,5},{5,4},{6,7},{7,6},{8,9},{9,8},{10,11... | collective-permute-start | bytes 3145736 | tf_op jit(solution)/shard_map/ppermute | solution.py:441
  44.4 4.0 %collective-permute-start.5 = (f32[256,1024]{1,0:T(8,128)S(1)}, f32[256,1024]{1,0:T(8,128)S(1)}, u32[]{:S(2)}, u32[]{:S(2)}) collective-permute-start(f32[256,1024]{1,0:T(8,128)S(1)} %copy-done.1), channel_id=1, source_target_pairs={{0,1},{1,0},{2,3},{3,2},{4,5},{5,4},{6,7},{7,6},{8,9},{9,8},{10,11... | collective-permute-start | bytes 3145736 | tf_op jit(solution)/shard_map/ppermute | solution.py:441
  46.9 1.5 %copy-start.6 = (f32[256,1024]{1,0:T(8,128)}, f32[256,1024]{1,0:T(8,128)S(1)}, u32[]{:S(2)}) copy-start(f32[256,1024]{1,0:T(8,128)S(1)} %collective-permute-done.9.p3) | copy-start | bytes 3145732
  48.4 1.0 copy-start.7
  49.4 1.0 copy-start.3
  62.1 2.8 %copy-start.2 = (f32[1032,256]{1,0:T(8,128)}, f32[1032,256]{1,0:T(8,128)S(1)}, u32[]{:S(2)}) copy-start(f32[1032,256]{1,0:T(8,128)S(1)} %collective-permute-done.3.h2) | copy-start | bytes 3170308
  62.2 2.8 %collective-permute-start.10 = (f32[1032,256]{1,0:T(8,128)S(1)}, f32[1032,256]{1,0:T(8,128)S(1)}, u32[]{:S(2)}, u32[]{:S(2)}) collective-permute-start(f32[1032,256]{1,0:T(8,128)S(1)} %collective-permute-done.3.h2), channel_id=1, source_target_pairs={{0,1},{1,0},{2,3},{3,2},{4,5},{5,4},{6,7},{7,6},{8,9},{9,8},{10,11... | collective-permute-start | bytes 3170312 | tf_op jit(solution)/shard_map/ppermute | solution.py:441
  62.4 35.0 %collective-permute-start.15 = (f32[768,256]{1,0:T(8,128)}, f32[768,256]{1,0:T(8,128)S(1)}, u32[]{:S(2)}, u32[]{:S(2)}) collective-permute-start(f32[768,256]{1,0:T(8,128)} %collective-permute-done.8.rest_4_), channel_id=1, source_target_pairs={{0,2},{1,3},{2,0},{3,1},{4,6},{5,7},{6,4},{7,5},{8,10},{9,11},{10,... | collective-permute-start | bytes 2359304 | tf_op jit(solution)/shard_map/ppermute | solution.py:441
  63.6 35.6 %collective-permute-start.12 = (f32[768,256]{1,0:T(8,128)}, f32[768,256]{1,0:T(8,128)S(1)}, u32[]{:S(2)}, u32[]{:S(2)}) collective-permute-start(f32[768,256]{1,0:T(8,128)} %collective-permute-done.7.rest_0_), channel_id=1, source_target_pairs={{0,2},{1,3},{2,0},{3,1},{4,6},{5,7},{6,4},{7,5},{8,10},{9,11},{10,... | collective-permute-start | bytes 2359304 | tf_op jit(solution)/shard_map/ppermute | solution.py:441
  64.4 34.8 %collective-permute-start.11 = (f32[768,256]{1,0:T(8,128)}, f32[768,256]{1,0:T(8,128)S(1)}, u32[]{:S(2)}, u32[]{:S(2)}) collective-permute-start(f32[768,256]{1,0:T(8,128)} %collective-permute-done.7.rest_0_), channel_id=1, source_target_pairs={{0,1},{1,0},{2,3},{3,2},{4,5},{5,4},{6,7},{7,6},{8,9},{9,8},{10,11... | collective-permute-start | bytes 2359304 | tf_op jit(solution)/shard_map/ppermute | solution.py:441
  64.4 34.8 %collective-permute-start.14 = (f32[768,256]{1,0:T(8,128)}, f32[768,256]{1,0:T(8,128)S(1)}, u32[]{:S(2)}, u32[]{:S(2)}) collective-permute-start(f32[768,256]{1,0:T(8,128)} %collective-permute-done.8.rest_4_), channel_id=1, source_target_pairs={{0,1},{1,0},{2,3},{3,2},{4,5},{5,4},{6,7},{7,6},{8,9},{9,8},{10,11... | collective-permute-start | bytes 2359304 | tf_op jit(solution)/shard_map/ppermute | solution.py:441
  64.9 1.0 copy-start.4
  97.4 4.1 %copy-start.8 = (f32[768,256]{1,0:T(8,128)}, f32[768,256]{1,0:T(8,128)S(1)}, u32[]{:S(2)}) copy-start(f32[768,256]{1,0:T(8,128)S(1)} %collective-permute-done.15.rest_6_) | copy-start | bytes 2359300
  97.4 2.3 %collective-permute-start.16 = (f32[768,256]{1,0:T(8,128)S(1)}, f32[768,256]{1,0:T(8,128)S(1)}, u32[]{:S(2)}, u32[]{:S(2)}) collective-permute-start(f32[768,256]{1,0:T(8,128)S(1)} %collective-permute-done.15.rest_6_), channel_id=1, source_target_pairs={{0,1},{1,0},{2,3},{3,2},{4,5},{5,4},{6,7},{7,6},{8,9},{9,8},{10,11... | collective-permute-start | bytes 2359304 | tf_op jit(solution)/shard_map/ppermute | solution.py:441
  99.2 2.3 %copy-start.9 = (f32[768,256]{1,0:T(8,128)}, f32[768,256]{1,0:T(8,128)S(1)}, u32[]{:S(2)}) copy-start(f32[768,256]{1,0:T(8,128)S(1)} %collective-permute-done.12.rest_2_) | copy-start | bytes 2359300
  99.2 2.3 %collective-permute-start.13 = (f32[768,256]{1,0:T(8,128)S(1)}, f32[768,256]{1,0:T(8,128)S(1)}, u32[]{:S(2)}, u32[]{:S(2)}) collective-permute-start(f32[768,256]{1,0:T(8,128)S(1)} %collective-permute-done.12.rest_2_), channel_id=1, source_target_pairs={{0,1},{1,0},{2,3},{3,2},{4,5},{5,4},{6,7},{7,6},{8,9},{9,8},{10,11... | collective-permute-start | bytes 2359304 | tf_op jit(solution)/shard_map/ppermute | solution.py:441
  99.2 2.3 %copy-start.10 = (f32[768,256]{1,0:T(8,128)}, f32[768,256]{1,0:T(8,128)S(1)}, u32[]{:S(2)}) copy-start(f32[768,256]{1,0:T(8,128)S(1)} %collective-permute-done.11.rest_1_) | copy-start | bytes 2359300
  99.3 2.3 %copy-start.11 = (f32[768,256]{1,0:T(8,128)}, f32[768,256]{1,0:T(8,128)S(1)}, u32[]{:S(2)}) copy-start(f32[768,256]{1,0:T(8,128)S(1)} %collective-permute-done.14.rest_5_) | copy-start | bytes 2359300
  99.7 1.8 %copy-start.12 = (f32[768,256]{1,0:T(8,128)}, f32[768,256]{1,0:T(8,128)S(1)}, u32[]{:S(2)}) copy-start(f32[768,256]{1,0:T(8,128)S(1)} %collective-permute-done.16.rest_7_) | copy-start | bytes 2359300
  101.5 0.9 copy-start.13
  108.5 14.7 %collective-permute-start.18 = (f32[256,512]{1,0:T(8,128)}, f32[256,512]{1,0:T(8,128)S(1)}, u32[]{:S(2)}, u32[]{:S(2)}) collective-permute-start(f32[256,512]{1,0:T(8,128)} %side_windows.1.after1.v0), channel_id=1, source_target_pairs={{0,2},{1,3},{2,0},{3,1},{4,6},{5,7},{6,4},{7,5},{8,10},{9,11},{10,... | collective-permute-start | bytes 1572872 | tf_op jit(solution)/shard_map/ppermute | solution.py:441
  110.3 12.9 %collective-permute-start.17 = (f32[256,512]{1,0:T(8,128)}, f32[256,512]{1,0:T(8,128)S(1)}, u32[]{:S(2)}, u32[]{:S(2)}) collective-permute-start(f32[256,512]{1,0:T(8,128)} %side_windows.1.after1.v0), channel_id=1, source_target_pairs={{0,1},{1,0},{2,3},{3,2},{4,5},{5,4},{6,7},{7,6},{8,9},{9,8},{10,11... | collective-permute-start | bytes 1572872 | tf_op jit(solution)/shard_map/ppermute | solution.py:441
  123.2 1.9 %copy-start.16 = (f32[256,512]{1,0:T(8,128)}, f32[256,512]{1,0:T(8,128)S(1)}, u32[]{:S(2)}) copy-start(f32[256,512]{1,0:T(8,128)S(1)} %collective-permute-done.18.v2) | copy-start | bytes 1572868
  123.2 1.9 %collective-permute-start.19 = (f32[256,512]{1,0:T(8,128)S(1)}, f32[256,512]{1,0:T(8,128)S(1)}, u32[]{:S(2)}, u32[]{:S(2)}) collective-permute-start(f32[256,512]{1,0:T(8,128)S(1)} %collective-permute-done.18.v2), channel_id=1, source_target_pairs={{0,1},{1,0},{2,3},{3,2},{4,5},{5,4},{6,7},{7,6},{8,9},{9,8},{10,11... | collective-permute-start | bytes 1572872 | tf_op jit(solution)/shard_map/ppermute | solution.py:441
  123.2 1.9 %copy-start.17 = (f32[256,512]{1,0:T(8,128)}, f32[256,512]{1,0:T(8,128)S(1)}, u32[]{:S(2)}) copy-start(f32[256,512]{1,0:T(8,128)S(1)} %collective-permute-done.17.v1) | copy-start | bytes 1572868
  125.1 0.8 copy-start.18

commit v4 on v3

--- a/solution.py
+++ b/solution.py
@@ -22,14 +22,15 @@
 AHEAD = 2
 MIDDLE = 30_000_000_000
 
-VMEM_BYTES = 56 * 1024 * 1024
+VMEM_BYTES = 64 * 1024 * 1024
+VMEM_EARLY = 48 * 1024 * 1024
 
 NN = (((1,), (0,)), ((), ()))
 TN = (((0,), (0,)), ((), ()))
 
 
-def params():
-    return pltpu.CompilerParams(vmem_limit_bytes=VMEM_BYTES)
+def params(limit=VMEM_BYTES):
+    return pltpu.CompilerParams(vmem_limit_bytes=limit)
 
 
 def in_vmem():
@@ -245,37 +246,66 @@
 
 
 def own_kernel(
-    me_ref, near_ref, far_ref, high_ref, low_ref, far_hbm, schur_ref, s1, s2, s3, out_ref, sems
+    me_ref, near_ref, far_ref, high_hbm, low_hbm, far_hbm, schur_hbm, s1, s2, s3,
+    out_ref, high_held, low_held, skel_held, sems, own_sem,
 ):
     slots = sibling_slots(me_ref, near_ref, far_ref)
-    copies = [
-        pltpu.make_async_copy(far_hbm.at[f], out_ref.at[block_rows(s + 1), :], sems.at[s])
-        for s, (_, _, f) in enumerate(slots)
-    ]
-    for copy in copies:
-        copy.start()
-    out_ref[block_rows(0), :] = schur_ref[...]
+    own_copy = pltpu.make_async_copy(schur_hbm, out_ref.at[block_rows(0), :], own_sem)
+    near_copies = []
+    far_copies = []
+    for s, sibling in enumerate((s1, s2, s3)):
+        near_copies.append(
+            [
+                pltpu.make_async_copy(high_hbm.at[s], high_held.at[s], sems.at[0, s]),
+                pltpu.make_async_copy(low_hbm.at[s], low_held.at[s], sems.at[1, s]),
+                pltpu.make_async_copy(sibling, skel_held.at[s], sems.at[2, s]),
+            ]
+        )
+        far_copies.append(
+            pltpu.make_async_copy(
+                far_hbm.at[slots[s][2]], out_ref.at[block_rows(s + 1), :], sems.at[0, s]
+            )
+        )
+
+        @pl.when(slots[s][0] < NEAR)
+        def _(s=s):
+            for copy in near_copies[s]:
+                copy.start()
+
+        @pl.when(slots[s][0] >= NEAR)
+        def _(s=s):
+            far_copies[s].start()
+
+    own_copy.start()
     out_ref[GROUP * RANK :, :] = jnp.zeros((ROWS, RANK), jnp.float32)
-    for s, sibling in enumerate((s1, s2, s3)):
-        copies[s].wait()
+    for s in range(GROUP - 1):
 
         @pl.when(slots[s][0] < NEAR)
-        def _(s=s, sibling=sibling):
-            out_ref[block_rows(s + 1), :] = dot3((high_ref[s], low_ref[s]), split(sibling[...]))
-
-
-def side_kernel(blocks, me_ref, near_ref, far_ref, high_hbm, low_hbm, far_hbm, *rest):
-    zs, (after1, out_ref, z_held, high_held, low_held, far_held, h_high, h_low, s_high, s_low, sems) = (
-        rest[:8],
-        rest[8:],
+        def _(s=s):
+            for copy in near_copies[s]:
+                copy.wait()
+            out_ref[block_rows(s + 1), :] = dot3((high_held[s], low_held[s]), split(skel_held[s]))
+
+        @pl.when(slots[s][0] >= NEAR)
+        def _(s=s):
+            far_copies[s].wait()
+
+    own_copy.wait()
+
+
+def side_kernel(blocks, members, me_ref, near_ref, far_ref, high_hbm, low_hbm, far_hbm, *rest):
+    count = len(members)
+    zs, (earlier, out_ref, z_held, high_held, low_held, far_held, h_high, h_low, s_high, s_low, sems) = (
+        rest[: 2 * count],
+        rest[2 * count :],
     )
     slots = []
     z_copies = []
     near_copies = []
     far_copies = []
     for side, shift in enumerate((blocks - GROUP, GROUP)):
-        for s in range(GROUP):
-            n = side * GROUP + s
+        for place, s in enumerate(members):
+            n = side * count + place
             leaf = lax.rem(jnp.bitwise_xor(me_ref[0], s) + shift, blocks)
             slot, m, f = source_of(leaf, near_ref, far_ref)
             slots.append(slot)
@@ -287,7 +317,7 @@
                 ]
             )
             far_copies.append(pltpu.make_async_copy(far_hbm.at[f], far_held.at[n], sems.at[1, n]))
-    for n in range(2 * GROUP):
+    for n in range(2 * count):
         z_copies[n].start()
 
         @pl.when(slots[n] < NEAR)
@@ -300,9 +330,9 @@
             far_copies[n].start()
 
     for side in range(2):
-        for s in range(GROUP):
-            n = side * GROUP + s
-            cols = slice(s * RANK, (s + 1) * RANK)
+        for place in range(count):
+            n = side * count + place
+            cols = slice(place * RANK, (place + 1) * RANK)
             z_copies[n].wait()
 
             @pl.when(slots[n] < NEAR)
@@ -323,9 +353,9 @@
             high, low = split(z_held[n, LEAF:, :])
             s_high[cols, :] = high
             s_low[cols, :] = low
-        out_ref[:, side * RANK : (side + 1) * RANK] = dot3(
-            (h_high[...], h_low[...]), (s_high[...], s_low[...])
-        )
+        half = slice(side * RANK, (side + 1) * RANK)
+        total = dot3((h_high[...], h_low[...]), (s_high[...], s_low[...]))
+        out_ref[:, half] = total
 
 
 def partial_sums(p_high, p_low, h_refs, first, v_high, v_low):
@@ -338,30 +368,61 @@
         v_low[rows, :] = low
 
 
+def load_bases(p_hbm, p_held, p_high, p_low, sems):
+    copies = []
+    for s, base in enumerate(p_hbm):
+        rows = block_rows(s)
+        copies.append(pltpu.make_async_copy(base, p_held.at[rows, :], sems.at[s]))
+        copies[s].start()
+
+    def finish(use=None):
+        for s in range(GROUP):
+            rows = block_rows(s)
+            copies[s].wait()
+            high, low = split(p_held[rows, :])
+            p_high[rows, :] = high
+            p_low[rows, :] = low
+            if use is not None:
+                use(rows)
+
+    return finish
+
+
 def chip_kernel(
-    me_ref, h0, h1, p0, p1, p2, p3, after1, p_high, p_low, t_high, t_low, part_ref, v_high, v_low
+    me_ref, h0, h1, p0, p1, p2, p3, after1, t_high, t_low, part_hbm,
+    h_held, p_held, p_high, p_low, v_high, v_low, part, sems, p_sems, o_sems,
 ):
     member = lax.rem(me_ref[0], GROUP)
     slab = pl.ds(pl.multiple_of(member * RANK, RANK), RANK)
-    for s, base in enumerate((p0, p1, p2, p3)):
-        rows = slice(s * RANK, (s + 1) * RANK)
-        high, low = split(base[...])
-        p_high[rows, :] = high
-        p_low[rows, :] = low
-        high, low = split(base[:, slab].T)
+    finish = load_bases((p0, p1, p2, p3), p_held, p_high, p_low, p_sems)
+    copies = [pltpu.make_async_copy(h, h_held.at[s], sems.at[s]) for s, h in enumerate((h0, h1))]
+    for copy in copies:
+        copy.start()
+
+    def own_slab(rows):
+        high, low = split(p_held[rows, slab].T)
         t_high[:, rows] = high
         t_low[:, rows] = low
-    partial_sums(p_high, p_low, (h0, h1), 0, v_high, v_low)
+
+    finish(own_slab)
+    for copy in copies:
+        copy.wait()
+    partial_sums(p_high, p_low, h_held, 0, v_high, v_low)
     half = slice(0, 2 * RANK)
+    sent = []
     for m in range(GROUP):
-        cols = slice(m * RANK, (m + 1) * RANK)
-        part_ref[cols, :] = dot3(
-            (p_high[half, cols], p_low[half, cols]), (v_high[...], v_low[...]), TN
-        )
-
-
-def eliminate(work, u_tile, m_tile, first, last):
+        cols = block_rows(m)
+        part[cols, :] = dot3((p_high[half, cols], p_low[half, cols]), (v_high[...], v_low[...]), TN)
+        sent.append(pltpu.make_async_copy(part.at[cols, :], part_hbm.at[cols, :], o_sems.at[m]))
+        sent[m].start()
+    for copy in sent:
+        copy.wait()
+
+
+def eliminate(work, u_tile, m_tile, first, last, before_last=None):
     def step(k, carry):
+        if before_last is not None:
+            pl.when(k == last - 1)(before_last)
         rows = pl.ds(pl.multiple_of(k * TILE, TILE), TILE)
         upper, inverse = tile_factor(work[rows, rows])
         u_tile[...] = upper
@@ -385,14 +446,25 @@
 
 
 def parent_kernel(
-    me_ref, h2, h3, p_high, p_low, part_ref, work, edge_ref, v_high, v_low, whole, u_tile, m_tile
+    me_ref, h2, h3, p0, p1, p2, p3, part_hbm, work_hbm, edge_ref,
+    h_held, p_held, p_high, p_low, v_high, v_low, part, whole, work, u_tile, m_tile, sems, p_sems, o_sems,
 ):
     member = lax.rem(me_ref[0], GROUP)
-    partial_sums(p_high, p_low, (h2, h3), 2, v_high, v_low)
+    copies = [pltpu.make_async_copy(h, h_held.at[s], sems.at[s]) for s, h in enumerate((h2, h3))]
+    for copy in copies:
+        copy.start()
+    finish = load_bases((p0, p1, p2, p3), p_held, p_high, p_low, p_sems)
+    part_copy = pltpu.make_async_copy(part_hbm, part, sems.at[2])
+    part_copy.start()
+    finish()
+    for copy in copies:
+        copy.wait()
+    partial_sums(p_high, p_low, h_held, 2, v_high, v_low)
     half = slice(2 * RANK, PAR)
+    part_copy.wait()
     for m in range(GROUP):
-        cols = slice(m * RANK, (m + 1) * RANK)
-        whole[cols, :] = part_ref[cols, :] + dot3(
+        cols = block_rows(m)
+        whole[cols, :] = part[cols, :] + dot3(
             (p_high[half, cols], p_low[half, cols]), (v_high[...], v_low[...]), TN
         )
     square = whole[:PRED, :PRED]
@@ -401,7 +473,13 @@
     work[:, PAR:] = whole[PRED:, :PRED].T
     slab = pl.ds(pl.multiple_of(member * RANK, RANK), RANK)
     edge_ref[...] = whole[slab, PRED:]
-    eliminate(work, u_tile, m_tile, 0, EARLY)
+    done = (EARLY - 1) * TILE
+    held_rows = pltpu.make_async_copy(work.at[:done, :], work_hbm.at[:done, :], o_sems.at[0])
+    open_rows = pltpu.make_async_copy(work.at[done:, :], work_hbm.at[done:, :], o_sems.at[1])
+    eliminate(work, u_tile, m_tile, 0, EARLY, held_rows.start)
+    open_rows.start()
+    held_rows.wait()
+    open_rows.wait()
 
 
 def finish_kernel(me_ref, work_hbm, edge_in, after1, factor_ref, edge_ref, work, u_tile, m_tile, sems):
@@ -429,7 +507,7 @@
 def couple_kernel(t_high, t_low, v0, v1, v2, v3, edge_ref, out_ref):
     total = jnp.zeros((RANK, 2 * RANK), jnp.float32)
     for s, v_ref in enumerate((v0, v1, v2, v3)):
-        cols = slice(s * RANK, (s + 1) * RANK)
+        cols = block_rows(s)
         total = total + dot3((t_high[:, cols], t_low[:, cols]), split(v_ref[...]))
     out_ref[:, :RANK] = total[:, :RANK]
     out_ref[:, RANK : 2 * RANK] = edge_ref[...]
@@ -458,14 +536,14 @@
     return [value, core, chip, both]
 
 
-def call(kernel, name, ins, outs, scratch, *operands, flops=1):
+def call(kernel, name, ins, outs, scratch, *operands, flops=1, spaces=None, limit=VMEM_BYTES):
     return pl.pallas_call(
         kernel,
         in_specs=ins,
-        out_specs=[in_vmem()] * len(outs),
+        out_specs=spaces or [in_vmem()] * len(outs),
         out_shape=[jax.ShapeDtypeStruct(shape, dtype) for shape, dtype in outs],
         scratch_shapes=scratch,
-        compiler_params=params(),
+        compiler_params=params(limit),
         cost_estimate=pl.CostEstimate(flops=flops, bytes_accessed=1, transcendentals=0),
 
         name=name,
@@ -504,6 +582,7 @@
         far_index,
         skeleton,
         near,
+        limit=VMEM_EARLY,
     )
     leaf_out, leaf_schur = call(
         leaf_kernel,
@@ -515,6 +594,7 @@
         basis,
         sib_high,
         flops=MIDDLE,
+        limit=VMEM_EARLY,
     )
     skel_chip = swapped(skeleton, "blk", 2)
     skel_core = swapped(skeleton, "blk", 1)
@@ -522,9 +602,14 @@
     (own,) = call(
         own_kernel,
         "own_window",
-        [in_smem()] * 3 + [in_vmem()] * 2 + [anywhere()] + [in_vmem()] * 4,
+        [in_smem()] * 3 + [anywhere()] * 7,
         [((GROUP * RANK + ROWS, RANK), f32)],
-        [pltpu.SemaphoreType.DMA((GROUP - 1,))],
+        [pltpu.VMEM((GROUP - 1, RANK, LEAF), b16)] * 2
+        + [
+            pltpu.VMEM((GROUP - 1, LEAF, RANK), f32),
+            pltpu.SemaphoreType.DMA((3, GROUP - 1)),
+            pltpu.SemaphoreType.DMA,
+        ],
         me,
         near_index,
         far_index,
@@ -556,63 +641,82 @@
     base_core = swapped(after(parent_basis, left_high), "blk", 1)
     base_both = swapped(after(base_chip, left_high, prev_load, next_load), "blk", 1)
     bases = [parent_basis, base_core, base_chip, base_both]
-    p_high, p_low, t_high, t_low, part = call(
+    dma = pltpu.SemaphoreType.DMA
+    loads = [
+        pltpu.VMEM((2, GROUP * RANK + ROWS, RANK), f32),
+        pltpu.VMEM((PAR, PAR), f32),
+        pltpu.VMEM((PAR, PAR), b16),
+        pltpu.VMEM((PAR, PAR), b16),
+        pltpu.VMEM((2 * RANK, PAR), b16),
+        pltpu.VMEM((2 * RANK, PAR), b16),
+        pltpu.VMEM((PAR, PAR), f32),
+    ]
+    t_high, t_low, part = call(
         chip_kernel,
         "chip_sums",
-        [in_smem()] + [in_vmem()] * 6 + [anywhere()],
-        [((PAR, PAR), b16)] * 2 + [((RANK, PAR), b16)] * 2 + [((PAR, PAR), f32)],
-        [pltpu.VMEM((2 * RANK, PAR), b16)] * 2,
+        [in_smem()] + [anywhere()] * 7,
+        [((RANK, PAR), b16)] * 2 + [((PAR, PAR), f32)],
+        loads + [dma((2,)), dma((GROUP,)), dma((GROUP,))],
         me,
         own,
         own_core,
         *bases,
         left_high,
+        spaces=[in_vmem(), in_vmem(), anywhere()],
     )
     own_both = swapped(after(own_chip, part), "blk", 1)
-    prev_load = after(prev_load, own_chip)
-    next_load = after(next_load, own_chip)
+    prev_load = after(prev_load, part)
+    next_load = after(next_load, part)
     tiles = [pltpu.VMEM((TILE, TILE), f32)] * 2
     work, edge_rows = call(
         parent_kernel,
         "parent_factor",
-        [in_smem()] + [in_vmem()] * 5,
+        [in_smem()] + [anywhere()] * 7,
         [((PRED, WIDE), f32), ((RANK, RANK), f32)],
-        [pltpu.VMEM((2 * RANK, PAR), b16)] * 2 + [pltpu.VMEM((PAR, PAR), f32)] + tiles,
+        loads
+        + [pltpu.VMEM((PAR, PAR), f32), pltpu.VMEM((PRED, WIDE), f32)]
+        + tiles
+        + [dma((3,)), dma((GROUP,)), dma((2,))],
         me,
         own_chip,
         own_both,
-        p_high,
-        p_low,
+        *bases,
         part,
+        spaces=[anywhere(), in_vmem()],
     )
     from_prev = gathered(prev_load, "blk", edge_rows)
     from_next = gathered(next_load, "blk", edge_rows)
-    (side,) = call(
-        functools.partial(side_kernel, blocks),
-        "side_windows",
-        [in_smem()] * 3 + [anywhere()] * 12,
-        [((RANK, 2 * RANK), f32)],
-        [
-            pltpu.VMEM((2 * GROUP, LEAF + RANK, RANK), f32),
-            pltpu.VMEM((2 * GROUP, RANK, LEAF), b16),
-            pltpu.VMEM((2 * GROUP, RANK, LEAF), b16),
-            pltpu.VMEM((2 * GROUP, RANK, RANK), f32),
-            pltpu.VMEM((RANK, PAR), b16),
-            pltpu.VMEM((RANK, PAR), b16),
-            pltpu.VMEM((PAR, RANK), b16),
-            pltpu.VMEM((PAR, RANK), b16),
-            pltpu.SemaphoreType.DMA((3, 2 * GROUP)),
-        ],
-        me,
-        near_index,
-        far_index,
-        left_high,
-        left_low,
-        far,
-        *from_prev,
-        *from_next,
-        edge_rows,
-    )
+
+    def windows(members, name, earlier):
+        count = len(members)
+        return call(
+            functools.partial(side_kernel, blocks, members),
+            name,
+            [in_smem()] * 3 + [anywhere()] * (4 + 2 * count),
+            [((RANK, 2 * RANK), f32)],
+            [
+                pltpu.VMEM((2 * count, LEAF + RANK, RANK), f32),
+                pltpu.VMEM((2 * count, RANK, LEAF), b16),
+                pltpu.VMEM((2 * count, RANK, LEAF), b16),
+                pltpu.VMEM((2 * count, RANK, RANK), f32),
+                pltpu.VMEM((RANK, count * RANK), b16),
+                pltpu.VMEM((RANK, count * RANK), b16),
+                pltpu.VMEM((count * RANK, RANK), b16),
+                pltpu.VMEM((count * RANK, RANK), b16),
+                dma((3, 2 * count)),
+            ],
+            me,
+            near_index,
+            far_index,
+            left_high,
+            left_low,
+            far,
+            *[from_prev[s] for s in members],
+            *[from_next[s] for s in members],
+            earlier,
+        )[0]
+
+    side = windows((0, 1, 2, 3), "side_windows", edge_rows)
     factor_rows, edge_rows = call(
         finish_kernel,
         "parent_finish",

time: 130 us -> 129 us (level)
  waiting for transfers between devices: 13.7 us -> 20 us
  Pallas kernels: 91.6 us -> 86.6 us
  local copies, waits for them, and re-layouts: 6.62 us -> 5.27 us
    pallas_call x8, Pallas kernels: 83.9 us -> 78.8 us  [call(): pl.pallas_call(kernel, in_specs=ins, out_specs=spaces or [in_vmem()] * le...]
    ppermute x18, waiting for transfers between devices: 13.7 us -> 17.6 us  [swapped(): return lax.ppermute(value, axis, pairs)]
    ppermute x2, waiting for transfers between devices: 0.01 us -> 2.44 us  [shifted(): return lax.ppermute(value, axis, pairs)]
    unnamed x38 -> x20, local copies, waits for them, and re-layouts: 5.43 us -> 3.18 us
  transfers between devices with their start and end apart: 20 -> 20, of which waited for: 8 -> 11; matrix products, arithmetic and copies ran while one was open for 1% -> 2% of each run, Pallas kernels for 63% -> 59%
where the time goes in v4:
time: 129 us
  Pallas kernels  86.6 us (67%)
  waiting for transfers between devices  20 us (16%)
  starting transfers between devices  15.1 us (12%)
  local copies, waits for them, and re-layouts  5.27 us (4%)
    pallas_call x8, Pallas kernels, call(): pl.pallas_call(kernel, in_specs=ins, out_specs=spaces or [in_vmem()] * le...  78.8 us
    ppermute x18, waiting for transfers between devices, swapped(): return lax.ppermute(value, axis, pairs)  17.6 us
    ppermute x18, starting transfers between devices, swapped(): return lax.ppermute(value, axis, pairs)  10.1 us
    pallas_call x1, Pallas kernels, on_device(): pl.pallas_call(left_kernel, grid=(NEAR,), in_specs=[pl.BlockSpec((LEAF, R...  7.73 us
    ppermute x2, starting transfers between devices, shifted(): return lax.ppermute(value, axis, pairs)  4.94 us
    unnamed x20, local copies, waits for them, and re-layouts  3.18 us
  transfers between devices with their start and end apart: 20, of which 11 were waited for; matrix products, arithmetic and copies ran while one was open for 2% of the time, Pallas kernels for 59%

profile of v4, /device:TPU:0, one launch (start us, length us, event | category | flops | bytes accessed | tf_op | source)
XLA Modules:
  0.0 128.7 jit_solution(11840597625133385594)
XLA Ops:
  0.6 0.0 copy-start.4
  0.6 0.0 copy-start.5
  0.7 1.1 slice.8.skel_ref
  1.7 3.0 %collective-permute-start.1 = (f32[512,256]{1,0:T(8,128)S(1)}, f32[512,256]{1,0:T(8,128)S(1)}, u32[]{:S(2)}, u32[]{:S(2)}) collective-permute-start(f32[512,256]{1,0:T(8,128)S(1)} %slice.8.skel_ref), channel_id=1, source_target_pairs={{0,2},{1,3},{2,0},{3,1},{4,6},{5,7},{6,4},{7,5},{8,10},{9,11},{10,... | collective-permute-start | bytes 1572872 | tf_op jit(solution)/shard_map/ppermute | solution.py:519
  4.7 0.0 collective-permute-start
  4.7 0.2 collective-permute-start.6
  4.9 1.0 slice.7
  5.9 0.9 pad_maximum_fusion
  6.8 1.9 %collective-permute-start.7 = (f32[768,256]{1,0:T(8,128)}, f32[768,256]{1,0:T(8,128)}, u32[]{:S(2)}, u32[]{:S(2)}) collective-permute-start(f32[768,256]{1,0:T(8,128)} %pad_maximum_fusion), channel_id=1, source_target_pairs={{0,4},{1,5},{2,6},{3,7},{4,8},{5,9},{6,10},{7,11},{8,12},{9,13},{1... | collective-permute-start | bytes 2359304 | tf_op jit(solution)/shard_map/ppermute | solution.py:525
  8.7 3.0 %collective-permute-start.8 = (f32[768,256]{1,0:T(8,128)}, f32[768,256]{1,0:T(8,128)}, u32[]{:S(2)}, u32[]{:S(2)}) collective-permute-start(f32[768,256]{1,0:T(8,128)} %pad_maximum_fusion), channel_id=1, source_target_pairs={{0,28},{1,29},{2,30},{3,31},{4,0},{5,1},{6,2},{7,3},{8,4},{9,5},{1... | collective-permute-start | bytes 2359304 | tf_op jit(solution)/shard_map/ppermute | solution.py:525
  11.8 3.1 %sibling_products.1 = (bf16[3,256,512]{2,1,0:T(8,128)(2,1)S(1)}, bf16[3,256,512]{2,1,0:T(8,128)(2,1)S(1)}) custom-call(s32[1]{0:T(128)} %bitcast.2.me_ref, s32[1,6]{1,0:T(1,128)S(1)} %copy-done.4, s32[1,5]{1,0:T(1,128)S(1)} %copy-done.5, f32[512,256]{1,0:T(8,128)S(1)} %slice.8.skel_ref, f32[6,512,512]{2,1,0:T(8,128)} %bitcast.9), custom_call_target="tpu_custom_call" | custom-call | flops 1 | bytes 1 | tf_op jit(solution)/shard_map/sibling_products/pallas_call | solution.py:540
  14.9 0.0 copy-start.2
  14.9 0.9 copy-done.2
  15.8 1.7 %collective-permute-done.1.s2 = f32[512,256]{1,0:T(8,128)S(1)} collective-permute-done((f32[512,256]{1,0:T(8,128)S(1)}, f32[512,256]{1,0:T(8,128)S(1)}, u32[]{:S(2)}, u32[]{:S(2)}) %collective-permute-start.1) | collective-permute-done | bytes 524320 | tf_op jit(solution)/shard_map/ppermute | solution.py:519
  17.5 9.2 %leaf_factor.1 = (f32[256,512]{1,0:T(8,128)}, f32[256,256]{1,0:T(8,128)S(1)}) custom-call(f32[512,512]{1,0:T(8,128)S(1)} %bitcast.8, f32[512,512]{1,0:T(8,128)S(1)} %bitcast.7, bf16[3,256,512]{2,1,0:T(8,128)(2,1)S(1)} %get-tuple-element.24.after1.high_hbm), custom_call_target="tpu_custom_call" | custom-call | flops 30000001024 | bytes 1 | tf_op jit(solution)/shard_map/leaf_factor/pallas_call | solution.py:540
  26.8 0.7 copy-done.3
  27.5 0.0 collective-permute-done.2.s3
  27.5 0.8 copy-done.8
  28.3 0.8 copy-done.9
  29.1 3.8 %own_window.1.after1.h0 = f32[1032,256]{1,0:T(8,128)} custom-call(s32[1]{0:T(128)} %bitcast.2.me_ref, s32[1,6]{1,0:T(1,128)} %near_ref.5, s32[1,5]{1,0:T(1,128)} %far_ref.5, bf16[3,256,512]{2,1,0:T(8,128)(2,1)} %copy-done.1, bf16[3,256,512]{2,1,0:T(8,128)(2,1)} %copy-done.2, f32[5,256,256]{2,1,0:T(8,128)} %bitcast.11, f32[256,256]{1,0:T(8,128)} %copy-done.3, ...), custom_call_target="tpu_custom_call" | custom-call | flops 1 | bytes 1 | tf_op jit(solution)/shard_map/own_window/pallas_call | solution.py:540
  32.8 0.3 collective-permute-start.4
  33.2 1.9 %collective-permute-start.3 = (f32[1032,256]{1,0:T(8,128)}, f32[1032,256]{1,0:T(8,128)}, u32[]{:S(2)}, u32[]{:S(2)}) collective-permute-start(f32[1032,256]{1,0:T(8,128)} %own_window.1.after1.h0), channel_id=1, source_target_pairs={{0,2},{1,3},{2,0},{3,1},{4,6},{5,7},{6,4},{7,5},{8,10},{9,11},{10,... | collective-permute-start | bytes 3170312 | tf_op jit(solution)/shard_map/ppermute | solution.py:519
  35.1 7.7 %left_products.1 = (bf16[6,256,512]{2,1,0:T(8,128)(2,1)}, bf16[6,256,512]{2,1,0:T(8,128)(2,1)}) custom-call(f32[512,512]{1,0:T(8,128)} %bitcast.6, f32[6,512,512]{2,1,0:T(8,128)} %bitcast.10, f32[1032,256]{1,0:T(8,128)} %own_window.1.after1.h0), custom_call_target="tpu_custom_call" | custom-call | flops 1 | bytes 1 | tf_op jit(solution)/shard_map/left_products/pallas_call | solution.py:625
  42.9 0.2 collective-permute-done.7.rest_0_
  43.1 2.2 %collective-permute-done.8.rest_4_ = f32[768,256]{1,0:T(8,128)} collective-permute-done((f32[768,256]{1,0:T(8,128)}, f32[768,256]{1,0:T(8,128)}, u32[]{:S(2)}, u32[]{:S(2)}) %collective-permute-start.8) | collective-permute-done | bytes 786464 | tf_op jit(solution)/shard_map/ppermute | solution.py:525
  45.3 0.8 collective-permute-done.5.p1
  46.1 2.2 %collective-permute-done.9.p3 = f32[256,1024]{1,0:T(8,128)} collective-permute-done((f32[256,1024]{1,0:T(8,128)}, f32[256,1024]{1,0:T(8,128)}, u32[]{:S(2)}, u32[]{:S(2)}) %collective-permute-start.9) | collective-permute-done | bytes 1048608 | tf_op jit(solution)/shard_map/ppermute | solution.py:519
  48.3 0.0 collective-permute-done.4.h1
  48.3 11.5 %chip_sums.1 = (bf16[256,1024]{1,0:T(8,128)(2,1)}, bf16[256,1024]{1,0:T(8,128)(2,1)}, f32[1024,1024]{1,0:T(8,128)}) custom-call(s32[1]{0:T(128)} %bitcast.2.me_ref, f32[1032,256]{1,0:T(8,128)} %own_window.1.after1.h0, f32[1032,256]{1,0:T(8,128)} %collective-permute-done.4.h1, f32[256,1024]{1,0:T(8,128)} %p0.3, f32[256,1024]{1,0:T(8,128)} %collective-permute-done.5.p1, ...), custom_call_target="tpu_custom_call" | custom-call | flops 1 | bytes 1 | tf_op jit(solution)/shard_map/chip_sums/pallas_call | solution.py:540
  59.8 2.0 %collective-permute-done.3.h2 = f32[1032,256]{1,0:T(8,128)} collective-permute-done((f32[1032,256]{1,0:T(8,128)}, f32[1032,256]{1,0:T(8,128)}, u32[]{:S(2)}, u32[]{:S(2)}) %collective-permute-start.3) | collective-permute-done | bytes 1056800 | tf_op jit(solution)/shard_map/ppermute | solution.py:519
  61.9 1.7 %collective-permute-start.12 = (f32[768,256]{1,0:T(8,128)}, f32[768,256]{1,0:T(8,128)}, u32[]{:S(2)}, u32[]{:S(2)}) collective-permute-start(f32[768,256]{1,0:T(8,128)} %collective-permute-done.7.rest_0_), channel_id=1, source_target_pairs={{0,2},{1,3},{2,0},{3,1},{4,6},{5,7},{6,4},{7,5},{8,10},{9,11},{10,... | collective-permute-start | bytes 2359304 | tf_op jit(solution)/shard_map/ppermute | solution.py:519
  63.6 0.3 collective-permute-start.15
  63.9 0.5 collective-permute-start.14
  64.4 0.5 collective-permute-done.10.h3
  64.9 30.6 %parent_factor.1 = (f32[768,1280]{1,0:T(8,128)}, f32[256,256]{1,0:T(8,128)}) custom-call(s32[1]{0:T(128)} %bitcast.2.me_ref, f32[1032,256]{1,0:T(8,128)} %collective-permute-done.3.h2, f32[1032,256]{1,0:T(8,128)} %collective-permute-done.10.h3, f32[256,1024]{1,0:T(8,128)} %p0.3, f32[256,1024]{1,0:T(8,128)} %collective-permute-done.5.p1, ...), custom_call_target="tpu_custom_call" | custom-call | flops 1 | bytes 1 | tf_op jit(solution)/shard_map/parent_factor/pallas_call | solution.py:540
  95.5 0.0 collective-permute-done.12.rest_2_
  95.6 0.2 collective-permute-start.13
  95.8 3.3 %collective-permute-done.15.rest_6_ = f32[768,256]{1,0:T(8,128)} collective-permute-done((f32[768,256]{1,0:T(8,128)}, f32[768,256]{1,0:T(8,128)}, u32[]{:S(2)}, u32[]{:S(2)}) %collective-permute-start.15) | collective-permute-done | bytes 786464 | tf_op jit(solution)/shard_map/ppermute | solution.py:519
  99.0 0.0 collective-permute-start.16
  99.0 0.0 collective-permute-done.11.rest_1_
  99.0 2.6 %collective-permute-done.16.rest_7_ = f32[768,256]{1,0:T(8,128)} collective-permute-done((f32[768,256]{1,0:T(8,128)}, f32[768,256]{1,0:T(8,128)}, u32[]{:S(2)}, u32[]{:S(2)}) %collective-permute-start.16) | collective-permute-done | bytes 786464 | tf_op jit(solution)/shard_map/ppermute | solution.py:519
  101.6 6.4 %side_windows.1.after1.v0 = f32[256,512]{1,0:T(8,128)} custom-call(s32[1]{0:T(128)} %bitcast.2.me_ref, s32[1,6]{1,0:T(1,128)} %near_ref.5, s32[1,5]{1,0:T(1,128)} %far_ref.5, bf16[6,256,512]{2,1,0:T(8,128)(2,1)} %get-tuple-element.28.after1.high_hbm, bf16[6,256,512]{2,1,0:T(8,128)(2,1)} %get-tuple-element.35.low_hbm, f32[5,256,256]{2,1,0:T(8,128)} %bitcast.12, ...), custom_call_target="tpu_custom_call" | custom-call | flops 1 | bytes 1 | tf_op jit(solution)/shard_map/side_windows/pallas_call | solution.py:540
  108.0 1.8 %collective-permute-start.18 = (f32[256,512]{1,0:T(8,128)}, f32[256,512]{1,0:T(8,128)}, u32[]{:S(2)}, u32[]{:S(2)}) collective-permute-start(f32[256,512]{1,0:T(8,128)} %side_windows.1.after1.v0), channel_id=1, source_target_pairs={{0,2},{1,3},{2,0},{3,1},{4,6},{5,7},{6,4},{7,5},{8,10},{9,11},{10,... | collective-permute-start | bytes 1572872 | tf_op jit(solution)/shard_map/ppermute | solution.py:519
  109.8 0.2 collective-permute-start.17
  110.0 10.4 %parent_finish.1 = (f32[256,768]{1,0:T(8,128)}, f32[256,256]{1,0:T(8,128)}) custom-call(s32[1]{0:T(128)} %bitcast.2.me_ref, f32[768,1280]{1,0:T(8,128)} %get-tuple-element.33.work_hbm, f32[256,256]{1,0:T(8,128)} %get-tuple-element.34.rest_8_.edge_in, f32[256,512]{1,0:T(8,128)} %side_windows.1.after1.v0), custom_call_target="tpu_custom_call" | custom-call | flops 1 | bytes 1 | tf_op jit(solution)/shard_map/parent_finish/pallas_call | solution.py:540
  120.4 2.3 %collective-permute-done.18.v2 = f32[256,512]{1,0:T(8,128)} collective-permute-done((f32[256,512]{1,0:T(8,128)}, f32[256,512]{1,0:T(8,128)}, u32[]{:S(2)}, u32[]{:S(2)}) %collective-permute-start.18) | collective-permute-done | bytes 524320 | tf_op jit(solution)/shard_map/ppermute | solution.py:519
  122.6 2.2 %collective-permute-done.19.v3 = f32[256,512]{1,0:T(8,128)} collective-permute-done((f32[256,512]{1,0:T(8,128)}, f32[256,512]{1,0:T(8,128)}, u32[]{:S(2)}, u32[]{:S(2)}) %collective-permute-start.19) | collective-permute-done | bytes 524320 | tf_op jit(solution)/shard_map/ppermute | solution.py:519
  124.9 3.8 %coupling.1 = f32[256,768]{1,0:T(8,128)} custom-call(bf16[256,1024]{1,0:T(8,128)(2,1)} %get-tuple-element.41.t_high, bf16[256,1024]{1,0:T(8,128)(2,1)} %get-tuple-element.42.t_low, f32[256,512]{1,0:T(8,128)} %side_windows.1.after1.v0, f32[256,512]{1,0:T(8,128)} %collective-permute-done.17.v1, f32[256,512]{1,0:T(8,128)} %collective-permute-done.18.v2, ...), custom_call_target="tpu_custom_call" | custom-call | flops 1 | bytes 1 | tf_op jit(solution)/shard_map/coupling/pallas_call | solution.py:540
  (24 shorter events, 0.1 us)
Async XLA Ops:
  0.6 11.2 %copy-start.4 = (s32[1,6]{1,0:T(1,128)S(1)}, s32[1,6]{1,0:T(1,128)}, u32[]{:S(2)}) copy-start(s32[1,6]{1,0:T(1,128)} %near_ref.5) | copy-start | bytes 76
  0.6 11.1 %copy-start.5 = (s32[1,5]{1,0:T(1,128)S(1)}, s32[1,5]{1,0:T(1,128)}, u32[]{:S(2)}) copy-start(s32[1,5]{1,0:T(1,128)} %far_ref.5) | copy-start | bytes 64
  1.7 15.8 %collective-permute-start.1 = (f32[512,256]{1,0:T(8,128)S(1)}, f32[512,256]{1,0:T(8,128)S(1)}, u32[]{:S(2)}, u32[]{:S(2)}) collective-permute-start(f32[512,256]{1,0:T(8,128)S(1)} %slice.8.skel_ref), channel_id=1, source_target_pairs={{0,2},{1,3},{2,0},{3,1},{4,6},{5,7},{6,4},{7,5},{8,10},{9,11},{10,... | collective-permute-start | bytes 1572872 | tf_op jit(solution)/shard_map/ppermute | solution.py:519
  4.7 22.7 %collective-permute-start = (f32[512,256]{1,0:T(8,128)S(1)}, f32[512,256]{1,0:T(8,128)S(1)}, u32[]{:S(2)}, u32[]{:S(2)}) collective-permute-start(f32[512,256]{1,0:T(8,128)S(1)} %slice.8.skel_ref), channel_id=1, source_target_pairs={{0,1},{1,0},{2,3},{3,2},{4,5},{5,4},{6,7},{7,6},{8,9},{9,8},{10,11... | collective-permute-start | bytes 1572872 | tf_op jit(solution)/shard_map/ppermute | solution.py:519
  4.7 40.6 %collective-permute-start.6 = (f32[256,1024]{1,0:T(8,128)}, f32[256,1024]{1,0:T(8,128)}, u32[]{:S(2)}, u32[]{:S(2)}) collective-permute-start(f32[256,1024]{1,0:T(8,128)} %p0.3), channel_id=1, source_target_pairs={{0,2},{1,3},{2,0},{3,1},{4,6},{5,7},{6,4},{7,5},{8,10},{9,11},{10,... | collective-permute-start | bytes 3145736 | tf_op jit(solution)/shard_map/ppermute | solution.py:519
  6.8 36.3 %collective-permute-start.7 = (f32[768,256]{1,0:T(8,128)}, f32[768,256]{1,0:T(8,128)}, u32[]{:S(2)}, u32[]{:S(2)}) collective-permute-start(f32[768,256]{1,0:T(8,128)} %pad_maximum_fusion), channel_id=1, source_target_pairs={{0,4},{1,5},{2,6},{3,7},{4,8},{5,9},{6,10},{7,11},{8,12},{9,13},{1... | collective-permute-start | bytes 2359304 | tf_op jit(solution)/shard_map/ppermute | solution.py:525
  8.7 36.6 %collective-permute-start.8 = (f32[768,256]{1,0:T(8,128)}, f32[768,256]{1,0:T(8,128)}, u32[]{:S(2)}, u32[]{:S(2)}) collective-permute-start(f32[768,256]{1,0:T(8,128)} %pad_maximum_fusion), channel_id=1, source_target_pairs={{0,28},{1,29},{2,30},{3,31},{4,0},{5,1},{6,2},{7,3},{8,4},{9,5},{1... | collective-permute-start | bytes 2359304 | tf_op jit(solution)/shard_map/ppermute | solution.py:525
  11.8 5.7 %copy-start = (f32[1,512,512]{2,1,0:T(8,128)S(1)}, f32[1,512,512]{2,1,0:T(8,128)}, u32[]{:S(2)}) copy-start(f32[1,512,512]{2,1,0:T(8,128)} %param.10) | copy-start | bytes 3145732
  11.8 5.7 %copy-start.6 = (f32[1,512,512]{2,1,0:T(8,128)S(1)}, f32[1,512,512]{2,1,0:T(8,128)}, u32[]{:S(2)}) copy-start(f32[1,512,512]{2,1,0:T(8,128)} %param.7) | copy-start | bytes 3145732
  14.9 0.9 copy-start.2
  15.8 11.0 %copy-start.1 = (bf16[3,256,512]{2,1,0:T(8,128)(2,1)}, bf16[3,256,512]{2,1,0:T(8,128)(2,1)S(1)}, u32[]{:S(2)}) copy-start(bf16[3,256,512]{2,1,0:T(8,128)(2,1)S(1)} %get-tuple-element.24.after1.high_hbm) | copy-start | bytes 2359300
  17.5 9.3 %copy-start.7 = (f32[512,256]{1,0:T(8,128)}, f32[512,256]{1,0:T(8,128)S(1)}, u32[]{:S(2)}) copy-start(f32[512,256]{1,0:T(8,128)S(1)} %collective-permute-done.1.s2) | copy-start | bytes 1572868
  17.5 10.0 %collective-permute-start.2 = (f32[512,256]{1,0:T(8,128)S(1)}, f32[512,256]{1,0:T(8,128)S(1)}, u32[]{:S(2)}, u32[]{:S(2)}) collective-permute-start(f32[512,256]{1,0:T(8,128)S(1)} %collective-permute-done.1.s2), channel_id=1, source_target_pairs={{0,1},{1,0},{2,3},{3,2},{4,5},{5,4},{6,7},{7,6},{8,9},{9,8},{10,11... | collective-permute-start | bytes 1572872 | tf_op jit(solution)/shard_map/ppermute | solution.py:519
  26.8 0.7 copy-start.3
  27.5 0.8 copy-start.8
  28.3 0.8 copy-start.9
  32.8 15.5 %collective-permute-start.4 = (f32[1032,256]{1,0:T(8,128)}, f32[1032,256]{1,0:T(8,128)}, u32[]{:S(2)}, u32[]{:S(2)}) collective-permute-start(f32[1032,256]{1,0:T(8,128)} %own_window.1.after1.h0), channel_id=1, source_target_pairs={{0,1},{1,0},{2,3},{3,2},{4,5},{5,4},{6,7},{7,6},{8,9},{9,8},{10,11... | collective-permute-start | bytes 3170312 | tf_op jit(solution)/shard_map/ppermute | solution.py:519
  33.2 28.7 %collective-permute-start.3 = (f32[1032,256]{1,0:T(8,128)}, f32[1032,256]{1,0:T(8,128)}, u32[]{:S(2)}, u32[]{:S(2)}) collective-permute-start(f32[1032,256]{1,0:T(8,128)} %own_window.1.after1.h0), channel_id=1, source_target_pairs={{0,2},{1,3},{2,0},{3,1},{4,6},{5,7},{6,4},{7,5},{8,10},{9,11},{10,... | collective-permute-start | bytes 3170312 | tf_op jit(solution)/shard_map/ppermute | solution.py:519
  43.1 3.0 %collective-permute-start.5 = (f32[256,1024]{1,0:T(8,128)}, f32[256,1024]{1,0:T(8,128)}, u32[]{:S(2)}, u32[]{:S(2)}) collective-permute-start(f32[256,1024]{1,0:T(8,128)} %p0.3), channel_id=1, source_target_pairs={{0,1},{1,0},{2,3},{3,2},{4,5},{5,4},{6,7},{7,6},{8,9},{9,8},{10,11... | collective-permute-start | bytes 3145736 | tf_op jit(solution)/shard_map/ppermute | solution.py:519
  45.3 3.0 %collective-permute-start.9 = (f32[256,1024]{1,0:T(8,128)}, f32[256,1024]{1,0:T(8,128)}, u32[]{:S(2)}, u32[]{:S(2)}) collective-permute-start(f32[256,1024]{1,0:T(8,128)} %collective-permute-done.6.p2), channel_id=1, source_target_pairs={{0,1},{1,0},{2,3},{3,2},{4,5},{5,4},{6,7},{7,6},{8,9},{9,8},{10,11... | collective-permute-start | bytes 3145736 | tf_op jit(solution)/shard_map/ppermute | solution.py:519
  61.9 3.0 %collective-permute-start.10 = (f32[1032,256]{1,0:T(8,128)}, f32[1032,256]{1,0:T(8,128)}, u32[]{:S(2)}, u32[]{:S(2)}) collective-permute-start(f32[1032,256]{1,0:T(8,128)} %collective-permute-done.3.h2), channel_id=1, source_target_pairs={{0,1},{1,0},{2,3},{3,2},{4,5},{5,4},{6,7},{7,6},{8,9},{9,8},{10,11... | collective-permute-start | bytes 3170312 | tf_op jit(solution)/shard_map/ppermute | solution.py:519
  61.9 33.7 %collective-permute-start.12 = (f32[768,256]{1,0:T(8,128)}, f32[768,256]{1,0:T(8,128)}, u32[]{:S(2)}, u32[]{:S(2)}) collective-permute-start(f32[768,256]{1,0:T(8,128)} %collective-permute-done.7.rest_0_), channel_id=1, source_target_pairs={{0,2},{1,3},{2,0},{3,1},{4,6},{5,7},{6,4},{7,5},{8,10},{9,11},{10,... | collective-permute-start | bytes 2359304 | tf_op jit(solution)/shard_map/ppermute | solution.py:519
  63.6 35.4 %collective-permute-start.15 = (f32[768,256]{1,0:T(8,128)}, f32[768,256]{1,0:T(8,128)}, u32[]{:S(2)}, u32[]{:S(2)}) collective-permute-start(f32[768,256]{1,0:T(8,128)} %collective-permute-done.8.rest_4_), channel_id=1, source_target_pairs={{0,2},{1,3},{2,0},{3,1},{4,6},{5,7},{6,4},{7,5},{8,10},{9,11},{10,... | collective-permute-start | bytes 2359304 | tf_op jit(solution)/shard_map/ppermute | solution.py:519
  63.9 35.1 %collective-permute-start.11 = (f32[768,256]{1,0:T(8,128)}, f32[768,256]{1,0:T(8,128)}, u32[]{:S(2)}, u32[]{:S(2)}) collective-permute-start(f32[768,256]{1,0:T(8,128)} %collective-permute-done.7.rest_0_), channel_id=1, source_target_pairs={{0,1},{1,0},{2,3},{3,2},{4,5},{5,4},{6,7},{7,6},{8,9},{9,8},{10,11... | collective-permute-start | bytes 2359304 | tf_op jit(solution)/shard_map/ppermute | solution.py:519
  63.9 35.1 %collective-permute-start.14 = (f32[768,256]{1,0:T(8,128)}, f32[768,256]{1,0:T(8,128)}, u32[]{:S(2)}, u32[]{:S(2)}) collective-permute-start(f32[768,256]{1,0:T(8,128)} %collective-permute-done.8.rest_4_), channel_id=1, source_target_pairs={{0,1},{1,0},{2,3},{3,2},{4,5},{5,4},{6,7},{7,6},{8,9},{9,8},{10,11... | collective-permute-start | bytes 2359304 | tf_op jit(solution)/shard_map/ppermute | solution.py:519
  95.6 3.5 %collective-permute-start.13 = (f32[768,256]{1,0:T(8,128)}, f32[768,256]{1,0:T(8,128)}, u32[]{:S(2)}, u32[]{:S(2)}) collective-permute-start(f32[768,256]{1,0:T(8,128)} %collective-permute-done.12.rest_2_), channel_id=1, source_target_pairs={{0,1},{1,0},{2,3},{3,2},{4,5},{5,4},{6,7},{7,6},{8,9},{9,8},{10,11... | collective-permute-start | bytes 2359304 | tf_op jit(solution)/shard_map/ppermute | solution.py:519
  99.0 2.6 %collective-permute-start.16 = (f32[768,256]{1,0:T(8,128)}, f32[768,256]{1,0:T(8,128)}, u32[]{:S(2)}, u32[]{:S(2)}) collective-permute-start(f32[768,256]{1,0:T(8,128)} %collective-permute-done.15.rest_6_), channel_id=1, source_target_pairs={{0,1},{1,0},{2,3},{3,2},{4,5},{5,4},{6,7},{7,6},{8,9},{9,8},{10,11... | collective-permute-start | bytes 2359304 | tf_op jit(solution)/shard_map/ppermute | solution.py:519
  108.0 14.6 %collective-permute-start.18 = (f32[256,512]{1,0:T(8,128)}, f32[256,512]{1,0:T(8,128)}, u32[]{:S(2)}, u32[]{:S(2)}) collective-permute-start(f32[256,512]{1,0:T(8,128)} %side_windows.1.after1.v0), channel_id=1, source_target_pairs={{0,2},{1,3},{2,0},{3,1},{4,6},{5,7},{6,4},{7,5},{8,10},{9,11},{10,... | collective-permute-start | bytes 1572872 | tf_op jit(solution)/shard_map/ppermute | solution.py:519
  109.8 12.9 %collective-permute-start.17 = (f32[256,512]{1,0:T(8,128)}, f32[256,512]{1,0:T(8,128)}, u32[]{:S(2)}, u32[]{:S(2)}) collective-permute-start(f32[256,512]{1,0:T(8,128)} %side_windows.1.after1.v0), channel_id=1, source_target_pairs={{0,1},{1,0},{2,3},{3,2},{4,5},{5,4},{6,7},{7,6},{8,9},{9,8},{10,11... | collective-permute-start | bytes 1572872 | tf_op jit(solution)/shard_map/ppermute | solution.py:519
  122.6 2.3 %collective-permute-start.19 = (f32[256,512]{1,0:T(8,128)}, f32[256,512]{1,0:T(8,128)}, u32[]{:S(2)}, u32[]{:S(2)}) collective-permute-start(f32[256,512]{1,0:T(8,128)} %collective-permute-done.18.v2), channel_id=1, source_target_pairs={{0,1},{1,0},{2,3},{3,2},{4,5},{5,4},{6,7},{7,6},{8,9},{9,8},{10,11... | collective-permute-start | bytes 1572872 | tf_op jit(solution)/shard_map/ppermute | solution.py:519

commit v5 on v4

--- a/solution.py
+++ b/solution.py
@@ -22,8 +22,9 @@
 AHEAD = 2
 MIDDLE = 30_000_000_000
 
-VMEM_BYTES = 64 * 1024 * 1024
-VMEM_EARLY = 48 * 1024 * 1024
+MIB = 1024 * 1024
+VMEM_BYTES = 64 * MIB
+VMEM_EARLY = 48 * MIB
 
 NN = (((1,), (0,)), ((), ()))
 TN = (((0,), (0,)), ((), ()))
@@ -683,6 +684,7 @@
         *bases,
         part,
         spaces=[anywhere(), in_vmem()],
+        limit=32 * MIB,
     )
     from_prev = gathered(prev_load, "blk", edge_rows)
     from_next = gathered(next_load, "blk", edge_rows)
@@ -714,6 +716,7 @@
             *[from_prev[s] for s in members],
             *[from_next[s] for s in members],
             earlier,
+            limit=24 * MIB,
         )[0]
 
     side = windows((0, 1, 2, 3), "side_windows", edge_rows)
@@ -727,6 +730,7 @@
         work,
         edge_rows,
         side,
+        limit=16 * MIB,
     )
     sides = gathered(side, "blk", edge_rows)
     (coupling_rows,) = call(
@@ -739,6 +743,7 @@
         t_low,
         *sides,
         edge_rows,
+        limit=16 * MIB,
     )
     return (leaf_out, factor_rows, coupling_rows)
 

time: 129 us -> 125 us (0.969)
  Pallas kernels: 86.6 us -> 79.7 us
  local copies, waits for them, and re-layouts: 5.27 us -> 8.73 us
  waiting for transfers between devices: 20 us -> 18.5 us
    pallas_call x8, Pallas kernels: 78.8 us -> 72 us  [call(): pl.pallas_call(kernel, in_specs=ins, out_specs=spaces or [in_vmem()] * le...]
    unnamed x20 -> x38, local copies, waits for them, and re-layouts: 3.18 us -> 6.65 us
  transfers between devices with their start and end apart: 20 -> 20, of which waited for: 11 -> 11; matrix products, arithmetic and copies ran while one was open for 2% -> 2% of each run, Pallas kernels for 59% -> 58%
where the time goes in v5:
time: 125 us; the launch traced here: 124 us
  Pallas kernels  79.7 us (64%)
  waiting for transfers between devices  18.5 us (15%)
  starting transfers between devices  15.7 us (13%)
  local copies, waits for them, and re-layouts  8.73 us (7%)
    pallas_call x8, Pallas kernels, call(): pl.pallas_call(kernel, in_specs=ins, out_specs=spaces or [in_vmem()] * le...  72 us
    ppermute x18, waiting for transfers between devices, swapped(): return lax.ppermute(value, axis, pairs)  17.1 us
    ppermute x18, starting transfers between devices, swapped(): return lax.ppermute(value, axis, pairs)  10.8 us
    pallas_call x1, Pallas kernels, on_device(): pl.pallas_call(left_kernel, grid=(NEAR,), in_specs=[pl.BlockSpec((LEAF, R...  7.74 us
    unnamed x38, local copies, waits for them, and re-layouts  6.65 us
    ppermute x2, starting transfers between devices, shifted(): return lax.ppermute(value, axis, pairs)  4.94 us
  transfers between devices with their start and end apart: 20, of which 11 were waited for; matrix products, arithmetic and copies ran while one was open for 2% of the time, Pallas kernels for 58%

profile of v5, /device:TPU:0, one launch (start us, length us, event | category | flops | bytes accessed | tf_op | source)
XLA Modules:
  0.0 124.4 jit_solution(7247156149430282196)
XLA Ops:
  0.6 0.0 copy-start.11
  0.6 0.0 copy-start.13
  0.7 1.1 slice.8.skel_ref
  1.7 3.0 %collective-permute-start.1 = (f32[512,256]{1,0:T(8,128)S(1)}, f32[512,256]{1,0:T(8,128)S(1)}, u32[]{:S(2)}, u32[]{:S(2)}) collective-permute-start(f32[512,256]{1,0:T(8,128)S(1)} %slice.8.skel_ref), channel_id=1, source_target_pairs={{0,2},{1,3},{2,0},{3,1},{4,6},{5,7},{6,4},{7,5},{8,10},{9,11},{10,... | collective-permute-start | bytes 1572872 | tf_op jit(solution)/shard_map/ppermute | solution.py:520
  4.7 0.0 collective-permute-start
  4.7 0.2 collective-permute-start.6
  4.9 1.0 slice.7
  5.9 0.9 pad_maximum_fusion
  6.8 1.9 %collective-permute-start.7 = (f32[768,256]{1,0:T(8,128)}, f32[768,256]{1,0:T(8,128)}, u32[]{:S(2)}, u32[]{:S(2)}) collective-permute-start(f32[768,256]{1,0:T(8,128)} %pad_maximum_fusion), channel_id=1, source_target_pairs={{0,4},{1,5},{2,6},{3,7},{4,8},{5,9},{6,10},{7,11},{8,12},{9,13},{1... | collective-permute-start | bytes 2359304 | tf_op jit(solution)/shard_map/ppermute | solution.py:526
  8.7 3.0 %collective-permute-start.8 = (f32[768,256]{1,0:T(8,128)}, f32[768,256]{1,0:T(8,128)}, u32[]{:S(2)}, u32[]{:S(2)}) collective-permute-start(f32[768,256]{1,0:T(8,128)} %pad_maximum_fusion), channel_id=1, source_target_pairs={{0,28},{1,29},{2,30},{3,31},{4,0},{5,1},{6,2},{7,3},{8,4},{9,5},{1... | collective-permute-start | bytes 2359304 | tf_op jit(solution)/shard_map/ppermute | solution.py:526
  11.8 3.2 %sibling_products.1 = (bf16[3,256,512]{2,1,0:T(8,128)(2,1)S(1)}, bf16[3,256,512]{2,1,0:T(8,128)(2,1)S(1)}) custom-call(s32[1]{0:T(128)} %bitcast.2.me_ref, s32[1,6]{1,0:T(1,128)S(1)} %copy-done.11, s32[1,5]{1,0:T(1,128)S(1)} %copy-done.13, f32[512,256]{1,0:T(8,128)S(1)} %slice.8.skel_ref, f32[6,512,512]{2,1,0:T(8,128)} %bitcast.11), custom_call_target="tpu_custom_call" | custom-call | flops 1 | bytes 1 | tf_op jit(solution)/shard_map/sibling_products/pallas_call | solution.py:541
  15.0 0.0 copy-start.7
  15.0 0.9 copy-done.7
  15.8 1.7 %collective-permute-done.1.s2 = f32[512,256]{1,0:T(8,128)S(1)} collective-permute-done((f32[512,256]{1,0:T(8,128)S(1)}, f32[512,256]{1,0:T(8,128)S(1)}, u32[]{:S(2)}, u32[]{:S(2)}) %collective-permute-start.1) | collective-permute-done | bytes 524320 | tf_op jit(solution)/shard_map/ppermute | solution.py:520
  17.5 9.2 %leaf_factor.1 = (f32[256,512]{1,0:T(8,128)}, f32[256,256]{1,0:T(8,128)S(1)}) custom-call(f32[512,512]{1,0:T(8,128)S(1)} %bitcast.10, f32[512,512]{1,0:T(8,128)S(1)} %bitcast.9, bf16[3,256,512]{2,1,0:T(8,128)(2,1)S(1)} %get-tuple-element.24.after1.high_hbm), custom_call_target="tpu_custom_call" | custom-call | flops 30000001024 | bytes 1 | tf_op jit(solution)/shard_map/leaf_factor/pallas_call | solution.py:541
  26.8 0.7 copy-done.10
  27.5 0.0 collective-permute-done.s1
  27.5 0.0 collective-permute-done.2.s3
  27.5 0.8 copy-done.17
  28.3 0.8 copy-done.18
  29.1 4.0 %own_window.1.after1.h0 = f32[1032,256]{1,0:T(8,128)} custom-call(s32[1]{0:T(128)} %bitcast.2.me_ref, s32[1,6]{1,0:T(1,128)} %near_ref.5, s32[1,5]{1,0:T(1,128)} %far_ref.5, bf16[3,256,512]{2,1,0:T(8,128)(2,1)} %copy-done.6, bf16[3,256,512]{2,1,0:T(8,128)(2,1)} %copy-done.7, f32[5,256,256]{2,1,0:T(8,128)} %bitcast.5, f32[256,256]{1,0:T(8,128)} %copy-done.10, ...), custom_call_target="tpu_custom_call" | custom-call | flops 1 | bytes 1 | tf_op jit(solution)/shard_map/own_window/pallas_call | solution.py:541
  33.1 0.6 collective-permute-start.4
  33.7 2.4 %collective-permute-start.3 = (f32[1032,256]{1,0:T(8,128)}, f32[1032,256]{1,0:T(8,128)}, u32[]{:S(2)}, u32[]{:S(2)}) collective-permute-start(f32[1032,256]{1,0:T(8,128)} %own_window.1.after1.h0), channel_id=1, source_target_pairs={{0,2},{1,3},{2,0},{3,1},{4,6},{5,7},{6,4},{7,5},{8,10},{9,11},{10,... | collective-permute-start | bytes 3170312 | tf_op jit(solution)/shard_map/ppermute | solution.py:520
  36.1 7.7 %left_products.1 = (bf16[6,256,512]{2,1,0:T(8,128)(2,1)}, bf16[6,256,512]{2,1,0:T(8,128)(2,1)}) custom-call(f32[512,512]{1,0:T(8,128)} %bitcast.8, f32[6,512,512]{2,1,0:T(8,128)} %bitcast.12, f32[1032,256]{1,0:T(8,128)} %own_window.1.after1.h0), custom_call_target="tpu_custom_call" | custom-call | flops 1 | bytes 1 | tf_op jit(solution)/shard_map/left_products/pallas_call | solution.py:626
  43.8 0.0 collective-permute-start.5
  43.8 1.5 %collective-permute-done.8.rest_4_ = f32[768,256]{1,0:T(8,128)} collective-permute-done((f32[768,256]{1,0:T(8,128)}, f32[768,256]{1,0:T(8,128)}, u32[]{:S(2)}, u32[]{:S(2)}) %collective-permute-start.8) | collective-permute-done | bytes 786464 | tf_op jit(solution)/shard_map/ppermute | solution.py:526
  45.3 0.0 collective-permute-done.6.p2
  45.3 1.5 %collective-permute-done.5.p1 = f32[256,1024]{1,0:T(8,128)} collective-permute-done((f32[256,1024]{1,0:T(8,128)}, f32[256,1024]{1,0:T(8,128)}, u32[]{:S(2)}, u32[]{:S(2)}) %collective-permute-start.5) | collective-permute-done | bytes 1048608 | tf_op jit(solution)/shard_map/ppermute | solution.py:520
  46.8 1.5 %collective-permute-done.9.p3 = f32[256,1024]{1,0:T(8,128)} collective-permute-done((f32[256,1024]{1,0:T(8,128)}, f32[256,1024]{1,0:T(8,128)}, u32[]{:S(2)}, u32[]{:S(2)}) %collective-permute-start.9) | collective-permute-done | bytes 1048608 | tf_op jit(solution)/shard_map/ppermute | solution.py:520
  48.3 11.5 %chip_sums.1 = (bf16[256,1024]{1,0:T(8,128)(2,1)}, bf16[256,1024]{1,0:T(8,128)(2,1)}, f32[1024,1024]{1,0:T(8,128)}) custom-call(s32[1]{0:T(128)} %bitcast.2.me_ref, f32[1032,256]{1,0:T(8,128)} %own_window.1.after1.h0, f32[1032,256]{1,0:T(8,128)} %collective-permute-done.4.h1, f32[256,1024]{1,0:T(8,128)} %p0.3, f32[256,1024]{1,0:T(8,128)} %collective-permute-done.5.p1, ...), custom_call_target="tpu_custom_call" | custom-call | flops 1 | bytes 1 | tf_op jit(solution)/shard_map/chip_sums/pallas_call | solution.py:541
  59.9 2.0 %collective-permute-done.3.h2 = f32[1032,256]{1,0:T(8,128)} collective-permute-done((f32[1032,256]{1,0:T(8,128)}, f32[1032,256]{1,0:T(8,128)}, u32[]{:S(2)}, u32[]{:S(2)}) %collective-permute-start.3) | collective-permute-done | bytes 1056800 | tf_op jit(solution)/shard_map/ppermute | solution.py:520
  61.9 1.8 %collective-permute-start.12 = (f32[768,256]{1,0:T(8,128)}, f32[768,256]{1,0:T(8,128)S(1)}, u32[]{:S(2)}, u32[]{:S(2)}) collective-permute-start(f32[768,256]{1,0:T(8,128)} %collective-permute-done.7.rest_0_), channel_id=1, source_target_pairs={{0,2},{1,3},{2,0},{3,1},{4,6},{5,7},{6,4},{7,5},{8,10},{9,11},{10,... | collective-permute-start | bytes 2359304 | tf_op jit(solution)/shard_map/ppermute | solution.py:520
  63.7 0.3 collective-permute-start.15
  64.0 0.5 collective-permute-start.14
  64.5 0.3 collective-permute-done.10.h3
  64.8 1.2 copy-done.1
  66.0 2.2 %copy-done.3 = f32[1024,1024]{1,0:T(8,128)S(1)} copy-done((f32[1024,1024]{1,0:T(8,128)S(1)}, f32[1024,1024]{1,0:T(8,128)}, u32[]{:S(2)}) %copy-start.3) | copy-done | bytes 4194328
  68.2 28.5 %parent_factor.1 = (f32[768,1280]{1,0:T(8,128)S(1)}, f32[256,256]{1,0:T(8,128)S(1)}) custom-call(s32[1]{0:T(128)} %bitcast.2.me_ref, f32[1032,256]{1,0:T(8,128)} %collective-permute-done.3.h2, f32[1032,256]{1,0:T(8,128)S(1)} %collective-permute-done.10.h3, f32[256,1024]{1,0:T(8,128)S(1)} %copy-done.1, f32[256,1024]{1,0:T(8,128)} %collective-permute-done.5.p1, ...), custom_call_target="tpu_custom_call" | custom-call | flops 1 | bytes 1 | tf_op jit(solution)/shard_map/parent_factor/pallas_call | solution.py:541
  96.7 0.2 collective-permute-start.13
  96.9 2.0 %collective-permute-done.15.rest_6_ = f32[768,256]{1,0:T(8,128)S(1)} collective-permute-done((f32[768,256]{1,0:T(8,128)}, f32[768,256]{1,0:T(8,128)S(1)}, u32[]{:S(2)}, u32[]{:S(2)}) %collective-permute-start.15) | collective-permute-done | bytes 786464 | tf_op jit(solution)/shard_map/ppermute | solution.py:520
  98.9 0.1 collective-permute-done.13.rest_3_
  99.0 2.2 %collective-permute-done.16.rest_7_ = f32[768,256]{1,0:T(8,128)S(1)} collective-permute-done((f32[768,256]{1,0:T(8,128)S(1)}, f32[768,256]{1,0:T(8,128)S(1)}, u32[]{:S(2)}, u32[]{:S(2)}) %collective-permute-start.16) | collective-permute-done | bytes 786464 | tf_op jit(solution)/shard_map/ppermute | solution.py:520
  101.2 5.3 %side_windows.1.after1.v0 = f32[256,512]{1,0:T(8,128)S(1)} custom-call(s32[1]{0:T(128)} %bitcast.2.me_ref, s32[1,6]{1,0:T(1,128)S(1)} %copy-done.12, s32[1,5]{1,0:T(1,128)S(1)} %copy-done.14, bf16[6,256,512]{2,1,0:T(8,128)(2,1)S(1)} %copy-done, bf16[6,256,512]{2,1,0:T(8,128)(2,1)S(1)} %copy-done.5, f32[5,256,256]{2,1,0:T(8,128)S(1)} %bitcast.6, ...), custom_call_target="tpu_custom_call" | custom-call | flops 1 | bytes 1 | tf_op jit(solution)/shard_map/side_windows/pallas_call | solution.py:541
  106.6 1.8 %collective-permute-start.18 = (f32[256,512]{1,0:T(8,128)S(1)}, f32[256,512]{1,0:T(8,128)S(1)}, u32[]{:S(2)}, u32[]{:S(2)}) collective-permute-start(f32[256,512]{1,0:T(8,128)S(1)} %side_windows.1.after1.v0), channel_id=1, source_target_pairs={{0,2},{1,3},{2,0},{3,1},{4,6},{5,7},{6,4},{7,5},{8,10},{9,11},{10,... | collective-permute-start | bytes 1572872 | tf_op jit(solution)/shard_map/ppermute | solution.py:520
  108.4 8.3 %parent_finish.1 = (f32[256,768]{1,0:T(8,128)}, f32[256,256]{1,0:T(8,128)S(1)}) custom-call(s32[1]{0:T(128)} %bitcast.2.me_ref, f32[768,1280]{1,0:T(8,128)S(1)} %get-tuple-element.33.work_hbm, f32[256,256]{1,0:T(8,128)S(1)} %get-tuple-element.34.rest_8_.edge_in, f32[256,512]{1,0:T(8,128)S(1)} %side_windows.1.after1.v0), custom_call_target="tpu_custom_call" | custom-call | flops 1 | bytes 1 | tf_op jit(solution)/shard_map/parent_finish/pallas_call | solution.py:541
  116.8 3.9 %collective-permute-done.18.v2 = f32[256,512]{1,0:T(8,128)S(1)} collective-permute-done((f32[256,512]{1,0:T(8,128)S(1)}, f32[256,512]{1,0:T(8,128)S(1)}, u32[]{:S(2)}, u32[]{:S(2)}) %collective-permute-start.18) | collective-permute-done | bytes 524320 | tf_op jit(solution)/shard_map/ppermute | solution.py:520
  120.6 1.9 %collective-permute-done.19.v3 = f32[256,512]{1,0:T(8,128)S(1)} collective-permute-done((f32[256,512]{1,0:T(8,128)S(1)}, f32[256,512]{1,0:T(8,128)S(1)}, u32[]{:S(2)}, u32[]{:S(2)}) %collective-permute-start.19) | collective-permute-done | bytes 524320 | tf_op jit(solution)/shard_map/ppermute | solution.py:520
  122.5 1.9 %coupling.1 = f32[256,768]{1,0:T(8,128)} custom-call(bf16[256,1024]{1,0:T(8,128)(2,1)S(1)} %copy-done.8, bf16[256,1024]{1,0:T(8,128)(2,1)S(1)} %copy-done.9, f32[256,512]{1,0:T(8,128)S(1)} %side_windows.1.after1.v0, f32[256,512]{1,0:T(8,128)S(1)} %collective-permute-done.17.v1, f32[256,512]{1,0:T(8,128)S(1)} %collective-permute-done.18.v2, ...), custom_call_target="tpu_custom_call" | custom-call | flops 1 | bytes 1 | tf_op jit(solution)/shard_map/coupling/pallas_call | solution.py:541
  (42 shorter events, 0.1 us)
Async XLA Ops:
  0.6 11.2 %copy-start.11 = (s32[1,6]{1,0:T(1,128)S(1)}, s32[1,6]{1,0:T(1,128)}, u32[]{:S(2)}) copy-start(s32[1,6]{1,0:T(1,128)} %near_ref.5) | copy-start | bytes 76
  0.6 11.1 %copy-start.13 = (s32[1,5]{1,0:T(1,128)S(1)}, s32[1,5]{1,0:T(1,128)}, u32[]{:S(2)}) copy-start(s32[1,5]{1,0:T(1,128)} %far_ref.5) | copy-start | bytes 64
  1.7 15.8 %collective-permute-start.1 = (f32[512,256]{1,0:T(8,128)S(1)}, f32[512,256]{1,0:T(8,128)S(1)}, u32[]{:S(2)}, u32[]{:S(2)}) collective-permute-start(f32[512,256]{1,0:T(8,128)S(1)} %slice.8.skel_ref), channel_id=1, source_target_pairs={{0,2},{1,3},{2,0},{3,1},{4,6},{5,7},{6,4},{7,5},{8,10},{9,11},{10,... | collective-permute-start | bytes 1572872 | tf_op jit(solution)/shard_map/ppermute | solution.py:520
  4.7 22.7 %collective-permute-start = (f32[512,256]{1,0:T(8,128)S(1)}, f32[512,256]{1,0:T(8,128)S(1)}, u32[]{:S(2)}, u32[]{:S(2)}) collective-permute-start(f32[512,256]{1,0:T(8,128)S(1)} %slice.8.skel_ref), channel_id=1, source_target_pairs={{0,1},{1,0},{2,3},{3,2},{4,5},{5,4},{6,7},{7,6},{8,9},{9,8},{10,11... | collective-permute-start | bytes 1572872 | tf_op jit(solution)/shard_map/ppermute | solution.py:520
  4.7 40.6 %collective-permute-start.6 = (f32[256,1024]{1,0:T(8,128)}, f32[256,1024]{1,0:T(8,128)}, u32[]{:S(2)}, u32[]{:S(2)}) collective-permute-start(f32[256,1024]{1,0:T(8,128)} %p0.3), channel_id=1, source_target_pairs={{0,2},{1,3},{2,0},{3,1},{4,6},{5,7},{6,4},{7,5},{8,10},{9,11},{10,... | collective-permute-start | bytes 3145736 | tf_op jit(solution)/shard_map/ppermute | solution.py:520
  6.8 37.0 %collective-permute-start.7 = (f32[768,256]{1,0:T(8,128)}, f32[768,256]{1,0:T(8,128)}, u32[]{:S(2)}, u32[]{:S(2)}) collective-permute-start(f32[768,256]{1,0:T(8,128)} %pad_maximum_fusion), channel_id=1, source_target_pairs={{0,4},{1,5},{2,6},{3,7},{4,8},{5,9},{6,10},{7,11},{8,12},{9,13},{1... | collective-permute-start | bytes 2359304 | tf_op jit(solution)/shard_map/ppermute | solution.py:526
  8.7 36.6 %collective-permute-start.8 = (f32[768,256]{1,0:T(8,128)}, f32[768,256]{1,0:T(8,128)}, u32[]{:S(2)}, u32[]{:S(2)}) collective-permute-start(f32[768,256]{1,0:T(8,128)} %pad_maximum_fusion), channel_id=1, source_target_pairs={{0,28},{1,29},{2,30},{3,31},{4,0},{5,1},{6,2},{7,3},{8,4},{9,5},{1... | collective-permute-start | bytes 2359304 | tf_op jit(solution)/shard_map/ppermute | solution.py:526
  11.8 5.7 %copy-start.4 = (f32[1,512,512]{2,1,0:T(8,128)S(1)}, f32[1,512,512]{2,1,0:T(8,128)}, u32[]{:S(2)}) copy-start(f32[1,512,512]{2,1,0:T(8,128)} %param.10) | copy-start | bytes 3145732
  11.8 5.7 %copy-start.15 = (f32[1,512,512]{2,1,0:T(8,128)S(1)}, f32[1,512,512]{2,1,0:T(8,128)}, u32[]{:S(2)}) copy-start(f32[1,512,512]{2,1,0:T(8,128)} %param.7) | copy-start | bytes 3145732
  15.0 0.9 copy-start.7
  15.8 10.9 %copy-start.6 = (bf16[3,256,512]{2,1,0:T(8,128)(2,1)}, bf16[3,256,512]{2,1,0:T(8,128)(2,1)S(1)}, u32[]{:S(2)}) copy-start(bf16[3,256,512]{2,1,0:T(8,128)(2,1)S(1)} %get-tuple-element.24.after1.high_hbm) | copy-start | bytes 2359300
  17.5 9.3 %copy-start.16 = (f32[512,256]{1,0:T(8,128)}, f32[512,256]{1,0:T(8,128)S(1)}, u32[]{:S(2)}) copy-start(f32[512,256]{1,0:T(8,128)S(1)} %collective-permute-done.1.s2) | copy-start | bytes 1572868
  17.5 10.0 %collective-permute-start.2 = (f32[512,256]{1,0:T(8,128)S(1)}, f32[512,256]{1,0:T(8,128)S(1)}, u32[]{:S(2)}, u32[]{:S(2)}) collective-permute-start(f32[512,256]{1,0:T(8,128)S(1)} %collective-permute-done.1.s2), channel_id=1, source_target_pairs={{0,1},{1,0},{2,3},{3,2},{4,5},{5,4},{6,7},{7,6},{8,9},{9,8},{10,11... | collective-permute-start | bytes 1572872 | tf_op jit(solution)/shard_map/ppermute | solution.py:520
  26.8 0.7 copy-start.10
  27.5 0.8 copy-start.17
  28.3 0.8 copy-start.18
  33.1 15.2 %collective-permute-start.4 = (f32[1032,256]{1,0:T(8,128)}, f32[1032,256]{1,0:T(8,128)}, u32[]{:S(2)}, u32[]{:S(2)}) collective-permute-start(f32[1032,256]{1,0:T(8,128)} %own_window.1.after1.h0), channel_id=1, source_target_pairs={{0,1},{1,0},{2,3},{3,2},{4,5},{5,4},{6,7},{7,6},{8,9},{9,8},{10,11... | collective-permute-start | bytes 3170312 | tf_op jit(solution)/shard_map/ppermute | solution.py:520
  33.7 28.2 %collective-permute-start.3 = (f32[1032,256]{1,0:T(8,128)}, f32[1032,256]{1,0:T(8,128)}, u32[]{:S(2)}, u32[]{:S(2)}) collective-permute-start(f32[1032,256]{1,0:T(8,128)} %own_window.1.after1.h0), channel_id=1, source_target_pairs={{0,2},{1,3},{2,0},{3,1},{4,6},{5,7},{6,4},{7,5},{8,10},{9,11},{10,... | collective-permute-start | bytes 3170312 | tf_op jit(solution)/shard_map/ppermute | solution.py:520
  43.8 3.0 %collective-permute-start.5 = (f32[256,1024]{1,0:T(8,128)}, f32[256,1024]{1,0:T(8,128)}, u32[]{:S(2)}, u32[]{:S(2)}) collective-permute-start(f32[256,1024]{1,0:T(8,128)} %p0.3), channel_id=1, source_target_pairs={{0,1},{1,0},{2,3},{3,2},{4,5},{5,4},{6,7},{7,6},{8,9},{9,8},{10,11... | collective-permute-start | bytes 3145736 | tf_op jit(solution)/shard_map/ppermute | solution.py:520
  45.3 3.0 %collective-permute-start.9 = (f32[256,1024]{1,0:T(8,128)}, f32[256,1024]{1,0:T(8,128)}, u32[]{:S(2)}, u32[]{:S(2)}) collective-permute-start(f32[256,1024]{1,0:T(8,128)} %collective-permute-done.6.p2), channel_id=1, source_target_pairs={{0,1},{1,0},{2,3},{3,2},{4,5},{5,4},{6,7},{7,6},{8,9},{9,8},{10,11... | collective-permute-start | bytes 3145736 | tf_op jit(solution)/shard_map/ppermute | solution.py:520
  61.9 39.3 %copy-start.12 = (s32[1,6]{1,0:T(1,128)S(1)}, s32[1,6]{1,0:T(1,128)}, u32[]{:S(2)}) copy-start(s32[1,6]{1,0:T(1,128)} %near_ref.5) | copy-start | bytes 76
  61.9 39.3 %copy-start.14 = (s32[1,5]{1,0:T(1,128)S(1)}, s32[1,5]{1,0:T(1,128)}, u32[]{:S(2)}) copy-start(s32[1,5]{1,0:T(1,128)} %far_ref.5) | copy-start | bytes 64
  61.9 39.3 %copy-start = (bf16[6,256,512]{2,1,0:T(8,128)(2,1)S(1)}, bf16[6,256,512]{2,1,0:T(8,128)(2,1)}, u32[]{:S(2)}) copy-start(bf16[6,256,512]{2,1,0:T(8,128)(2,1)} %get-tuple-element.28.after1.high_hbm) | copy-start | bytes 4718596
  61.9 2.9 %collective-permute-start.10 = (f32[1032,256]{1,0:T(8,128)}, f32[1032,256]{1,0:T(8,128)S(1)}, u32[]{:S(2)}, u32[]{:S(2)}) collective-permute-start(f32[1032,256]{1,0:T(8,128)} %collective-permute-done.3.h2), channel_id=1, source_target_pairs={{0,1},{1,0},{2,3},{3,2},{4,5},{5,4},{6,7},{7,6},{8,9},{9,8},{10,11... | collective-permute-start | bytes 3170312 | tf_op jit(solution)/shard_map/ppermute | solution.py:520
  61.9 34.8 %collective-permute-start.12 = (f32[768,256]{1,0:T(8,128)}, f32[768,256]{1,0:T(8,128)S(1)}, u32[]{:S(2)}, u32[]{:S(2)}) collective-permute-start(f32[768,256]{1,0:T(8,128)} %collective-permute-done.7.rest_0_), channel_id=1, source_target_pairs={{0,2},{1,3},{2,0},{3,1},{4,6},{5,7},{6,4},{7,5},{8,10},{9,11},{10,... | collective-permute-start | bytes 2359304 | tf_op jit(solution)/shard_map/ppermute | solution.py:520
  63.7 35.2 %collective-permute-start.15 = (f32[768,256]{1,0:T(8,128)}, f32[768,256]{1,0:T(8,128)S(1)}, u32[]{:S(2)}, u32[]{:S(2)}) collective-permute-start(f32[768,256]{1,0:T(8,128)} %collective-permute-done.8.rest_4_), channel_id=1, source_target_pairs={{0,2},{1,3},{2,0},{3,1},{4,6},{5,7},{6,4},{7,5},{8,10},{9,11},{10,... | collective-permute-start | bytes 2359304 | tf_op jit(solution)/shard_map/ppermute | solution.py:520
  64.0 34.9 %collective-permute-start.11 = (f32[768,256]{1,0:T(8,128)}, f32[768,256]{1,0:T(8,128)S(1)}, u32[]{:S(2)}, u32[]{:S(2)}) collective-permute-start(f32[768,256]{1,0:T(8,128)} %collective-permute-done.7.rest_0_), channel_id=1, source_target_pairs={{0,1},{1,0},{2,3},{3,2},{4,5},{5,4},{6,7},{7,6},{8,9},{9,8},{10,11... | collective-permute-start | bytes 2359304 | tf_op jit(solution)/shard_map/ppermute | solution.py:520
  64.0 34.9 %collective-permute-start.14 = (f32[768,256]{1,0:T(8,128)}, f32[768,256]{1,0:T(8,128)S(1)}, u32[]{:S(2)}, u32[]{:S(2)}) collective-permute-start(f32[768,256]{1,0:T(8,128)} %collective-permute-done.8.rest_4_), channel_id=1, source_target_pairs={{0,1},{1,0},{2,3},{3,2},{4,5},{5,4},{6,7},{7,6},{8,9},{9,8},{10,11... | collective-permute-start | bytes 2359304 | tf_op jit(solution)/shard_map/ppermute | solution.py:520
  64.8 1.2 copy-start.1
  66.0 2.2 %copy-start.3 = (f32[1024,1024]{1,0:T(8,128)S(1)}, f32[1024,1024]{1,0:T(8,128)}, u32[]{:S(2)}) copy-start(f32[1024,1024]{1,0:T(8,128)} %get-tuple-element.31.part_hbm) | copy-start | bytes 12582916
  68.2 33.0 %copy-start.2 = (f32[1,5,256,256]{3,2,1,0:T(8,128)S(1)}, f32[1,5,256,256]{3,2,1,0:T(8,128)}, u32[]{:S(2)}) copy-start(f32[1,5,256,256]{3,2,1,0:T(8,128)} %param.9) | copy-start | bytes 3932164
  68.2 33.0 %copy-start.5 = (bf16[6,256,512]{2,1,0:T(8,128)(2,1)S(1)}, bf16[6,256,512]{2,1,0:T(8,128)(2,1)}, u32[]{:S(2)}) copy-start(bf16[6,256,512]{2,1,0:T(8,128)(2,1)} %get-tuple-element.35.low_hbm) | copy-start | bytes 4718596
  96.7 2.4 %collective-permute-start.13 = (f32[768,256]{1,0:T(8,128)S(1)}, f32[768,256]{1,0:T(8,128)S(1)}, u32[]{:S(2)}, u32[]{:S(2)}) collective-permute-start(f32[768,256]{1,0:T(8,128)S(1)} %collective-permute-done.12.rest_2_), channel_id=1, source_target_pairs={{0,1},{1,0},{2,3},{3,2},{4,5},{5,4},{6,7},{7,6},{8,9},{9,8},{10,11... | collective-permute-start | bytes 2359304 | tf_op jit(solution)/shard_map/ppermute | solution.py:520
  98.9 2.3 %collective-permute-start.16 = (f32[768,256]{1,0:T(8,128)S(1)}, f32[768,256]{1,0:T(8,128)S(1)}, u32[]{:S(2)}, u32[]{:S(2)}) collective-permute-start(f32[768,256]{1,0:T(8,128)S(1)} %collective-permute-done.15.rest_6_), channel_id=1, source_target_pairs={{0,1},{1,0},{2,3},{3,2},{4,5},{5,4},{6,7},{7,6},{8,9},{9,8},{10,11... | collective-permute-start | bytes 2359304 | tf_op jit(solution)/shard_map/ppermute | solution.py:520
  106.6 14.0 %collective-permute-start.18 = (f32[256,512]{1,0:T(8,128)S(1)}, f32[256,512]{1,0:T(8,128)S(1)}, u32[]{:S(2)}, u32[]{:S(2)}) collective-permute-start(f32[256,512]{1,0:T(8,128)S(1)} %side_windows.1.after1.v0), channel_id=1, source_target_pairs={{0,2},{1,3},{2,0},{3,1},{4,6},{5,7},{6,4},{7,5},{8,10},{9,11},{10,... | collective-permute-start | bytes 1572872 | tf_op jit(solution)/shard_map/ppermute | solution.py:520
  108.4 12.2 %collective-permute-start.17 = (f32[256,512]{1,0:T(8,128)S(1)}, f32[256,512]{1,0:T(8,128)S(1)}, u32[]{:S(2)}, u32[]{:S(2)}) collective-permute-start(f32[256,512]{1,0:T(8,128)S(1)} %side_windows.1.after1.v0), channel_id=1, source_target_pairs={{0,1},{1,0},{2,3},{3,2},{4,5},{5,4},{6,7},{7,6},{8,9},{9,8},{10,11... | collective-permute-start | bytes 1572872 | tf_op jit(solution)/shard_map/ppermute | solution.py:520
  108.4 14.1 %copy-start.8 = (bf16[256,1024]{1,0:T(8,128)(2,1)S(1)}, bf16[256,1024]{1,0:T(8,128)(2,1)}, u32[]{:S(2)}) copy-start(bf16[256,1024]{1,0:T(8,128)(2,1)} %get-tuple-element.41.t_high) | copy-start | bytes 1572868
  108.4 14.1 %copy-start.9 = (bf16[256,1024]{1,0:T(8,128)(2,1)S(1)}, bf16[256,1024]{1,0:T(8,128)(2,1)}, u32[]{:S(2)}) copy-start(bf16[256,1024]{1,0:T(8,128)(2,1)} %get-tuple-element.42.t_low) | copy-start | bytes 1572868
  120.6 1.9 %collective-permute-start.19 = (f32[256,512]{1,0:T(8,128)S(1)}, f32[256,512]{1,0:T(8,128)S(1)}, u32[]{:S(2)}, u32[]{:S(2)}) collective-permute-start(f32[256,512]{1,0:T(8,128)S(1)} %collective-permute-done.18.v2), channel_id=1, source_target_pairs={{0,1},{1,0},{2,3},{3,2},{4,5},{5,4},{6,7},{7,6},{8,9},{9,8},{10,11... | collective-permute-start | bytes 1572872 | tf_op jit(solution)/shard_map/ppermute | solution.py:520

commit v6 on v5

--- a/solution.py
+++ b/solution.py
@@ -294,31 +294,29 @@
     own_copy.wait()
 
 
-def side_kernel(blocks, members, me_ref, near_ref, far_ref, high_hbm, low_hbm, far_hbm, *rest):
-    count = len(members)
-    zs, (earlier, out_ref, z_held, high_held, low_held, far_held, h_high, h_low, s_high, s_low, sems) = (
-        rest[: 2 * count],
-        rest[2 * count :],
+def side_kernel(blocks, shift, me_ref, near_ref, far_ref, high_hbm, low_hbm, far_hbm, *rest):
+    count = GROUP
+    zs, (after1, out_ref, z_held, high_held, low_held, far_held, h_high, h_low, s_high, s_low, sems) = (
+        rest[:count],
+        rest[count:],
     )
     slots = []
     z_copies = []
     near_copies = []
     far_copies = []
-    for side, shift in enumerate((blocks - GROUP, GROUP)):
-        for place, s in enumerate(members):
-            n = side * count + place
-            leaf = lax.rem(jnp.bitwise_xor(me_ref[0], s) + shift, blocks)
-            slot, m, f = source_of(leaf, near_ref, far_ref)
-            slots.append(slot)
-            z_copies.append(pltpu.make_async_copy(zs[n], z_held.at[n], sems.at[0, n]))
-            near_copies.append(
-                [
-                    pltpu.make_async_copy(high_hbm.at[m], high_held.at[n], sems.at[1, n]),
-                    pltpu.make_async_copy(low_hbm.at[m], low_held.at[n], sems.at[2, n]),
-                ]
-            )
-            far_copies.append(pltpu.make_async_copy(far_hbm.at[f], far_held.at[n], sems.at[1, n]))
-    for n in range(2 * count):
+    for n in range(count):
+        leaf = lax.rem(jnp.bitwise_xor(me_ref[0], n) + shift, blocks)
+        slot, m, f = source_of(leaf, near_ref, far_ref)
+        slots.append(slot)
+        z_copies.append(pltpu.make_async_copy(zs[n], z_held.at[n], sems.at[0, n]))
+        near_copies.append(
+            [
+                pltpu.make_async_copy(high_hbm.at[m], high_held.at[n], sems.at[1, n]),
+                pltpu.make_async_copy(low_hbm.at[m], low_held.at[n], sems.at[2, n]),
+            ]
+        )
+        far_copies.append(pltpu.make_async_copy(far_hbm.at[f], far_held.at[n], sems.at[1, n]))
+    for n in range(count):
         z_copies[n].start()
 
         @pl.when(slots[n] < NEAR)
@@ -330,33 +328,29 @@
         def _(n=n):
             far_copies[n].start()
 
-    for side in range(2):
-        for place in range(count):
-            n = side * count + place
-            cols = slice(place * RANK, (place + 1) * RANK)
-            z_copies[n].wait()
-
-            @pl.when(slots[n] < NEAR)
-            def _(n=n, cols=cols):
-                for copy in near_copies[n]:
-                    copy.wait()
-                high, low = split(dot3((high_held[n], low_held[n]), split(z_held[n, :LEAF, :])))
-                h_high[:, cols] = high
-                h_low[:, cols] = low
-
-            @pl.when(slots[n] >= NEAR)
-            def _(n=n, cols=cols):
-                far_copies[n].wait()
-                high, low = split(far_held[n])
-                h_high[:, cols] = high
-                h_low[:, cols] = low
-
-            high, low = split(z_held[n, LEAF:, :])
-            s_high[cols, :] = high
-            s_low[cols, :] = low
-        half = slice(side * RANK, (side + 1) * RANK)
-        total = dot3((h_high[...], h_low[...]), (s_high[...], s_low[...]))
-        out_ref[:, half] = total
+    for n in range(count):
+        cols = block_rows(n)
+        z_copies[n].wait()
+
+        @pl.when(slots[n] < NEAR)
+        def _(n=n, cols=cols):
+            for copy in near_copies[n]:
+                copy.wait()
+            high, low = split(dot3((high_held[n], low_held[n]), split(z_held[n, :LEAF, :])))
+            h_high[:, cols] = high
+            h_low[:, cols] = low
+
+        @pl.when(slots[n] >= NEAR)
+        def _(n=n, cols=cols):
+            far_copies[n].wait()
+            high, low = split(far_held[n])
+            h_high[:, cols] = high
+            h_low[:, cols] = low
+
+        high, low = split(z_held[n, LEAF:, :])
+        s_high[cols, :] = high
+        s_low[cols, :] = low
+    out_ref[...] = dot3((h_high[...], h_low[...]), (s_high[...], s_low[...]))
 
 
 def partial_sums(p_high, p_low, h_refs, first, v_high, v_low):
@@ -505,14 +499,18 @@
         edge_ref[...] = edge_in[...] - product
 
 
-def couple_kernel(t_high, t_low, v0, v1, v2, v3, edge_ref, out_ref):
-    total = jnp.zeros((RANK, 2 * RANK), jnp.float32)
-    for s, v_ref in enumerate((v0, v1, v2, v3)):
-        cols = block_rows(s)
-        total = total + dot3((t_high[:, cols], t_low[:, cols]), split(v_ref[...]))
-    out_ref[:, :RANK] = total[:, :RANK]
+def couple_kernel(t_high, t_low, *rest):
+    sides, (edge_ref, out_ref) = rest[: 2 * GROUP], rest[2 * GROUP :]
     out_ref[:, RANK : 2 * RANK] = edge_ref[...]
-    out_ref[:, 2 * RANK :] = total[:, RANK:]
+    for side in range(2):
+        total = jnp.zeros((RANK, RANK), jnp.float32)
+        for s in range(GROUP):
+            cols = block_rows(s)
+            total = total + dot3(
+                (t_high[:, cols], t_low[:, cols]), split(sides[side * GROUP + s][...])
+            )
+        start = 2 * side * RANK
+        out_ref[:, start : start + RANK] = total
 
 
 def swapped(value, axis, mask):
@@ -689,23 +687,22 @@
     from_prev = gathered(prev_load, "blk", edge_rows)
     from_next = gathered(next_load, "blk", edge_rows)
 
-    def windows(members, name, earlier):
-        count = len(members)
+    def windows(shift, name, loads, earlier):
         return call(
-            functools.partial(side_kernel, blocks, members),
+            functools.partial(side_kernel, blocks, shift),
             name,
-            [in_smem()] * 3 + [anywhere()] * (4 + 2 * count),
-            [((RANK, 2 * RANK), f32)],
+            [in_smem()] * 3 + [anywhere()] * (GROUP + 4),
+            [((RANK, RANK), f32)],
             [
-                pltpu.VMEM((2 * count, LEAF + RANK, RANK), f32),
-                pltpu.VMEM((2 * count, RANK, LEAF), b16),
-                pltpu.VMEM((2 * count, RANK, LEAF), b16),
-                pltpu.VMEM((2 * count, RANK, RANK), f32),
-                pltpu.VMEM((RANK, count * RANK), b16),
-                pltpu.VMEM((RANK, count * RANK), b16),
-                pltpu.VMEM((count * RANK, RANK), b16),
-                pltpu.VMEM((count * RANK, RANK), b16),
-                dma((3, 2 * count)),
+                pltpu.VMEM((GROUP, LEAF + RANK, RANK), f32),
+                pltpu.VMEM((GROUP, RANK, LEAF), b16),
+                pltpu.VMEM((GROUP, RANK, LEAF), b16),
+                pltpu.VMEM((GROUP, RANK, RANK), f32),
+                pltpu.VMEM((RANK, PAR), b16),
+                pltpu.VMEM((RANK, PAR), b16),
+                pltpu.VMEM((PAR, RANK), b16),
+                pltpu.VMEM((PAR, RANK), b16),
+                dma((3, GROUP)),
             ],
             me,
             near_index,
@@ -713,13 +710,13 @@
             left_high,
             left_low,
             far,
-            *[from_prev[s] for s in members],
-            *[from_next[s] for s in members],
+            *loads,
             earlier,
             limit=24 * MIB,
         )[0]
 
-    side = windows((0, 1, 2, 3), "side_windows", edge_rows)
+    prev_side = windows(blocks - GROUP, "prev_windows", from_prev, edge_rows)
+    next_side = windows(GROUP, "next_windows", from_next, prev_side)
     factor_rows, edge_rows = call(
         finish_kernel,
         "parent_finish",
@@ -729,19 +726,21 @@
         me,
         work,
         edge_rows,
-        side,
+        next_side,
         limit=16 * MIB,
     )
-    sides = gathered(side, "blk", edge_rows)
+    prev_sides = gathered(prev_side, "blk", edge_rows)
+    next_sides = gathered(next_side, "blk", edge_rows)
     (coupling_rows,) = call(
         couple_kernel,
         "coupling",
-        [in_vmem()] * 7,
+        [in_vmem()] * 11,
         [((RANK, 3 * RANK), f32)],
         [],
         t_high,
         t_low,
-        *sides,
+        *prev_sides,
+        *next_sides,
         edge_rows,
         limit=16 * MIB,
     )

time: 125 us -> 122 us (0.976)
  waiting for transfers between devices: 18.5 us -> 12.8 us
  starting transfers between devices: 15.7 us -> 17 us
  Pallas kernels: 79.7 us -> 81 us
    ppermute x18 -> x21, waiting for transfers between devices: 17.1 us -> 11 us  [swapped(): return lax.ppermute(value, axis, pairs)]
    pallas_call x8 -> x9, Pallas kernels: 72 us -> 73.3 us  [call(): pl.pallas_call(kernel, in_specs=ins, out_specs=spaces or [in_vmem()] * le...]
    ppermute x18 -> x21, starting transfers between devices: 10.8 us -> 12.1 us  [swapped(): return lax.ppermute(value, axis, pairs)]
  transfers between devices with their start and end apart: 20 -> 23, of which waited for: 11 -> 9; matrix products, arithmetic and copies ran while one was open for 2% -> 2% of each run, Pallas kernels for 58% -> 65%
where the time goes in v6:
time: 122 us; the launch traced here: 121 us
  Pallas kernels  81 us (66%)
  starting transfers between devices  17 us (14%)
  waiting for transfers between devices  12.8 us (10%)
  local copies, waits for them, and re-layouts  8.75 us (7%)
    pallas_call x9, Pallas kernels, call(): pl.pallas_call(kernel, in_specs=ins, out_specs=spaces or [in_vmem()] * le...  73.3 us
    ppermute x21, starting transfers between devices, swapped(): return lax.ppermute(value, axis, pairs)  12.1 us
    ppermute x21, waiting for transfers between devices, swapped(): return lax.ppermute(value, axis, pairs)  11 us
    pallas_call x1, Pallas kernels, on_device(): pl.pallas_call(left_kernel, grid=(NEAR,), in_specs=[pl.BlockSpec((LEAF, R...  7.71 us
    unnamed x38, local copies, waits for them, and re-layouts  6.66 us
    ppermute x2, starting transfers between devices, shifted(): return lax.ppermute(value, axis, pairs)  4.94 us
  transfers between devices with their start and end apart: 23, of which 9 were waited for; matrix products, arithmetic and copies ran while one was open for 2% of the time, Pallas kernels for 65%

profile of v6, /device:TPU:0, one launch (start us, length us, event | category | flops | bytes accessed | tf_op | source)
XLA Modules:
  0.0 121.4 jit_solution(2540014302191747048)
XLA Ops:
  0.6 0.0 copy-start.11
  0.6 0.0 copy-start.13
  0.7 1.1 slice.8.skel_ref
  1.7 3.0 %collective-permute-start.1 = (f32[512,256]{1,0:T(8,128)S(1)}, f32[512,256]{1,0:T(8,128)S(1)}, u32[]{:S(2)}, u32[]{:S(2)}) collective-permute-start(f32[512,256]{1,0:T(8,128)S(1)} %slice.8.skel_ref), channel_id=1, source_target_pairs={{0,2},{1,3},{2,0},{3,1},{4,6},{5,7},{6,4},{7,5},{8,10},{9,11},{10,... | collective-permute-start | bytes 1572872 | tf_op jit(solution)/shard_map/ppermute | solution.py:518
  4.7 0.2 collective-permute-start.6
  4.9 1.0 slice.7
  5.9 0.9 pad_maximum_fusion
  6.8 1.9 %collective-permute-start.7 = (f32[768,256]{1,0:T(8,128)}, f32[768,256]{1,0:T(8,128)}, u32[]{:S(2)}, u32[]{:S(2)}) collective-permute-start(f32[768,256]{1,0:T(8,128)} %pad_maximum_fusion), channel_id=1, source_target_pairs={{0,4},{1,5},{2,6},{3,7},{4,8},{5,9},{6,10},{7,11},{8,12},{9,13},{1... | collective-permute-start | bytes 2359304 | tf_op jit(solution)/shard_map/ppermute | solution.py:524
  8.7 3.0 %collective-permute-start.8 = (f32[768,256]{1,0:T(8,128)}, f32[768,256]{1,0:T(8,128)}, u32[]{:S(2)}, u32[]{:S(2)}) collective-permute-start(f32[768,256]{1,0:T(8,128)} %pad_maximum_fusion), channel_id=1, source_target_pairs={{0,28},{1,29},{2,30},{3,31},{4,0},{5,1},{6,2},{7,3},{8,4},{9,5},{1... | collective-permute-start | bytes 2359304 | tf_op jit(solution)/shard_map/ppermute | solution.py:524
  11.8 2.8 %sibling_products.1 = (bf16[3,256,512]{2,1,0:T(8,128)(2,1)S(1)}, bf16[3,256,512]{2,1,0:T(8,128)(2,1)S(1)}) custom-call(s32[1]{0:T(128)} %bitcast.2.me_ref, s32[1,6]{1,0:T(1,128)S(1)} %copy-done.11, s32[1,5]{1,0:T(1,128)S(1)} %copy-done.13, f32[512,256]{1,0:T(8,128)S(1)} %slice.8.skel_ref, f32[6,512,512]{2,1,0:T(8,128)} %bitcast.12), custom_call_target="tpu_custom_call" | custom-call | flops 1 | bytes 1 | tf_op jit(solution)/shard_map/sibling_products/pallas_call | solution.py:539
  14.6 0.0 copy-start.7
  14.7 0.9 copy-done.7
  15.5 2.0 %collective-permute-done.1.s2 = f32[512,256]{1,0:T(8,128)S(1)} collective-permute-done((f32[512,256]{1,0:T(8,128)S(1)}, f32[512,256]{1,0:T(8,128)S(1)}, u32[]{:S(2)}, u32[]{:S(2)}) %collective-permute-start.1) | collective-permute-done | bytes 524320 | tf_op jit(solution)/shard_map/ppermute | solution.py:518
  17.5 9.2 %leaf_factor.1 = (f32[256,512]{1,0:T(8,128)}, f32[256,256]{1,0:T(8,128)S(1)}) custom-call(f32[512,512]{1,0:T(8,128)S(1)} %bitcast.11, f32[512,512]{1,0:T(8,128)S(1)} %bitcast.10, bf16[3,256,512]{2,1,0:T(8,128)(2,1)S(1)} %get-tuple-element.25.after1.high_hbm), custom_call_target="tpu_custom_call" | custom-call | flops 30000001024 | bytes 1 | tf_op jit(solution)/shard_map/leaf_factor/pallas_call | solution.py:539
  26.8 0.7 copy-done.10
  27.5 0.8 copy-done.17
  28.3 0.8 copy-done.18
  29.1 3.7 %own_window.1.after1.h0 = f32[1032,256]{1,0:T(8,128)} custom-call(s32[1]{0:T(128)} %bitcast.2.me_ref, s32[1,6]{1,0:T(1,128)} %near_ref.7, s32[1,5]{1,0:T(1,128)} %far_ref.7, bf16[3,256,512]{2,1,0:T(8,128)(2,1)} %copy-done.6, bf16[3,256,512]{2,1,0:T(8,128)(2,1)} %copy-done.7, f32[5,256,256]{2,1,0:T(8,128)} %bitcast.5, f32[256,256]{1,0:T(8,128)} %copy-done.10, ...), custom_call_target="tpu_custom_call" | custom-call | flops 1 | bytes 1 | tf_op jit(solution)/shard_map/own_window/pallas_call | solution.py:539
  32.8 0.6 collective-permute-start.4
  33.4 2.3 %collective-permute-start.3 = (f32[1032,256]{1,0:T(8,128)}, f32[1032,256]{1,0:T(8,128)}, u32[]{:S(2)}, u32[]{:S(2)}) collective-permute-start(f32[1032,256]{1,0:T(8,128)} %own_window.1.after1.h0), channel_id=1, source_target_pairs={{0,2},{1,3},{2,0},{3,1},{4,6},{5,7},{6,4},{7,5},{8,10},{9,11},{10,... | collective-permute-start | bytes 3170312 | tf_op jit(solution)/shard_map/ppermute | solution.py:518
  35.7 7.7 %left_products.1 = (bf16[6,256,512]{2,1,0:T(8,128)(2,1)}, bf16[6,256,512]{2,1,0:T(8,128)(2,1)}) custom-call(f32[512,512]{1,0:T(8,128)} %bitcast.9, f32[6,512,512]{2,1,0:T(8,128)} %bitcast.13, f32[1032,256]{1,0:T(8,128)} %own_window.1.after1.h0), custom_call_target="tpu_custom_call" | custom-call | flops 1 | bytes 1 | tf_op jit(solution)/shard_map/left_products/pallas_call | solution.py:624
  43.4 1.9 %collective-permute-done.8.rest_0_ = f32[768,256]{1,0:T(8,128)} collective-permute-done((f32[768,256]{1,0:T(8,128)}, f32[768,256]{1,0:T(8,128)}, u32[]{:S(2)}, u32[]{:S(2)}) %collective-permute-start.8) | collective-permute-done | bytes 786464 | tf_op jit(solution)/shard_map/ppermute | solution.py:524
  45.3 1.1 collective-permute-done.5.p1
  46.4 1.9 %collective-permute-done.9.p3 = f32[256,1024]{1,0:T(8,128)} collective-permute-done((f32[256,1024]{1,0:T(8,128)}, f32[256,1024]{1,0:T(8,128)}, u32[]{:S(2)}, u32[]{:S(2)}) %collective-permute-start.9) | collective-permute-done | bytes 1048608 | tf_op jit(solution)/shard_map/ppermute | solution.py:518
  48.3 11.5 %chip_sums.1 = (bf16[256,1024]{1,0:T(8,128)(2,1)}, bf16[256,1024]{1,0:T(8,128)(2,1)}, f32[1024,1024]{1,0:T(8,128)}) custom-call(s32[1]{0:T(128)} %bitcast.2.me_ref, f32[1032,256]{1,0:T(8,128)} %own_window.1.after1.h0, f32[1032,256]{1,0:T(8,128)} %collective-permute-done.4.h1, f32[256,1024]{1,0:T(8,128)} %p0.3, f32[256,1024]{1,0:T(8,128)} %collective-permute-done.5.p1, ...), custom_call_target="tpu_custom_call" | custom-call | flops 1 | bytes 1 | tf_op jit(solution)/shard_map/chip_sums/pallas_call | solution.py:539
  59.9 2.0 %collective-permute-done.3.h2 = f32[1032,256]{1,0:T(8,128)} collective-permute-done((f32[1032,256]{1,0:T(8,128)}, f32[1032,256]{1,0:T(8,128)}, u32[]{:S(2)}, u32[]{:S(2)}) %collective-permute-start.3) | collective-permute-done | bytes 1056800 | tf_op jit(solution)/shard_map/ppermute | solution.py:518
  61.9 0.1 collective-permute-start.10
  62.0 1.8 %collective-permute-start.15 = (f32[768,256]{1,0:T(8,128)}, f32[768,256]{1,0:T(8,128)S(1)}, u32[]{:S(2)}, u32[]{:S(2)}) collective-permute-start(f32[768,256]{1,0:T(8,128)} %collective-permute-done.7.rest_0_), channel_id=1, source_target_pairs={{0,2},{1,3},{2,0},{3,1},{4,6},{5,7},{6,4},{7,5},{8,10},{9,11},{10,... | collective-permute-start | bytes 2359304 | tf_op jit(solution)/shard_map/ppermute | solution.py:518
  63.8 0.3 collective-permute-start.12
  64.1 0.8 collective-permute-done.10.h3
  64.9 1.2 %copy-done.3 = f32[256,1024]{1,0:T(8,128)S(1)} copy-done((f32[256,1024]{1,0:T(8,128)S(1)}, f32[256,1024]{1,0:T(8,128)}, u32[]{:S(2)}) %copy-start.3) | copy-done | bytes 1048600
  66.1 2.2 %copy-done.4 = f32[1024,1024]{1,0:T(8,128)S(1)} copy-done((f32[1024,1024]{1,0:T(8,128)S(1)}, f32[1024,1024]{1,0:T(8,128)}, u32[]{:S(2)}) %copy-start.4) | copy-done | bytes 4194328
  68.3 28.4 %parent_factor.1 = (f32[768,1280]{1,0:T(8,128)S(1)}, f32[256,256]{1,0:T(8,128)S(1)}) custom-call(s32[1]{0:T(128)} %bitcast.2.me_ref, f32[1032,256]{1,0:T(8,128)} %collective-permute-done.3.h2, f32[1032,256]{1,0:T(8,128)S(1)} %collective-permute-done.10.h3, f32[256,1024]{1,0:T(8,128)S(1)} %copy-done.3, f32[256,1024]{1,0:T(8,128)} %collective-permute-done.5.p1, ...), custom_call_target="tpu_custom_call" | custom-call | flops 1 | bytes 1 | tf_op jit(solution)/shard_map/parent_factor/pallas_call | solution.py:539
  96.7 0.2 collective-permute-start.16
  96.9 0.4 collective-permute-start.11
  97.2 1.8 %collective-permute-done.12.rest_2_ = f32[768,256]{1,0:T(8,128)S(1)} collective-permute-done((f32[768,256]{1,0:T(8,128)}, f32[768,256]{1,0:T(8,128)S(1)}, u32[]{:S(2)}, u32[]{:S(2)}) %collective-permute-start.12) | collective-permute-done | bytes 786464 | tf_op jit(solution)/shard_map/ppermute | solution.py:518
  99.1 3.6 %prev_windows.1.rest_4_.rest_0_ = f32[256,256]{1,0:T(8,128)S(1)} custom-call(s32[1]{0:T(128)} %bitcast.2.me_ref, s32[1,6]{1,0:T(1,128)S(1)} %copy-done.12, s32[1,5]{1,0:T(1,128)S(1)} %copy-done.14, bf16[6,256,512]{2,1,0:T(8,128)(2,1)S(1)} %copy-done, bf16[6,256,512]{2,1,0:T(8,128)(2,1)S(1)} %copy-done.2, f32[5,256,256]{2,1,0:T(8,128)S(1)} %bitcast.6, ...), custom_call_target="tpu_custom_call" | custom-call | flops 1 | bytes 1 | tf_op jit(solution)/shard_map/prev_windows/pallas_call | solution.py:539
  102.7 1.5 %collective-permute-start.18 = (f32[256,256]{1,0:T(8,128)S(1)}, f32[256,256]{1,0:T(8,128)S(1)}, u32[]{:S(2)}, u32[]{:S(2)}) collective-permute-start(f32[256,256]{1,0:T(8,128)S(1)} %prev_windows.1.rest_4_.rest_0_), channel_id=1, source_target_pairs={{0,2},{1,3},{2,0},{3,1},{4,6},{5,7},{6,4},{7,5},{8,10},{9,11},{10,... | collective-permute-start | bytes 786440 | tf_op jit(solution)/shard_map/ppermute | solution.py:518
  104.2 3.7 %next_windows.1.after1.rest_4_ = f32[256,256]{1,0:T(8,128)S(1)} custom-call(s32[1]{0:T(128)} %bitcast.2.me_ref, s32[1,6]{1,0:T(1,128)S(1)} %copy-done.12, s32[1,5]{1,0:T(1,128)S(1)} %copy-done.14, bf16[6,256,512]{2,1,0:T(8,128)(2,1)S(1)} %copy-done, bf16[6,256,512]{2,1,0:T(8,128)(2,1)S(1)} %copy-done.2, f32[5,256,256]{2,1,0:T(8,128)S(1)} %bitcast.7, ...), custom_call_target="tpu_custom_call" | custom-call | flops 1 | bytes 1 | tf_op jit(solution)/shard_map/next_windows/pallas_call | solution.py:539
  107.9 0.7 collective-permute-start.21
  108.6 0.0 collective-permute-start.17
  108.6 0.5 collective-permute-start.20
  109.1 8.3 %parent_finish.1 = (f32[256,768]{1,0:T(8,128)}, f32[256,256]{1,0:T(8,128)S(1)}) custom-call(s32[1]{0:T(128)} %bitcast.2.me_ref, f32[768,1280]{1,0:T(8,128)S(1)} %get-tuple-element.34.work_hbm, f32[256,256]{1,0:T(8,128)S(1)} %get-tuple-element.35.rest_4_.edge_in, f32[256,256]{1,0:T(8,128)S(1)} %next_windows.1.after1.rest_4_), custom_call_target="tpu_custom_call" | custom-call | flops 1 | bytes 1 | tf_op jit(solution)/shard_map/parent_finish/pallas_call | solution.py:539
  117.5 0.1 collective-permute-start.19
  117.6 0.5 collective-permute-start.22
  118.1 1.0 collective-permute-done.19.rest_3_
  119.1 0.4 collective-permute-done.22.rest_7_
  119.5 1.9 %coupling.1 = f32[256,768]{1,0:T(8,128)} custom-call(bf16[256,1024]{1,0:T(8,128)(2,1)S(1)} %copy-done.8, bf16[256,1024]{1,0:T(8,128)(2,1)S(1)} %copy-done.9, f32[256,256]{1,0:T(8,128)S(1)} %prev_windows.1.rest_4_.rest_0_, f32[256,256]{1,0:T(8,128)S(1)} %collective-permute-done.17.rest_1_, f32[256,256]{1,0:T(8,128)S(1)} %collective-permute-done.18.rest_2_, ...), custom_call_target="tpu_custom_call" | custom-call | flops 1 | bytes 1 | tf_op jit(solution)/shard_map/coupling/pallas_call | solution.py:539
  (49 shorter events, 0.1 us)
Async XLA Ops:
  0.6 11.2 %copy-start.11 = (s32[1,6]{1,0:T(1,128)S(1)}, s32[1,6]{1,0:T(1,128)}, u32[]{:S(2)}) copy-start(s32[1,6]{1,0:T(1,128)} %near_ref.7) | copy-start | bytes 76
  0.6 11.1 %copy-start.13 = (s32[1,5]{1,0:T(1,128)S(1)}, s32[1,5]{1,0:T(1,128)}, u32[]{:S(2)}) copy-start(s32[1,5]{1,0:T(1,128)} %far_ref.7) | copy-start | bytes 64
  1.7 15.8 %collective-permute-start.1 = (f32[512,256]{1,0:T(8,128)S(1)}, f32[512,256]{1,0:T(8,128)S(1)}, u32[]{:S(2)}, u32[]{:S(2)}) collective-permute-start(f32[512,256]{1,0:T(8,128)S(1)} %slice.8.skel_ref), channel_id=1, source_target_pairs={{0,2},{1,3},{2,0},{3,1},{4,6},{5,7},{6,4},{7,5},{8,10},{9,11},{10,... | collective-permute-start | bytes 1572872 | tf_op jit(solution)/shard_map/ppermute | solution.py:518
  4.7 22.7 %collective-permute-start = (f32[512,256]{1,0:T(8,128)S(1)}, f32[512,256]{1,0:T(8,128)S(1)}, u32[]{:S(2)}, u32[]{:S(2)}) collective-permute-start(f32[512,256]{1,0:T(8,128)S(1)} %slice.8.skel_ref), channel_id=1, source_target_pairs={{0,1},{1,0},{2,3},{3,2},{4,5},{5,4},{6,7},{7,6},{8,9},{9,8},{10,11... | collective-permute-start | bytes 1572872 | tf_op jit(solution)/shard_map/ppermute | solution.py:518
  4.7 40.6 %collective-permute-start.6 = (f32[256,1024]{1,0:T(8,128)}, f32[256,1024]{1,0:T(8,128)}, u32[]{:S(2)}, u32[]{:S(2)}) collective-permute-start(f32[256,1024]{1,0:T(8,128)} %p0.3), channel_id=1, source_target_pairs={{0,2},{1,3},{2,0},{3,1},{4,6},{5,7},{6,4},{7,5},{8,10},{9,11},{10,... | collective-permute-start | bytes 3145736 | tf_op jit(solution)/shard_map/ppermute | solution.py:518
  6.8 36.6 %collective-permute-start.7 = (f32[768,256]{1,0:T(8,128)}, f32[768,256]{1,0:T(8,128)}, u32[]{:S(2)}, u32[]{:S(2)}) collective-permute-start(f32[768,256]{1,0:T(8,128)} %pad_maximum_fusion), channel_id=1, source_target_pairs={{0,4},{1,5},{2,6},{3,7},{4,8},{5,9},{6,10},{7,11},{8,12},{9,13},{1... | collective-permute-start | bytes 2359304 | tf_op jit(solution)/shard_map/ppermute | solution.py:524
  8.7 36.6 %collective-permute-start.8 = (f32[768,256]{1,0:T(8,128)}, f32[768,256]{1,0:T(8,128)}, u32[]{:S(2)}, u32[]{:S(2)}) collective-permute-start(f32[768,256]{1,0:T(8,128)} %pad_maximum_fusion), channel_id=1, source_target_pairs={{0,28},{1,29},{2,30},{3,31},{4,0},{5,1},{6,2},{7,3},{8,4},{9,5},{1... | collective-permute-start | bytes 2359304 | tf_op jit(solution)/shard_map/ppermute | solution.py:524
  11.8 5.7 %copy-start.5 = (f32[1,512,512]{2,1,0:T(8,128)S(1)}, f32[1,512,512]{2,1,0:T(8,128)}, u32[]{:S(2)}) copy-start(f32[1,512,512]{2,1,0:T(8,128)} %param.10) | copy-start | bytes 3145732
  11.8 5.7 %copy-start.15 = (f32[1,512,512]{2,1,0:T(8,128)S(1)}, f32[1,512,512]{2,1,0:T(8,128)}, u32[]{:S(2)}) copy-start(f32[1,512,512]{2,1,0:T(8,128)} %param.7) | copy-start | bytes 3145732
  14.6 0.9 copy-start.7
  15.5 11.2 %copy-start.6 = (bf16[3,256,512]{2,1,0:T(8,128)(2,1)}, bf16[3,256,512]{2,1,0:T(8,128)(2,1)S(1)}, u32[]{:S(2)}) copy-start(bf16[3,256,512]{2,1,0:T(8,128)(2,1)S(1)} %get-tuple-element.25.after1.high_hbm) | copy-start | bytes 2359300
  17.5 9.3 %copy-start.16 = (f32[512,256]{1,0:T(8,128)}, f32[512,256]{1,0:T(8,128)S(1)}, u32[]{:S(2)}) copy-start(f32[512,256]{1,0:T(8,128)S(1)} %collective-permute-done.1.s2) | copy-start | bytes 1572868
  17.5 10.0 %collective-permute-start.2 = (f32[512,256]{1,0:T(8,128)S(1)}, f32[512,256]{1,0:T(8,128)S(1)}, u32[]{:S(2)}, u32[]{:S(2)}) collective-permute-start(f32[512,256]{1,0:T(8,128)S(1)} %collective-permute-done.1.s2), channel_id=1, source_target_pairs={{0,1},{1,0},{2,3},{3,2},{4,5},{5,4},{6,7},{7,6},{8,9},{9,8},{10,11... | collective-permute-start | bytes 1572872 | tf_op jit(solution)/shard_map/ppermute | solution.py:518
  26.8 0.7 copy-start.10
  27.5 0.8 copy-start.17
  28.3 0.8 copy-start.18
  32.8 15.5 %collective-permute-start.4 = (f32[1032,256]{1,0:T(8,128)}, f32[1032,256]{1,0:T(8,128)}, u32[]{:S(2)}, u32[]{:S(2)}) collective-permute-start(f32[1032,256]{1,0:T(8,128)} %own_window.1.after1.h0), channel_id=1, source_target_pairs={{0,1},{1,0},{2,3},{3,2},{4,5},{5,4},{6,7},{7,6},{8,9},{9,8},{10,11... | collective-permute-start | bytes 3170312 | tf_op jit(solution)/shard_map/ppermute | solution.py:518
  33.4 28.5 %collective-permute-start.3 = (f32[1032,256]{1,0:T(8,128)}, f32[1032,256]{1,0:T(8,128)}, u32[]{:S(2)}, u32[]{:S(2)}) collective-permute-start(f32[1032,256]{1,0:T(8,128)} %own_window.1.after1.h0), channel_id=1, source_target_pairs={{0,2},{1,3},{2,0},{3,1},{4,6},{5,7},{6,4},{7,5},{8,10},{9,11},{10,... | collective-permute-start | bytes 3170312 | tf_op jit(solution)/shard_map/ppermute | solution.py:518
  43.4 3.0 %collective-permute-start.5 = (f32[256,1024]{1,0:T(8,128)}, f32[256,1024]{1,0:T(8,128)}, u32[]{:S(2)}, u32[]{:S(2)}) collective-permute-start(f32[256,1024]{1,0:T(8,128)} %p0.3), channel_id=1, source_target_pairs={{0,1},{1,0},{2,3},{3,2},{4,5},{5,4},{6,7},{7,6},{8,9},{9,8},{10,11... | collective-permute-start | bytes 3145736 | tf_op jit(solution)/shard_map/ppermute | solution.py:518
  45.3 3.0 %collective-permute-start.9 = (f32[256,1024]{1,0:T(8,128)}, f32[256,1024]{1,0:T(8,128)}, u32[]{:S(2)}, u32[]{:S(2)}) collective-permute-start(f32[256,1024]{1,0:T(8,128)} %collective-permute-done.6.p2), channel_id=1, source_target_pairs={{0,1},{1,0},{2,3},{3,2},{4,5},{5,4},{6,7},{7,6},{8,9},{9,8},{10,11... | collective-permute-start | bytes 3145736 | tf_op jit(solution)/shard_map/ppermute | solution.py:518
  61.9 37.1 %copy-start.12 = (s32[1,6]{1,0:T(1,128)S(1)}, s32[1,6]{1,0:T(1,128)}, u32[]{:S(2)}) copy-start(s32[1,6]{1,0:T(1,128)} %near_ref.7) | copy-start | bytes 76
  61.9 37.1 %copy-start.14 = (s32[1,5]{1,0:T(1,128)S(1)}, s32[1,5]{1,0:T(1,128)}, u32[]{:S(2)}) copy-start(s32[1,5]{1,0:T(1,128)} %far_ref.7) | copy-start | bytes 64
  61.9 37.2 %copy-start = (bf16[6,256,512]{2,1,0:T(8,128)(2,1)S(1)}, bf16[6,256,512]{2,1,0:T(8,128)(2,1)}, u32[]{:S(2)}) copy-start(bf16[6,256,512]{2,1,0:T(8,128)(2,1)} %get-tuple-element.29.after1.high_hbm) | copy-start | bytes 4718596
  61.9 37.2 %copy-start.1 = (f32[1,5,256,256]{3,2,1,0:T(8,128)S(1)}, f32[1,5,256,256]{3,2,1,0:T(8,128)}, u32[]{:S(2)}) copy-start(f32[1,5,256,256]{3,2,1,0:T(8,128)} %param.9) | copy-start | bytes 3932164
  61.9 37.2 %copy-start.2 = (bf16[6,256,512]{2,1,0:T(8,128)(2,1)S(1)}, bf16[6,256,512]{2,1,0:T(8,128)(2,1)}, u32[]{:S(2)}) copy-start(bf16[6,256,512]{2,1,0:T(8,128)(2,1)} %get-tuple-element.36.low_hbm) | copy-start | bytes 4718596
  61.9 2.9 %collective-permute-start.10 = (f32[1032,256]{1,0:T(8,128)}, f32[1032,256]{1,0:T(8,128)S(1)}, u32[]{:S(2)}, u32[]{:S(2)}) collective-permute-start(f32[1032,256]{1,0:T(8,128)} %collective-permute-done.3.h2), channel_id=1, source_target_pairs={{0,1},{1,0},{2,3},{3,2},{4,5},{5,4},{6,7},{7,6},{8,9},{9,8},{10,11... | collective-permute-start | bytes 3170312 | tf_op jit(solution)/shard_map/ppermute | solution.py:518
  62.0 34.7 %collective-permute-start.15 = (f32[768,256]{1,0:T(8,128)}, f32[768,256]{1,0:T(8,128)S(1)}, u32[]{:S(2)}, u32[]{:S(2)}) collective-permute-start(f32[768,256]{1,0:T(8,128)} %collective-permute-done.7.rest_0_), channel_id=1, source_target_pairs={{0,2},{1,3},{2,0},{3,1},{4,6},{5,7},{6,4},{7,5},{8,10},{9,11},{10,... | collective-permute-start | bytes 2359304 | tf_op jit(solution)/shard_map/ppermute | solution.py:518
  63.8 35.2 %collective-permute-start.12 = (f32[768,256]{1,0:T(8,128)}, f32[768,256]{1,0:T(8,128)S(1)}, u32[]{:S(2)}, u32[]{:S(2)}) collective-permute-start(f32[768,256]{1,0:T(8,128)} %collective-permute-done.8.rest_0_), channel_id=1, source_target_pairs={{0,2},{1,3},{2,0},{3,1},{4,6},{5,7},{6,4},{7,5},{8,10},{9,11},{10,... | collective-permute-start | bytes 2359304 | tf_op jit(solution)/shard_map/ppermute | solution.py:518
  64.1 34.9 %collective-permute-start.14 = (f32[768,256]{1,0:T(8,128)}, f32[768,256]{1,0:T(8,128)S(1)}, u32[]{:S(2)}, u32[]{:S(2)}) collective-permute-start(f32[768,256]{1,0:T(8,128)} %collective-permute-done.7.rest_0_), channel_id=1, source_target_pairs={{0,1},{1,0},{2,3},{3,2},{4,5},{5,4},{6,7},{7,6},{8,9},{9,8},{10,11... | collective-permute-start | bytes 2359304 | tf_op jit(solution)/shard_map/ppermute | solution.py:518
  64.9 1.2 %copy-start.3 = (f32[256,1024]{1,0:T(8,128)S(1)}, f32[256,1024]{1,0:T(8,128)}, u32[]{:S(2)}) copy-start(f32[256,1024]{1,0:T(8,128)} %p0.3) | copy-start | bytes 3145732
  66.1 2.2 %copy-start.4 = (f32[1024,1024]{1,0:T(8,128)S(1)}, f32[1024,1024]{1,0:T(8,128)}, u32[]{:S(2)}) copy-start(f32[1024,1024]{1,0:T(8,128)} %get-tuple-element.32.part_hbm) | copy-start | bytes 12582916
  96.7 2.4 %collective-permute-start.16 = (f32[768,256]{1,0:T(8,128)S(1)}, f32[768,256]{1,0:T(8,128)S(1)}, u32[]{:S(2)}, u32[]{:S(2)}) collective-permute-start(f32[768,256]{1,0:T(8,128)S(1)} %collective-permute-done.15.rest_2_), channel_id=1, source_target_pairs={{0,1},{1,0},{2,3},{3,2},{4,5},{5,4},{6,7},{7,6},{8,9},{9,8},{10,11... | collective-permute-start | bytes 2359304 | tf_op jit(solution)/shard_map/ppermute | solution.py:518
  96.9 7.3 %collective-permute-start.11 = (f32[768,256]{1,0:T(8,128)}, f32[768,256]{1,0:T(8,128)S(1)}, u32[]{:S(2)}, u32[]{:S(2)}) collective-permute-start(f32[768,256]{1,0:T(8,128)} %collective-permute-done.8.rest_0_), channel_id=1, source_target_pairs={{0,1},{1,0},{2,3},{3,2},{4,5},{5,4},{6,7},{7,6},{8,9},{9,8},{10,11... | collective-permute-start | bytes 2359304 | tf_op jit(solution)/shard_map/ppermute | solution.py:518
  99.0 5.2 %collective-permute-start.13 = (f32[768,256]{1,0:T(8,128)S(1)}, f32[768,256]{1,0:T(8,128)S(1)}, u32[]{:S(2)}, u32[]{:S(2)}) collective-permute-start(f32[768,256]{1,0:T(8,128)S(1)} %collective-permute-done.12.rest_2_), channel_id=1, source_target_pairs={{0,1},{1,0},{2,3},{3,2},{4,5},{5,4},{6,7},{7,6},{8,9},{9,8},{10,11... | collective-permute-start | bytes 2359304 | tf_op jit(solution)/shard_map/ppermute | solution.py:518
  102.7 14.8 %collective-permute-start.18 = (f32[256,256]{1,0:T(8,128)S(1)}, f32[256,256]{1,0:T(8,128)S(1)}, u32[]{:S(2)}, u32[]{:S(2)}) collective-permute-start(f32[256,256]{1,0:T(8,128)S(1)} %prev_windows.1.rest_4_.rest_0_), channel_id=1, source_target_pairs={{0,2},{1,3},{2,0},{3,1},{4,6},{5,7},{6,4},{7,5},{8,10},{9,11},{10,... | collective-permute-start | bytes 786440 | tf_op jit(solution)/shard_map/ppermute | solution.py:518
  107.9 9.7 %collective-permute-start.21 = (f32[256,256]{1,0:T(8,128)S(1)}, f32[256,256]{1,0:T(8,128)S(1)}, u32[]{:S(2)}, u32[]{:S(2)}) collective-permute-start(f32[256,256]{1,0:T(8,128)S(1)} %next_windows.1.after1.rest_4_), channel_id=1, source_target_pairs={{0,2},{1,3},{2,0},{3,1},{4,6},{5,7},{6,4},{7,5},{8,10},{9,11},{10,... | collective-permute-start | bytes 786440 | tf_op jit(solution)/shard_map/ppermute | solution.py:518
  108.6 9.5 %collective-permute-start.17 = (f32[256,256]{1,0:T(8,128)S(1)}, f32[256,256]{1,0:T(8,128)S(1)}, u32[]{:S(2)}, u32[]{:S(2)}) collective-permute-start(f32[256,256]{1,0:T(8,128)S(1)} %prev_windows.1.rest_4_.rest_0_), channel_id=1, source_target_pairs={{0,1},{1,0},{2,3},{3,2},{4,5},{5,4},{6,7},{7,6},{8,9},{9,8},{10,11... | collective-permute-start | bytes 786440 | tf_op jit(solution)/shard_map/ppermute | solution.py:518
  108.6 9.5 %collective-permute-start.20 = (f32[256,256]{1,0:T(8,128)S(1)}, f32[256,256]{1,0:T(8,128)S(1)}, u32[]{:S(2)}, u32[]{:S(2)}) collective-permute-start(f32[256,256]{1,0:T(8,128)S(1)} %next_windows.1.after1.rest_4_), channel_id=1, source_target_pairs={{0,1},{1,0},{2,3},{3,2},{4,5},{5,4},{6,7},{7,6},{8,9},{9,8},{10,11... | collective-permute-start | bytes 786440 | tf_op jit(solution)/shard_map/ppermute | solution.py:518
  109.1 10.3 %copy-start.8 = (bf16[256,1024]{1,0:T(8,128)(2,1)S(1)}, bf16[256,1024]{1,0:T(8,128)(2,1)}, u32[]{:S(2)}) copy-start(bf16[256,1024]{1,0:T(8,128)(2,1)} %get-tuple-element.42.t_high) | copy-start | bytes 1572868
  109.1 10.3 %copy-start.9 = (bf16[256,1024]{1,0:T(8,128)(2,1)S(1)}, bf16[256,1024]{1,0:T(8,128)(2,1)}, u32[]{:S(2)}) copy-start(bf16[256,1024]{1,0:T(8,128)(2,1)} %get-tuple-element.43.t_low) | copy-start | bytes 1572868
  117.5 1.6 %collective-permute-start.19 = (f32[256,256]{1,0:T(8,128)S(1)}, f32[256,256]{1,0:T(8,128)S(1)}, u32[]{:S(2)}, u32[]{:S(2)}) collective-permute-start(f32[256,256]{1,0:T(8,128)S(1)} %collective-permute-done.18.rest_2_), channel_id=1, source_target_pairs={{0,1},{1,0},{2,3},{3,2},{4,5},{5,4},{6,7},{7,6},{8,9},{9,8},{10,11... | collective-permute-start | bytes 786440 | tf_op jit(solution)/shard_map/ppermute | solution.py:518
  117.6 1.9 %collective-permute-start.22 = (f32[256,256]{1,0:T(8,128)S(1)}, f32[256,256]{1,0:T(8,128)S(1)}, u32[]{:S(2)}, u32[]{:S(2)}) collective-permute-start(f32[256,256]{1,0:T(8,128)S(1)} %collective-permute-done.21.rest_6_), channel_id=1, source_target_pairs={{0,1},{1,0},{2,3},{3,2},{4,5},{5,4},{6,7},{7,6},{8,9},{9,8},{10,11... | collective-permute-start | bytes 786440 | tf_op jit(solution)/shard_map/ppermute | solution.py:518
